TPU v7x, 32 devices: a whole 2x2x4 slice. The times are simulated.
32 devices in a mesh: dp: 8 (over z, x), seq: 4 (over y, core).
Axes of the slice: x: 2, y: 2, z: 4, core: 2. Of those that a mesh axis runs over, the one named last changes fastest.
Arguments:
- tokens: bfloat16 [8, 1024, 768], P('dp', 'seq'), may hold values from -6 to 6
- prefix_len: int32 [8], P('dp'), may hold values from 102 to 512
- neighbours: bfloat16 [8, 32, 128, 768], P('dp', 'seq'), may hold values from -6 to 6
- neighbour_index: int32 [8, 16, 2], P('dp', 'seq'), may hold values from 0 to 31, as said below
- w_qkv: bfloat16 [768, 2304], P(('dp', 'seq')), may hold values from -0.21875 to 0.21875
- w_out: bfloat16 [768, 768], P(('dp', 'seq')), may hold values from -2.5 to 2.5
- w_cross_q: bfloat16 [768, 768], P(('dp', 'seq')), may hold values from -0.21875 to 0.21875
- w_cross_kv: bfloat16 [768, 1536], P(('dp', 'seq')), may hold values from -0.21875 to 0.21875
- w_cross_out: bfloat16 [768, 768], P(('dp', 'seq')), may hold values from -1.75 to 1.75
- w_up: bfloat16 [768, 3072], P(('dp', 'seq')), may hold values from -0.21875 to 0.21875
- w_down: bfloat16 [3072, 768], P(('dp', 'seq')), may hold values from -0.109375 to 0.109375
- gain_one: bfloat16 [768], P(('dp', 'seq')), may hold values from 0.5 to 1.5
- shift_one: bfloat16 [768], P(('dp', 'seq')), may hold values from -3 to 3
- gain_two: bfloat16 [768], P(('dp', 'seq')), may hold values from 0.5 to 1.5
- shift_two: bfloat16 [768], P(('dp', 'seq')), may hold values from -3 to 3
- gain_three: bfloat16 [768], P(('dp', 'seq')), may hold values from 0.5 to 1.5
- shift_three: bfloat16 [768], P(('dp', 'seq')), may hold values from -3 to 3
- cotangent: bfloat16 [8, 1024, 768], P('dp', 'seq'), may hold values from -6 to 6
Outputs:
- output: bfloat16 [8, 1024, 768], P('dp', 'seq')
- grad_tokens: float32 [8, 1024, 768], P('dp', 'seq')
- grad_neighbours: float32 [8, 32, 128, 768], P('dp', 'seq')
- grad_w_qkv: float32 [768, 2304], P(('dp', 'seq'))
- grad_w_out: float32 [768, 768], P(('dp', 'seq'))
- grad_w_cross_q: float32 [768, 768], P(('dp', 'seq'))
- grad_w_cross_kv: float32 [768, 1536], P(('dp', 'seq'))
- grad_w_cross_out: float32 [768, 768], P(('dp', 'seq'))
- grad_w_up: float32 [768, 3072], P(('dp', 'seq'))
- grad_w_down: float32 [3072, 768], P(('dp', 'seq'))
- grad_gain_one: float32 [768], P(('dp', 'seq'))
- grad_shift_one: float32 [768], P(('dp', 'seq'))
- grad_gain_two: float32 [768], P(('dp', 'seq'))
- grad_shift_two: float32 [768], P(('dp', 'seq'))
- grad_gain_three: float32 [768], P(('dp', 'seq'))
- grad_shift_three: float32 [768], P(('dp', 'seq'))
Inputs may be any that keep to these rules, and one draw needn't show every extreme that they name: `neighbour_index`: for sequence s and quarter j (blocks j * 4 to (j + 1) * 4 - 1), the 8 indices name each slot from 2 * j * 4 to 2 * (j + 1) * 4 - 1 exactly once.
All inputs are finite; a program needn't handle non-finite values.
Results may differ from a plain program's by a relative error of at most 0.019.
Values may be sent and summed in bfloat16 or wider, within the bound.
A program may use at most 192 MiB of HBM per device.

v0:
```python
from functools import partial

import jax
import jax.numpy as jnp
from jax import lax
from jax.sharding import PartitionSpec as P

HEAD = 64


eps = 1e-05
masked = -1e30


def dense_dot(left_side, weight):
    return jnp.dot(left_side, weight, preferred_element_type=jnp.float32)


def input_grad(grad_out, weight):
    return lax.dot_general(
        grad_out,
        weight,
        (((grad_out.ndim - 1,), (1,)), ((), ())),
        preferred_element_type=jnp.float32,
    )


def weight_grad(left_side, grad_out):
    flat_left = left_side.reshape(-1, left_side.shape[-1])
    flat_grad = grad_out.reshape(-1, grad_out.shape[-1])
    return lax.dot_general(
        flat_left, flat_grad, (((0,), (0,)), ((), ())), preferred_element_type=jnp.float32
    )


def norm_parts(array_in):
    avg_value = jnp.mean(array_in, -1, keepdims=True)
    centred = array_in - avg_value
    inv_std = lax.rsqrt(jnp.mean(centred * centred, -1, keepdims=True) + eps)
    return (centred * inv_std, inv_std)


def norm_back(grad_out, unit_part, inv_std, gain_f):
    scaled = grad_out * gain_f
    grad_in = inv_std * (
        scaled
        - jnp.mean(scaled, -1, keepdims=True)
        - unit_part * jnp.mean(scaled * unit_part, -1, keepdims=True)
    )
    return (grad_in, jnp.sum(grad_out * unit_part, (0, 1)), jnp.sum(grad_out, (0, 1)))


def rotary_tables(positions):
    half_size = HEAD // 2
    frequency = 10000.0 ** (-jnp.arange(half_size).astype(jnp.float32) / half_size)
    angles = positions.astype(jnp.float32)[:, None] * frequency[None, :]
    return (jnp.cos(angles)[:, None, :], jnp.sin(angles)[:, None, :])


def rotate(array_in, cosine, sine_part):
    half_size = HEAD // 2
    first_half = array_in[..., :half_size]
    second = array_in[..., half_size:]
    return jnp.concatenate(
        [first_half * cosine - second * sine_part, second * cosine + first_half * sine_part], -1
    )


def unrotate(grad_in, cosine, sine_part):
    half_size = HEAD // 2
    first_half = grad_in[..., :half_size]
    second = grad_in[..., half_size:]
    return jnp.concatenate(
        [first_half * cosine + second * sine_part, second * cosine - first_half * sine_part], -1
    )


def grouped(array_in):
    split_heads = array_in.reshape(
        array_in.shape[0], array_in.shape[1], array_in.shape[2] // 4, 4, array_in.shape[3]
    )
    return jnp.moveaxis(split_heads, 2, 0)


def ungrouped(array_in):
    shifted_axes = jnp.moveaxis(array_in, 0, 2)
    return shifted_axes.reshape(
        shifted_axes.shape[0], shifted_axes.shape[1], -1, shifted_axes.shape[-1]
    )


def masked_scores(visible, queries, key_rows):
    scores = jnp.einsum(
        "sqhd,skhd->shqk", queries, key_rows, preferred_element_type=jnp.float32
    ) * HEAD ** (-0.5)
    return jnp.where(visible[:, None], scores, masked)


def attend_group(visible, packed):
    queries, key_rows, values = packed
    scores = masked_scores(visible, queries, key_rows)
    row_max = jnp.max(scores, -1, keepdims=True)
    exp_scores = jnp.exp(scores - row_max)
    row_total = jnp.sum(exp_scores, -1, keepdims=True)
    probabilities = (exp_scores / row_total).astype(jnp.bfloat16)
    mixed_out = jnp.einsum(
        "shqk,skhd->sqhd", probabilities, values, preferred_element_type=jnp.float32
    )
    return (mixed_out, (row_max + jnp.log(row_total))[..., 0])


def attend_back(visible, packed):
    queries, key_rows, values, grad_out, logsum = packed
    scores = masked_scores(visible, queries, key_rows)
    probabilities = jnp.exp(scores - logsum[..., None])
    grad_probs = jnp.einsum("sqhd,skhd->shqk", grad_out, values, preferred_element_type=jnp.float32)
    grad_scores = (
        probabilities * (grad_probs - jnp.sum(probabilities * grad_probs, -1, keepdims=True))
    ).astype(jnp.bfloat16)
    grad_query = jnp.einsum(
        "shqk,skhd->sqhd", grad_scores, key_rows, preferred_element_type=jnp.float32
    ) * HEAD ** (-0.5)
    grad_key = jnp.einsum(
        "shqk,sqhd->skhd", grad_scores, queries, preferred_element_type=jnp.float32
    ) * HEAD ** (-0.5)
    grad_value = jnp.einsum(
        "shqk,sqhd->skhd",
        probabilities.astype(jnp.bfloat16),
        grad_out,
        preferred_element_type=jnp.float32,
    )
    return (grad_query, grad_key, grad_value)


def local(
    tokens,
    prefix_len,
    neighbours,
    neighbour_index,
    w_qkv,
    w_out,
    w_cross_q,
    w_cross_kv,
    w_cross_out,
    w_up,
    w_down,
    gain_one,
    shift_one,
    gain_two,
    shift_two,
    gain_three,
    shift_three,
    cotangent,
):
    forward_set = (
        lax.all_gather(w_qkv, ("dp", "seq"), axis=0, tiled=True),
        lax.all_gather(w_out, ("dp", "seq"), axis=0, tiled=True),
        lax.all_gather(w_cross_q, ("dp", "seq"), axis=0, tiled=True),
        lax.all_gather(w_cross_kv, ("dp", "seq"), axis=0, tiled=True),
        lax.all_gather(w_cross_out, ("dp", "seq"), axis=0, tiled=True),
        lax.all_gather(w_up, ("dp", "seq"), axis=0, tiled=True),
        lax.all_gather(w_down, ("dp", "seq"), axis=0, tiled=True),
        lax.all_gather(gain_one, ("dp", "seq"), axis=0, tiled=True),
        lax.all_gather(shift_one, ("dp", "seq"), axis=0, tiled=True),
        lax.all_gather(gain_two, ("dp", "seq"), axis=0, tiled=True),
        lax.all_gather(shift_two, ("dp", "seq"), axis=0, tiled=True),
        lax.all_gather(gain_three, ("dp", "seq"), axis=0, tiled=True),
        lax.all_gather(shift_three, ("dp", "seq"), axis=0, tiled=True),
    )
    (
        full_qkv,
        full_out,
        full_cross_q,
        full_cross_kv,
        full_cross_out,
        full_up,
        full_down,
        full_gain_one,
        full_shift_one,
        full_gain_two,
        full_shift_two,
        full_gain_three,
        full_shift_three,
    ) = forward_set
    seq_here, quarter, width = tokens.shape
    heads = width // HEAD
    hidden_width = full_up.shape[1]
    length = quarter * lax.axis_size("seq")
    seq_index = lax.axis_index("seq")
    query_pos = seq_index * quarter + jnp.arange(quarter)
    key_pos = jnp.arange(length)
    visible = (key_pos[None, None, :] <= query_pos[None, :, None]) | (
        key_pos[None, None, :] < prefix_len[:, None, None]
    )
    cosine, sine_part = rotary_tables(query_pos)
    gain_f1 = full_gain_one.astype(jnp.float32)
    gain_f2 = full_gain_two.astype(jnp.float32)
    gain_f3 = full_gain_three.astype(jnp.float32)
    resid_in = tokens.astype(jnp.float32)
    unit_one, inv_one = norm_parts(resid_in)
    normed_one = (unit_one * gain_f1 + full_shift_one.astype(jnp.float32)).astype(jnp.bfloat16)
    joined = dense_dot(normed_one, full_qkv)
    query_rot = rotate(
        joined[..., :width].reshape(seq_here, quarter, heads, HEAD), cosine, sine_part
    ).astype(jnp.bfloat16)
    key_local = (
        rotate(
            joined[..., width : 2 * width].reshape(seq_here, quarter, heads, HEAD),
            cosine,
            sine_part,
        )
        .astype(jnp.bfloat16)
        .reshape(seq_here, quarter, width)
    )
    value_local = joined[..., 2 * width :].astype(jnp.bfloat16)
    key_all, value_all = (
        lax.all_gather(key_local, "seq", axis=1, tiled=True),
        lax.all_gather(value_local, "seq", axis=1, tiled=True),
    )
    key_heads = key_all.reshape(seq_here, length, heads, HEAD)
    value_heads = value_all.reshape(seq_here, length, heads, HEAD)
    attended, logsum = lax.map(
        partial(attend_group, visible),
        (grouped(query_rot), grouped(key_heads), grouped(value_heads)),
    )
    attended = ungrouped(attended).reshape(seq_here, quarter, width).astype(jnp.bfloat16)
    first_sum = resid_in + dense_dot(attended, full_out)
    unit_two, inv_two = norm_parts(first_sum)
    normed_two = (unit_two * gain_f2 + full_shift_two.astype(jnp.float32)).astype(jnp.bfloat16)
    cross_query = dense_dot(normed_two, full_cross_q).astype(jnp.bfloat16)
    pool_kv = dense_dot(neighbours, full_cross_kv).astype(jnp.bfloat16)
    slots = neighbours.shape[1]
    spans = slots // 2
    span_len = quarter // spans
    neighbour_rows = 2 * neighbours.shape[2]
    local_index = neighbour_index.reshape(seq_here, slots) - seq_index * slots
    picked = jnp.take_along_axis(pool_kv, local_index[:, :, None, None], axis=1)
    picked = picked.reshape(seq_here, spans, neighbour_rows, 2 * width)
    cross_keys = picked[..., :width].reshape(seq_here, spans, neighbour_rows, heads, HEAD)
    cross_values = picked[..., width:].reshape(seq_here, spans, neighbour_rows, heads, HEAD)
    cross_queries = cross_query.reshape(seq_here, spans, span_len, heads, HEAD)
    cross_scores = jnp.einsum(
        "scqhd,sckhd->schqk", cross_queries, cross_keys, preferred_element_type=jnp.float32
    ) * HEAD ** (-0.5)
    cross_probs = jax.nn.softmax(cross_scores, -1)
    cross_weights = cross_probs.astype(jnp.bfloat16)
    cross_mixed = jnp.einsum(
        "schqk,sckhd->scqhd", cross_weights, cross_values, preferred_element_type=jnp.float32
    )
    cross_mixed = cross_mixed.reshape(seq_here, quarter, width).astype(jnp.bfloat16)
    second_sum = first_sum + dense_dot(cross_mixed, full_cross_out)
    unit_three, inv_three = norm_parts(second_sum)
    normed_three = (unit_three * gain_f3 + full_shift_three.astype(jnp.float32)).astype(
        jnp.bfloat16
    )
    hidden_pre = dense_dot(normed_three, full_up)
    activated = jax.nn.gelu(hidden_pre, approximate=False).astype(jnp.bfloat16)
    output = (second_sum + dense_dot(activated, full_down)).astype(jnp.bfloat16)
    backward_set = (
        lax.all_gather(w_qkv, ("dp", "seq"), axis=0, tiled=True),
        lax.all_gather(w_out, ("dp", "seq"), axis=0, tiled=True),
        lax.all_gather(w_cross_q, ("dp", "seq"), axis=0, tiled=True),
        lax.all_gather(w_cross_kv, ("dp", "seq"), axis=0, tiled=True),
        lax.all_gather(w_cross_out, ("dp", "seq"), axis=0, tiled=True),
        lax.all_gather(w_up, ("dp", "seq"), axis=0, tiled=True),
        lax.all_gather(w_down, ("dp", "seq"), axis=0, tiled=True),
        lax.all_gather(gain_one, ("dp", "seq"), axis=0, tiled=True),
        lax.all_gather(shift_one, ("dp", "seq"), axis=0, tiled=True),
        lax.all_gather(gain_two, ("dp", "seq"), axis=0, tiled=True),
        lax.all_gather(shift_two, ("dp", "seq"), axis=0, tiled=True),
        lax.all_gather(gain_three, ("dp", "seq"), axis=0, tiled=True),
        lax.all_gather(shift_three, ("dp", "seq"), axis=0, tiled=True),
    )
    (
        back_qkv,
        back_out,
        back_cross_q,
        back_cross_kv,
        back_cross_out,
        back_up,
        back_down,
        back_gain_one,
        back_shift_one,
        back_gain_two,
        back_shift_two,
        back_gain_three,
        back_shift_three,
    ) = backward_set
    grad_act = input_grad(cotangent, back_down)
    _, gelu_back = jax.vjp(partial(jax.nn.gelu, approximate=False), hidden_pre)
    grad_hidden = gelu_back(grad_act)[0].astype(jnp.bfloat16)
    grad_normed_three = input_grad(grad_hidden, back_up)
    back_three, grad_gain_three, grad_shift_three = norm_back(
        grad_normed_three, unit_three, inv_three, back_gain_three.astype(jnp.float32)
    )
    grad_second = cotangent.astype(jnp.float32) + back_three
    grad_cross_branch = grad_second.astype(jnp.bfloat16)
    grad_mixed = (
        input_grad(grad_cross_branch, back_cross_out)
        .astype(jnp.bfloat16)
        .reshape(seq_here, spans, span_len, heads, HEAD)
    )
    grad_cross_probs = jnp.einsum(
        "scqhd,sckhd->schqk", grad_mixed, cross_values, preferred_element_type=jnp.float32
    )
    grad_cross_scores = (
        cross_probs
        * (grad_cross_probs - jnp.sum(cross_probs * grad_cross_probs, -1, keepdims=True))
    ).astype(jnp.bfloat16)
    grad_cross_query = (
        (
            jnp.einsum(
                "schqk,sckhd->scqhd",
                grad_cross_scores,
                cross_keys,
                preferred_element_type=jnp.float32,
            )
            * HEAD ** (-0.5)
        )
        .astype(jnp.bfloat16)
        .reshape(seq_here, quarter, width)
    )
    grad_cross_keys = jnp.einsum(
        "schqk,scqhd->sckhd", grad_cross_scores, cross_queries, preferred_element_type=jnp.float32
    ) * HEAD ** (-0.5)
    grad_cross_values = jnp.einsum(
        "schqk,scqhd->sckhd", cross_weights, grad_mixed, preferred_element_type=jnp.float32
    )
    grad_picked = jnp.concatenate(
        [
            grad_cross_keys.reshape(seq_here, spans, neighbour_rows, width),
            grad_cross_values.reshape(seq_here, spans, neighbour_rows, width),
        ],
        -1,
    )
    grad_picked = grad_picked.reshape(seq_here, slots, neighbours.shape[2], 2 * width)
    seq_rows = jnp.arange(seq_here)[:, None]
    grad_pool_kv = (
        jnp.zeros(pool_kv.shape, jnp.float32)
        .at[seq_rows, local_index]
        .add(grad_picked)
        .astype(jnp.bfloat16)
    )
    grad_neighbours = input_grad(grad_pool_kv, back_cross_kv)
    grad_normed_two = input_grad(grad_cross_query, back_cross_q)
    back_two, grad_gain_two, grad_shift_two = norm_back(
        grad_normed_two, unit_two, inv_two, back_gain_two.astype(jnp.float32)
    )
    grad_first = grad_second + back_two
    grad_self_branch = grad_first.astype(jnp.bfloat16)
    grad_attended = (
        input_grad(grad_self_branch, back_out)
        .astype(jnp.bfloat16)
        .reshape(seq_here, quarter, heads, HEAD)
    )
    grad_query, grad_key_all, grad_value_all = lax.map(
        partial(attend_back, visible),
        (
            grouped(query_rot),
            grouped(key_heads),
            grouped(value_heads),
            grouped(grad_attended),
            logsum,
        ),
    )
    grad_query = ungrouped(grad_query)
    grad_key_all = ungrouped(grad_key_all).reshape(seq_here, length, width)
    grad_value_all = ungrouped(grad_value_all).reshape(seq_here, length, width)
    grad_key, grad_value = (
        lax.psum_scatter(
            grad_key_all.astype(jnp.bfloat16), "seq", scatter_dimension=1, tiled=True
        ).astype(jnp.float32),
        lax.psum_scatter(
            grad_value_all.astype(jnp.bfloat16), "seq", scatter_dimension=1, tiled=True
        ).astype(jnp.float32),
    )
    grad_joined = jnp.concatenate(
        [
            unrotate(grad_query, cosine, sine_part).reshape(seq_here, quarter, width),
            unrotate(grad_key.reshape(seq_here, quarter, heads, HEAD), cosine, sine_part).reshape(
                seq_here, quarter, width
            ),
            grad_value,
        ],
        -1,
    ).astype(jnp.bfloat16)
    grad_normed_one = input_grad(grad_joined, back_qkv)
    back_one, grad_gain_one, grad_shift_one = norm_back(
        grad_normed_one, unit_one, inv_one, back_gain_one.astype(jnp.float32)
    )
    grad_tokens = grad_first + back_one
    norm_grads = jnp.stack(
        [
            grad_gain_one,
            grad_shift_one,
            grad_gain_two,
            grad_shift_two,
            grad_gain_three,
            grad_shift_three,
        ],
        1,
    )
    width_owned = lax.psum_scatter(
        jnp.concatenate(
            [
                weight_grad(normed_one, grad_joined),
                weight_grad(attended, grad_self_branch),
                weight_grad(normed_two, grad_cross_query),
                weight_grad(neighbours, grad_pool_kv),
                weight_grad(cross_mixed, grad_cross_branch),
                weight_grad(normed_three, grad_hidden),
                norm_grads,
            ],
            1,
        ),
        ("dp", "seq"),
        scatter_dimension=0,
        tiled=True,
    )
    down_owned = lax.psum_scatter(
        weight_grad(activated, cotangent), ("dp", "seq"), scatter_dimension=0, tiled=True
    )
    column = 8 * width + hidden_width
    return (
        output,
        grad_tokens,
        grad_neighbours,
        width_owned[:, : 3 * width],
        width_owned[:, 3 * width : 4 * width],
        width_owned[:, 4 * width : 5 * width],
        width_owned[:, 5 * width : 7 * width],
        width_owned[:, 7 * width : 8 * width],
        width_owned[:, 8 * width : column],
        down_owned,
        width_owned[:, column],
        width_owned[:, column + 1],
        width_owned[:, column + 2],
        width_owned[:, column + 3],
        width_owned[:, column + 4],
        width_owned[:, column + 5],
    )


def solution(mesh):
    return jax.shard_map(
        local,
        mesh=mesh,
        in_specs=(
            P("dp", "seq", None),
            P("dp"),
            P("dp", "seq", None, None),
            P("dp", "seq", None),
            P(("dp", "seq"), None),
            P(("dp", "seq"), None),
            P(("dp", "seq"), None),
            P(("dp", "seq"), None),
            P(("dp", "seq"), None),
            P(("dp", "seq"), None),
            P(("dp", "seq"), None),
            P(("dp", "seq")),
            P(("dp", "seq")),
            P(("dp", "seq")),
            P(("dp", "seq")),
            P(("dp", "seq")),
            P(("dp", "seq")),
            P("dp", "seq", None),
        ),
        out_specs=(
            P("dp", "seq", None),
            P("dp", "seq", None),
            P("dp", "seq", None, None),
            P(("dp", "seq"), None),
            P(("dp", "seq"), None),
            P(("dp", "seq"), None),
            P(("dp", "seq"), None),
            P(("dp", "seq"), None),
            P(("dp", "seq"), None),
            P(("dp", "seq"), None),
            P(("dp", "seq")),
            P(("dp", "seq")),
            P(("dp", "seq")),
            P(("dp", "seq")),
            P(("dp", "seq")),
            P(("dp", "seq")),
        ),
        check_vma=False,
    )
```

profile of v0, /device:TPU:1, one launch (start us, length us, event | category | flops | bytes accessed | tf_op | source)
XLA Modules:
  0.0 1250.6 jit_solution(5479940722575085981)
XLA Ops:
  13.8 40.9 %all-reduce.8 = (bf16[768]{0:T(1024)(128)(2,1)S(1)}, bf16[768]{0:T(1024)(128)(2,1)S(1)}, bf16[768]{0:T(1024)(128)(2,1)S(1)}, bf16[768]{0:T(1024)(128)(2,1)S(1)},...) all-reduce(bf16[768]{0:T(1024)(128)(2,1)S(1)} %dynamic-update-slice, ...), channel_id=1, replica_groups=mesh['dp'=8,'seq'=4] {'dp','seq'}, use_global_device_ids=true, to_apply=%add.2 | all-reduce | flops 4608 | bytes 18432
  57.2 16.7 %all-gather.10.cloned.1.call-done = bf16[768,2304]{1,0:T(8,128)(2,1)} async-done(((bf16[24,2304]{1,0:T(8,128)(2,1)}), bf16[768,2304]{1,0:T(8,128)(2,1)}) %all-gather.10.cloned.1.call-update) | async-done | bytes 3538960 | tf_op jit(solution)/shard_map/all_gather | solution.py:156
  73.9 3.3 convolution_bitcast_fusion
  79.7 2.4 fusion.156
  92.2 40.7 %all-gather.18.cloned.1.call-done = bf16[768,1536]{1,0:T(8,128)(2,1)} async-done(((bf16[24,1536]{1,0:T(8,128)(2,1)}), bf16[768,1536]{1,0:T(8,128)(2,1)}) %all-gather.18.cloned.1.call-update) | async-done | bytes 2359312 | tf_op jit(solution)/shard_map/all_gather | solution.py:159
  132.9 5.6 convolution_convert_fusion
  138.5 4.5 gather_fusion
  143.0 2.2 broadcast_select_fusion
  146.6 2.6 copy.102
  154.7 20.2 %all-gather.14.cloned.1.call-done = bf16[1,1024,768]{1,2,0:T(8,128)(2,1)} async-done(((bf16[1,256,768]{1,2,0:T(8,128)(2,1)}), bf16[1,1024,768]{1,2,0:T(8,128)(2,1)}) %all-gather.14.cloned.1.call-update) | async-done | bytes 1572880 | tf_op jit(solution)/shard_map/all_gather | solution.py:217
  174.9 17.0 %while.30 = (s32[]{:T(128)}, bf16[3,1,256,4,64]{2,4,3,1,0:T(8,128)(2,1)}, f32[3,1,4,256]{3,2,1,0:T(4,128)}, bf16[3,1,1024,4,64]{2,4,3,1,0:T(8,128)(2,1)S(1)}, bf...) while((s32[]{:T(128)}, ...), condition=%wide.region_5.6_spmd.clone.clone, body=%wide.region_2.5_spmd.clone.sunk.clone | while | flops 281541632 | bytes 18256024 | solution.py:222
  175.1 2.0 fusion.234
  180.8 2.0 fusion.234
  186.5 2.0 fusion.234
  191.9 39.9 %all-gather.16.cloned.1.call-done = bf16[768,768]{1,0:T(8,128)(2,1)} async-done(((bf16[24,768]{1,0:T(8,128)(2,1)}), bf16[768,768]{1,0:T(8,128)(2,1)}) %all-gather.16.cloned.1.call-update) | async-done | bytes 1179664 | tf_op jit(solution)/shard_map/all_gather | solution.py:157
  231.8 2.1 fusion.157
  234.1 53.5 %all-gather.20.cloned.1.call-done = bf16[768,768]{1,0:T(8,128)(2,1)} async-done(((bf16[24,768]{1,0:T(8,128)(2,1)}), bf16[768,768]{1,0:T(8,128)(2,1)}) %all-gather.20.cloned.1.call-update) | async-done | bytes 1179664 | tf_op jit(solution)/shard_map/all_gather | solution.py:158
  287.6 1.8 convolution_convert_fusion.4
  291.1 1.8 copy.114
  292.9 5.0 fusion.158
  297.9 3.0 fusion.82
  302.4 2.9 convert_element_type.236
  305.3 38.3 %all-gather.22.cloned.1.call-done = bf16[768,768]{1,0:T(8,128)(2,1)} async-done(((bf16[24,768]{1,0:T(8,128)(2,1)}), bf16[768,768]{1,0:T(8,128)(2,1)}) %all-gather.22.cloned.1.call-update) | async-done | bytes 1179664 | tf_op jit(solution)/shard_map/all_gather | solution.py:160
  343.6 2.0 fusion.159
  346.9 62.1 %all-gather.24.cloned.1.call-done = bf16[768,3072]{1,0:T(8,128)(2,1)} async-done(((bf16[24,3072]{1,0:T(8,128)(2,1)}), bf16[768,3072]{1,0:T(8,128)(2,1)}) %all-gather.24.cloned.1.call-update) | async-done | bytes 4718608 | tf_op jit(solution)/shard_map/all_gather | solution.py:161
  409.0 11.4 multiply_convert_fusion.2
  420.4 54.0 %all-gather.26.cloned.1.call-done = bf16[3072,768]{1,0:T(8,128)(2,1)} async-done(((bf16[96,768]{1,0:T(8,128)(2,1)}), bf16[3072,768]{1,0:T(8,128)(2,1)}) %all-gather.26.cloned.1.call-update) | async-done | bytes 4718608 | tf_op jit(solution)/shard_map/all_gather | solution.py:162
  474.4 6.4 add_convert_fusion
  480.9 2.1 fusion.102
  486.4 2.4 reshape.993
  488.8 2.5 copy.116
  491.3 4.0 multiply_reduce_fusion.1
  499.5 1.9 reshape.931
  501.4 2.7 fusion.103
  504.8 1.8 fusion.106
  508.8 1.9 copy.110
  510.7 30.4 %while.31 = (s32[]{:T(128)}, f32[3,1,256,4,64]{2,4,3,1,0:T(8,128)}, bf16[3,1,1024,4,64]{2,4,3,1,0:T(8,128)(2,1)}, bf16[3,1,1024,4,64]{2,4,3,1,0:T(8,128)(2,1)}, ...) while((s32[]{:T(128)}, f32[3,1,256,4,64]{2,4,3,1,0:T(8,128)}, ...), condition=%wide.region_19.20_spmd.clone.clone, body=%wide.region_17.19_spmd.clone.sunk.clone | while | flops 687668224 | bytes 63737092 | solution.py:356
  512.4 2.8 multiply_reduce_fusion.10
  522.5 2.8 multiply_reduce_fusion.10
  532.6 2.8 multiply_reduce_fusion.10
  541.9 2.7 convolution_bitcast_fusion.2
  544.7 3.7 copy.117
  548.4 5.2 concatenate.71
  555.6 3.7 copy.115
  559.3 5.1 concatenate.70
  564.3 5.3 maximum_bitcast_fusion
  569.6 6.6 copy.118
  576.3 3.5 broadcast.606
  579.7 14.8 %scatter_fusion = f32[8,128,1536]{2,1,0:T(8,128)} fusion(f32[8,128,1536]{2,1,0:T(8,128)} %broadcast.606, s32[8]{0:T(128)S(1)} %fusion.135, f32[8,128,1536]{2,1,0:T(8,128)} %copy.118), kind=kCustom, calls=%fused_computation.1 | custom fusion | flops 1572864 | bytes 18874400 | tf_op jit(solution)/shard_map/scatter-add | solution.py:341
  594.5 7.7 convolution_bitcast_fusion.1
  602.2 6.4 copy.122
  612.4 1.9 fusion.117
  614.3 1.9 fusion.120
  616.2 2.1 fusion.147
  618.3 5.3 fusion.143
  627.7 5.5 fusion.112
  633.3 1.9 fusion.100
  638.6 31.8 %concatenate.73 = f32[768,9222]{1,0:T(8,128)} concatenate(f32[768,2304]{1,0:T(8,128)} %fusion.112, f32[768,768]{1,0:T(8,128)} %fusion.117, f32[768,768]{1,0:T(8,128)} %fusion.147, f32[768,1536]{1,0:T(8,128)} %copy.122, f32[768,768]{1,0:T(8,128)} %fusion.120, f32[768,3072]{1,0:T(8,128)} %fusion.143, f32[768,1]{1,0:T(8,128)} %stack.24, f32[768,1]{1,0:T(8,128)} %stack.25, ...), dimensions={1} | concatenate | bytes 56659968 | tf_op jit(solution)/shard_map/concatenate | solution.py:404
  670.5 7.4 fusion.123
  677.9 5.2 fusion.87
  683.1 7.3 fusion.74
  691.6 410.8 %all-reduce.11.cloned.1.call-done = f32[768,9222]{1,0:T(8,128)} async-done(((f32[768,9222]{1,0:T(8,128)}), f32[768,9222]{1,0:T(8,128)}) %all-reduce.11.cloned.1.call-update) | async-done | bytes 28330000
  1104.1 1.8 dynamic-slice.6
  1111.1 132.6 %reduce-scatter.8.cloned.1.call-done = f32[96,768]{1,0:T(8,128)} async-done(((f32[3072,768]{1,0:T(8,128)}), f32[96,768]{1,0:T(8,128)}) %reduce-scatter.8.cloned.1.call-update) | async-done | bytes 294928 | tf_op jit(solution)/shard_map/reduce_scatter | solution.py:420
  (325 shorter events, 97.5 us)
Async XLA Ops:
  7.2 125.7 %copy-start = (bf16[1,8,128,768]{3,2,1,0:T(8,128)(2,1)S(1)}, bf16[1,8,128,768]{3,2,1,0:T(8,128)(2,1)}, u32[]{:S(2)}) copy-start(bf16[1,8,128,768]{3,2,1,0:T(8,128)(2,1)} %param.24) | copy-start | bytes 4718596
  7.2 66.7 %all-gather.10.cloned.1.call-start = ((), (), s32[]{:S(2)}) async-start(), calls=%async_computation.3 | async-start | bytes 3649536 | tf_op jit(solution)/shard_map/all_gather | solution.py:156
  7.9 125.0 %all-gather.18.cloned.1.call-start = ((), (), s32[]{:S(2)}) async-start(), calls=%async_computation.7 | async-start | bytes 2433024 | tf_op jit(solution)/shard_map/all_gather | solution.py:159
  8.7 144.3 %all-gather.12.cloned.1.call-start = ((), (), s32[]{:S(2)}) async-start(), calls=%async_computation.4 | async-start | bytes 1966080 | tf_op jit(solution)/shard_map/all_gather | solution.py:218
  54.7 22.5 %copy-start.44 = (f32[768]{0:T(1024)}, f32[768]{0:T(1024)S(1)}, u32[]{:S(2)}) copy-start(f32[768]{0:T(1024)S(1)} %convert_element_type.218) | copy-start | bytes 9220
  54.7 22.5 %copy-start.41 = (f32[768]{0:T(1024)}, f32[768]{0:T(1024)S(1)}, u32[]{:S(2)}) copy-start(f32[768]{0:T(1024)S(1)} %convert_element_type.217) | copy-start | bytes 9220
  55.8 21.4 %copy-start.50 = (f32[256]{0:T(256)}, f32[256]{0:T(256)S(1)}, u32[]{:S(2)}) copy-start(f32[256]{0:T(256)S(1)} %broadcast_multiply_fusion.8) | copy-start | bytes 3076
  57.2 20.0 %copy-start.62 = (f32[256]{0:T(256)}, f32[256]{0:T(256)S(1)}, u32[]{:S(2)}) copy-start(f32[256]{0:T(256)S(1)} %add_rsqrt_fusion.2) | copy-start | bytes 3076
  79.4 95.5 %all-gather.14.cloned.1.call-start = ((), (), s32[]{:S(2)}) async-start(), calls=%async_computation.5 | async-start | bytes 1966080 | tf_op jit(solution)/shard_map/all_gather | solution.py:217
  79.7 4.1 copy-start.39
  79.7 4.1 copy-start.40
  82.4 8.4 copy-start.68
  85.6 146.2 %all-gather.16.cloned.1.call-start = ((), (), s32[]{:S(2)}) async-start(), calls=%async_computation.6 | async-start | bytes 1216512 | tf_op jit(solution)/shard_map/all_gather | solution.py:157
  86.2 201.4 %all-gather.20.cloned.1.call-start = ((), (), s32[]{:S(2)}) async-start(), calls=%async_computation.8 | async-start | bytes 1216512 | tf_op jit(solution)/shard_map/all_gather | solution.py:158
  86.8 256.8 %all-gather.22.cloned.1.call-start = ((), (), s32[]{:S(2)}) async-start(), calls=%async_computation.9 | async-start | bytes 1216512 | tf_op jit(solution)/shard_map/all_gather | solution.py:160
  87.5 321.5 %all-gather.24.cloned.1.call-start = ((), (), s32[]{:S(2)}) async-start(), calls=%async_computation.10 | async-start | bytes 4866048 | tf_op jit(solution)/shard_map/all_gather | solution.py:161
  88.3 386.1 %all-gather.26.cloned.1.call-start = ((), (), s32[]{:S(2)}) async-start(), calls=%async_computation.11 | async-start | bytes 4866048 | tf_op jit(solution)/shard_map/all_gather | solution.py:162
  89.0 534.6 %reduce-scatter.4.cloned.1.call-start = ((), (), s32[]{:S(2)}) async-start(), calls=%async_computation.12 | async-start | bytes 1966080 | tf_op jit(solution)/shard_map/reduce_scatter | solution.py:370
  90.9 47.6 %copy-start.55 = (s32[1,4,2]{2,1,0:T(4,128)}, s32[1,4,2]{2,1,0:T(4,128)S(1)}, u32[]{:S(2)}) copy-start(s32[1,4,2]{2,1,0:T(4,128)S(1)} %copy.101) | copy-start | bytes 100
  191.9 39.9 %copy-start.14 = (bf16[3,1,1024,4,64]{2,4,3,1,0:T(8,128)(2,1)}, bf16[3,1,1024,4,64]{2,4,3,1,0:T(8,128)(2,1)S(1)}, u32[]{:S(2)}) copy-start(bf16[3,1,1024,4,64]{2,4,3,1,0:T(8,128)(2,1)S(1)} %get-tuple-element.549) | copy-start | bytes 4718596
  233.9 267.5 %copy-start.2 = (f32[1,256,768]{2,1,0:T(8,128)}, f32[1,256,768]{2,1,0:T(8,128)S(1)}, u32[]{:S(2)}) copy-start(f32[1,256,768]{2,1,0:T(8,128)S(1)} %get-tuple-element.289) | copy-start | bytes 2359300
  233.9 55.6 %copy-start.48 = (f32[256]{0:T(256)}, f32[256]{0:T(256)S(1)}, u32[]{:S(2)}) copy-start(f32[256]{0:T(256)S(1)} %broadcast_multiply_fusion.7) | copy-start | bytes 3076
  234.1 55.4 %copy-start.56 = (f32[256]{0:T(256)}, f32[256]{0:T(256)S(1)}, u32[]{:S(2)}) copy-start(f32[256]{0:T(256)S(1)} %add_rsqrt_fusion.1) | copy-start | bytes 3076
  292.9 8.0 copy-start.16
  345.6 135.2 %copy-start.12 = (f32[1,256,768]{2,1,0:T(8,128)}, f32[1,256,768]{2,1,0:T(8,128)S(1)}, u32[]{:S(2)}) copy-start(f32[1,256,768]{2,1,0:T(8,128)S(1)} %get-tuple-element.293) | copy-start | bytes 2359300
  474.4 6.4 copy-start.53
  474.4 6.4 copy-start.64
  474.4 6.4 copy-start.70
  485.1 10.2 copy-start.9
  491.3 4.1 copy-start.11
  491.3 4.1 copy-start.43
  499.5 4.7 copy-start.46
  501.4 6.1 copy-start.17
  504.8 5.9 copy-start.1
  541.1 86.5 %reduce-scatter.6.cloned.1.call-start = ((), (), s32[]{:S(2)}) async-start(), calls=%async_computation.13 | async-start | bytes 1966080 | tf_op jit(solution)/shard_map/reduce_scatter | solution.py:373
  548.4 5.5 copy-start.6
  553.6 548.8 %all-reduce.11.cloned.1.call-start = ((), (), s32[]{:S(2)}) async-start(), calls=%async_computation.15 | async-start | bytes 57409536
  602.2 6.4 copy-start.59
  602.2 7.4 copy-start.60
  602.2 8.3 copy-start.66
  602.2 9.2 copy-start.58
  602.2 10.1 copy-start.8
  602.2 10.1 copy-start.21
  608.6 5.7 copy-start.10
  608.6 5.7 copy-start.24
  612.3 3.8 copy-start.23
  614.3 4.0 copy-start.13
  614.3 4.0 copy-start.35
  614.3 4.0 copy-start.54
  614.3 4.0 copy-start.65
  623.6 4.1 copy-start.15
  623.6 4.1 copy-start.42
  623.6 4.1 copy-start.45
  623.6 4.1 copy-start.51
  623.6 4.1 copy-start.63
  627.7 5.6 copy-start.36
  627.7 5.5 copy-start.37
  627.7 5.5 copy-start.38
  627.7 5.5 copy-start.71
  670.5 573.1 %reduce-scatter.8.cloned.1.call-start = ((), (), s32[]{:S(2)}) async-start(), calls=%async_computation.14 | async-start | bytes 9732096 | tf_op jit(solution)/shard_map/reduce_scatter | solution.py:420
  677.9 5.2 copy-start.72
  683.1 7.3 copy-start.69
  683.1 7.3 copy-start.67
  683.1 7.3 copy-start.26
  (36 other events, 68.4 us)
Sparse Core Ops, SparseCore 0:
  10.9 62.8 all-gather.9
  76.8 56.0 all-gather.17
  134.5 18.5 all-gather.11
  155.0 19.8 all-gather.13
  177.7 54.1 all-gather.15
  234.6 53.0 all-gather.19
  290.5 53.0 all-gather.21
  346.5 62.4 all-gather.23
  412.0 62.3 all-gather.25
  541.2 26.5 reduce-scatter.3
  570.5 28.1 reduce-scatter.5
  670.6 431.8 all-reduce.10
  1108.9 134.6 reduce-scatter.7
where the time goes:
time: 1260 us; the launch traced here: 1250 us
  waiting for transfers between devices  875 us (69%)
  matrix products  133 us (11%)
  local copies, waits for them, and re-layouts  131 us (10%)
  other arithmetic  53.4 us (4%)
  blocking collectives  40.9 us (3%)
  between operations  15.9 us (1%)
    unnamed x14, waiting for transfers between devices  415 us
    reduce_scatter x1, waiting for transfers between devices, local(): lax.psum_scatter(weight_grad(activated, cotangent), ('dp', 'seq'), scatte...  133 us
    all_gather x1, waiting for transfers between devices, local(): lax.all_gather(w_up, ('dp', 'seq'), axis=0, tiled=True)  62.1 us
    all_gather x1, waiting for transfers between devices, local(): lax.all_gather(w_down, ('dp', 'seq'), axis=0, tiled=True)  54 us
    all_gather x1, waiting for transfers between devices, local(): lax.all_gather(w_cross_q, ('dp', 'seq'), axis=0, tiled=True)  53.5 us
    unnamed x1, blocking collectives  40.9 us
    all_gather x1, waiting for transfers between devices, local(): lax.all_gather(w_cross_kv, ('dp', 'seq'), axis=0, tiled=True)  40.7 us
    all_gather x1, waiting for transfers between devices, local(): lax.all_gather(w_out, ('dp', 'seq'), axis=0, tiled=True)  39.9 us
  transfers between devices with their start and end apart: 13, of which 11 were waited for; matrix products, arithmetic and copies ran while one was open for 17% of the time, Pallas kernels for 0%

commit v1 on v0

--- a/solution.py
+++ b/solution.py
@@ -1,15 +1,631 @@
-from functools import partial
+import functools
+import math
 
 import jax
 import jax.numpy as jnp
+import numpy as np
 from jax import lax
+from jax.experimental import pallas as pl
+from jax.experimental.pallas import tpu as pltpu
 from jax.sharding import PartitionSpec as P
 
 HEAD = 64
-
-
 eps = 1e-05
 masked = -1e30
+MESH = pl.DeviceIdType.MESH
+bf16 = jnp.bfloat16
+f32 = jnp.float32
+NN = (((1,), (0,)), ((), ()))
+NT = (((1,), (1,)), ((), ()))
+TN = (((0,), (0,)), ((), ()))
+LANES = 128
+
+
+def dot(a, b, dims=NN):
+    return lax.dot_general(a, b, dims, preferred_element_type=f32)
+
+
+def norm_parts(v):
+    centred = v - jnp.mean(v, -1, keepdims=True)
+    inv = lax.rsqrt(jnp.mean(centred * centred, -1, keepdims=True) + eps)
+    return centred * inv, inv
+
+
+class Place:
+    def __init__(self, nz):
+        dp, s = lax.axis_index("dp"), lax.axis_index("seq")
+        self.nz, self.dp, self.s = nz, dp, s
+        self.z, self.x = lax.div(dp, 2), lax.rem(dp, 2)
+        self.y, self.c = lax.div(s, 2), lax.rem(s, 2)
+        x, y, z, c = self.x, self.y, self.z, self.c
+        self.o = 1 - c
+        self.own, self.at_x, self.at_y, self.at_d = (
+            x * 2 + y,
+            (1 - x) * 2 + y,
+            x * 2 + 1 - y,
+            (1 - x) * 2 + 1 - y,
+        )
+        self.to_z = [(lax.rem(z + j, nz) * 2 + x, s) for j in range(1, nz)]
+        self.z_of = [lax.rem(z + j, nz) for j in range(1, nz)]
+        self.z_from = [lax.rem(z - j + nz, nz) for j in range(1, nz)]
+        self.to_x = (z * 2 + 1 - x, s)
+        self.to_y = (dp, (1 - y) * 2 + c)
+        self.to_c = (dp, y * 2 + 1 - c)
+        self.s_y = (1 - y) * 2 + c
+        self.s_c = y * 2 + 1 - c
+        self.s_d = (1 - y) * 2 + 1 - c
+
+
+def remote(src, dst, send, recv, device):
+    return pltpu.make_async_remote_copy(
+        src_ref=src, dst_ref=dst, send_sem=send, recv_sem=recv, device_id=device, device_id_type=MESH
+    )
+
+
+class Gather:
+    def __init__(self, place, weights, chunks, send, recv):
+        self.p, self.w, self.chunks, self.ss, self.rs = place, weights, chunks, send, recv
+        self.sent = [[] for _ in chunks]
+
+    def part(self, q, half, z, xy):
+        k, start, width, _ = self.chunks[q]
+        return self.w[k].at[half, z, xy, :, pl.ds(start, width)]
+
+    def copy(self, q, j, ref, device):
+        return remote(ref, ref, self.ss.at[q, j], self.rs.at[q, j], device)
+
+    def send(self, q, j, ref, device):
+        cp = self.copy(q, j, ref, device)
+        cp.start()
+        self.sent[q].append(cp)
+
+    def wait(self, q, j, ref):
+        self.copy(q, j, ref, self.p.to_c).wait_recv()
+
+    def along_z(self, q):
+        p = self.p
+        for j, device in enumerate(p.to_z):
+            self.send(q, j, self.part(q, p.c, p.z, p.own), device)
+
+    def along_xy(self, q):
+        p, allz = self.p, slice(None)
+        for j, z in enumerate(p.z_from):
+            self.wait(q, j, self.part(q, p.c, z, p.own))
+        mine = self.part(q, p.c, allz, p.own)
+        self.send(q, 3, mine, p.to_x)
+        self.send(q, 4, mine, p.to_y)
+        self.send(q, 7, mine, p.to_c)
+
+    def across(self, q):
+        p, allz, cut = self.p, slice(None), self.chunks[q][3]
+        from_x, from_y = self.part(q, p.c, allz, p.at_x), self.part(q, p.c, allz, p.at_y)
+        self.wait(q, 3, from_x)
+        self.send(q, 5, self.part(q, p.c, pl.ds(0, cut), p.at_x), p.to_y)
+        self.send(q, 8, from_x, p.to_c)
+        self.wait(q, 4, from_y)
+        self.send(q, 6, self.part(q, p.c, pl.ds(cut, p.nz - cut), p.at_y), p.to_x)
+        self.send(q, 9, from_y, p.to_c)
+
+    def last(self, q):
+        p, cut = self.p, self.chunks[q][3]
+        for j, z in ((5, pl.ds(0, cut)), (6, pl.ds(cut, p.nz - cut))):
+            ref = self.part(q, p.c, z, p.at_d)
+            self.wait(q, j, ref)
+            self.send(q, j + 5, ref, p.to_c)
+
+    def ready(self, q):
+        p, allz, cut = self.p, slice(None), self.chunks[q][3]
+        for j, z, xy in (
+            (7, allz, p.own),
+            (8, allz, p.at_x),
+            (9, allz, p.at_y),
+            (10, pl.ds(0, cut), p.at_d),
+            (11, pl.ds(cut, p.nz - cut), p.at_d),
+        ):
+            self.wait(q, j, self.part(q, p.o, z, xy))
+
+    def settle(self, q):
+        for cp in self.sent[q]:
+            cp.wait_send()
+        self.sent[q] = []
+
+
+def half_of(w, h, start=None, width=None):
+    v = w[h] if start is None else w[h, :, :, :, pl.ds(start, width)]
+    return v.reshape(-1, v.shape[-1])
+
+
+def lane_masks():
+    lane = lax.broadcasted_iota(jnp.int32, (1, LANES), 1)
+    low = lane < HEAD
+    return low, jnp.where(low, 1.0, 0.0).astype(bf16), jnp.where(low, 0.0, 1.0).astype(bf16)
+
+
+def stacked(v, low, high):
+    return jnp.concatenate([v * low, v * high], 0)
+
+
+def swap_halves(v):
+    lane = lax.broadcasted_iota(jnp.int32, v.shape, 1)
+    first = lax.rem(lane, HEAD) < HEAD // 2
+    return jnp.where(first, pltpu.roll(v, LANES - HEAD // 2, 1), pltpu.roll(v, HEAD // 2, 1))
+
+
+def rotate(v, cosine, signed):
+    return v * cosine + swap_halves(v) * signed
+
+
+def forward(p, r, g, kv_sem):
+    n = len(g.chunks)
+    c, z = p.c, p.z
+    w = r.w
+
+    def step(t):
+        if t < n:
+            g.along_xy(t)
+        if t + 3 < n:
+            g.along_z(t + 3)
+        if 0 <= t - 1 < n:
+            g.across(t - 1)
+        if 0 <= t - 2 < n:
+            g.last(t - 2)
+
+    first = remote(r.shards.at[p.o], r.beside, r.pair_sem.at[0], r.pair_sem.at[1], p.to_c)
+    first.start()
+    w[6][c, z, p.own] = r.w_down[...]
+    first.wait_recv()
+    start = 0
+    for k in range(6):
+        width = w[k].shape[-1]
+        mine, other = r.shards[c, :, start : start + width], r.beside[:, start : start + width]
+        top, low = jnp.where(c == 0, mine, other), jnp.where(c == 0, other, mine)
+        w[k][c, z, p.own] = jnp.concatenate([top, low], 0).astype(bf16)
+        start += width
+        for q in range(3):
+            if g.chunks[q][0] == k:
+                g.along_z(q)
+    step(0)
+    tokens = r.tokens[...].astype(f32)
+    unit, _ = norm_parts(tokens)
+    step(1)
+    step(2)
+    g.ready(0)
+    qkv_half = 3 * 384
+    for h in range(2):
+        r.vec[h] = jnp.transpose(half_of(w[0], h, qkv_half, LANES).astype(f32))[:8]
+
+    def affine(v, i):
+        return (v * r.vec[0, i : i + 1] + r.vec[1, i : i + 1]).astype(bf16)
+
+    r.n1[...] = affine(unit, 0)
+    cosine, signed = r.rope[p.s, :, :LANES], r.rope[p.s, :, LANES:]
+    for i in (2, 3, 4, 5, 0, 1):
+        joined = dot(r.n1[...], half_of(w[0], i // 3, (i % 3) * 384, 384))
+        if i < 4:
+            joined = jnp.concatenate(
+                [rotate(joined[:, b : b + LANES], cosine, signed) for b in range(0, 384, LANES)], 1
+            )
+        part = joined.astype(bf16)
+        if i < 2:
+            r.q[:, i * 384 : (i + 1) * 384] = part
+        else:
+            r.kv[p.s, :, (i - 2) * 384 : (i - 1) * 384] = part
+            if i == 5:
+                kv_c = remote(r.kv.at[p.s], r.kv.at[p.s], kv_sem.at[0], kv_sem.at[1], p.to_c)
+                kv_y = remote(r.kv.at[p.s], r.kv.at[p.s], kv_sem.at[2], kv_sem.at[3], p.to_y)
+                kv_y.start()
+                kv_c.start()
+    step(3)
+
+    g.ready(1)
+
+    def pool_rows(i, carry):
+        rows = r.neighbours[pl.ds(i * 2, 2)].reshape(-1, r.neighbours.shape[2])
+        for h in range(2):
+            width = w[1].shape[-1]
+            r.pool[pl.ds(i * 2, 2), :, h * width : (h + 1) * width] = (
+                dot(rows, half_of(w[1], h)).astype(bf16).reshape(2, -1, width)
+            )
+        return carry
+
+    lax.fori_loop(0, r.neighbours.shape[0] // 2, pool_rows, 0)
+    landed = r.kv.at[p.s_y]
+    remote(landed, landed, kv_sem.at[2], kv_sem.at[3], p.to_y).wait_recv()
+    kv_d = remote(landed, landed, kv_sem.at[4], kv_sem.at[5], p.to_c)
+    kv_d.start()
+    step(4)
+    for ref, j in ((r.kv.at[p.s_c], 1), (r.kv.at[p.s_d], 5)):
+        remote(ref, ref, kv_sem.at[j - 1], kv_sem.at[j], p.to_c).wait_recv()
+
+    low_lane, low, high = lane_masks()
+    quarter = tokens.shape[0]
+    place = lax.rem(lax.broadcasted_iota(jnp.int32, (1, 2 * quarter), 1), quarter) + p.s * quarter
+    limit = jnp.maximum(place, r.prefix[0] - 1)
+
+    def self_pair(i, carry):
+        cols = pl.ds(pl.multiple_of(i * LANES, LANES), LANES)
+        vcols = pl.ds(pl.multiple_of(i * LANES + w[1].shape[-1], LANES), LANES)
+        queries = stacked(r.q[:, cols], low, high) * bf16(HEAD**-0.5)
+        keys = r.kv[:, :, cols].reshape(-1, LANES)
+        values = r.kv[:, :, vcols].reshape(-1, LANES)
+        scores = dot(keys, queries, NT)
+        key_place = lax.broadcasted_iota(jnp.int32, scores.shape, 0)
+        scores = jnp.where(key_place <= limit, scores, masked)
+        top = jnp.max(scores, 0, keepdims=True)
+        e = jnp.exp(scores - top)
+        total = jnp.sum(e, 0, keepdims=True)
+        weights = (e * (1.0 / total)).astype(bf16)
+        r.lse[i] = top + jnp.log(total)
+        mixed = dot(weights, values, TN)
+        r.att[:, cols] = jnp.where(low_lane, mixed[:quarter], mixed[quarter:]).astype(bf16)
+        return carry
+
+    lax.fori_loop(0, 3, self_pair, 0)
+    step(5)
+    lax.fori_loop(3, 6, self_pair, 0)
+    g.ready(2)
+
+    def project(v, k):
+        return jnp.concatenate([dot(v, half_of(w[k], h)) for h in range(2)], 1)
+
+    first_sum = tokens + project(r.att[...], 2)
+    r.first[...] = first_sum
+    r.n2[...] = affine(norm_parts(first_sum)[0], 1)
+    step(6)
+    g.ready(3)
+    r.cq[...] = project(r.n2[...], 3).astype(bf16)
+    slots = r.neighbours.shape[0]
+    span = quarter // (slots // 2)
+
+    def cross_pair(i, carry):
+        cols = pl.ds(pl.multiple_of(i * LANES, LANES), LANES)
+        vcols = pl.ds(pl.multiple_of(i * LANES + w[1].shape[-1], LANES), LANES)
+        for b in range(slots // 2):
+            two = [lax.rem(r.index[2 * b + j], slots) for j in range(2)]
+            rows = slice(b * span, (b + 1) * span)
+            queries = stacked(r.cq[rows, cols], low, high) * bf16(HEAD**-0.5)
+            keys = jnp.concatenate([r.pool[t, :, cols] for t in two], 0)
+            values = jnp.concatenate([r.pool[t, :, vcols] for t in two], 0)
+            scores = dot(keys, queries, NT)
+            top = jnp.max(scores, 0, keepdims=True)
+            e = jnp.exp(scores - top)
+            total = jnp.sum(e, 0, keepdims=True)
+            weights = (e * (1.0 / total)).astype(bf16)
+            r.lse_cross[i, b : b + 1] = top + jnp.log(total)
+            mixed = dot(weights, values, TN)
+            r.cm[rows, cols] = jnp.where(low_lane, mixed[:span], mixed[span:]).astype(bf16)
+        return carry
+
+    lax.fori_loop(0, 6, cross_pair, 0)
+    step(7)
+    g.ready(4)
+    second_sum = r.first[...] + project(r.cm[...], 4)
+    r.second[...] = second_sum
+    r.n3[...] = affine(norm_parts(second_sum)[0], 2)
+    step(8)
+    hidden_half = w[5].shape[-1]
+
+    def up_tiles(start, width, tile):
+        def body(i, carry):
+            h, col = lax.div(i, width // tile), start + lax.rem(i, width // tile) * tile
+            col = pl.multiple_of(col, tile)
+            hidden = dot(r.n3[...], half_of(w[5], h, col, tile))
+            cdf = 0.5 * (1.0 + lax.erf(hidden * (0.5**0.5)))
+            density = jnp.exp(-0.5 * hidden * hidden) * ((2 * math.pi) ** -0.5)
+            cols = pl.ds(pl.multiple_of(h * hidden_half + col, tile), tile)
+            r.act[:, cols] = (hidden * cdf).astype(bf16)
+            r.slope[:, cols] = (cdf + hidden * density).astype(bf16)
+            return carry
+
+        lax.fori_loop(0, 2 * (width // tile), body, 0)
+
+    g.ready(5)
+    up_tiles(0, 768, 256)
+    step(9)
+    g.ready(6)
+    up_tiles(768, 768, 256)
+    step(10)
+    for q in (7, 8):
+        g.ready(q)
+        col = g.chunks[q][1]
+        cols = slice(col, col + 384)
+        down = sum(dot(r.act[:, h * hidden_half : (h + 1) * hidden_half], half_of(w[6], h, col, 384)) for h in range(2))
+        r.out[:, cols] = (r.second[:, cols] + down).astype(bf16)
+    first.wait_send()
+    for cp in (kv_c, kv_y, kv_d):
+        cp.wait_send()
+
+
+class Refs:
+    pass
+
+
+NAMES_IN = ("shards", "w_down", "tokens", "prefix", "neighbours", "index", "rope")
+
+
+def buffers(nz, quarter, length, width, hidden, slots, rows_n, row_block):
+    heads2 = width // LANES
+    halves = (3 * width // 2 + LANES, width, width // 2, width // 2, width // 2, hidden // 2)
+    weights = [((2, nz, 4, row_block, h), bf16) for h in halves]
+    weights.append(((2, nz, 4, hidden // (8 * nz), width), bf16))
+    acts = dict(
+        n1=((quarter, width), bf16),
+        q=((quarter, width), bf16),
+        kv=((4, quarter, 2 * width), bf16),
+        att=((quarter, width), bf16),
+        lse=((heads2, 1, 2 * quarter), f32),
+        first=((quarter, width), f32),
+        n2=((quarter, width), bf16),
+        cq=((quarter, width), bf16),
+        pool=((slots, rows_n, 2 * width), bf16),
+        lse_cross=((heads2, 8, LANES), f32),
+        cm=((quarter, width), bf16),
+        second=((quarter, width), f32),
+        n3=((quarter, width), bf16),
+        act=((quarter, hidden), bf16),
+        slope=((quarter, hidden), bf16),
+        out=((quarter, width), bf16),
+        vec=((2, 8, width), f32),
+    )
+    return weights, acts
+
+
+CHUNKS = (
+    (0, 0, 1280, 2),
+    (1, 0, 768, 2),
+    (2, 0, 384, 2),
+    (3, 0, 384, 2),
+    (4, 0, 384, 2),
+    (5, 0, 768, 2),
+    (5, 768, 768, 2),
+    (6, 0, 384, 2),
+    (6, 384, 384, 2),
+)
+
+
+def forward_kernel(nz, names, *args):
+    n_in = len(NAMES_IN)
+    r = Refs()
+    for name, ref in zip(NAMES_IN, args[:n_in]):
+        setattr(r, name, ref)
+    r.w = args[n_in : n_in + 7]
+    outs = args[n_in + 7 : n_in + 7 + len(names)]
+    for name, ref in zip(names, outs):
+        setattr(r, name, ref)
+    r.beside, r.pair_sem, send, recv, kv_sem = args[n_in + 7 + len(names) :]
+    p = Place(nz)
+    barrier = pltpu.get_barrier_semaphore()
+    friends = [*p.to_z, p.to_x, p.to_y, p.to_c]
+    for device in friends:
+        pl.semaphore_signal(barrier, inc=1, device_id=device, device_id_type=MESH)
+    pl.semaphore_wait(barrier, len(friends))
+    g = Gather(p, r.w, CHUNKS, send, recv)
+    forward(p, r, g, kv_sem)
+    for q in range(len(CHUNKS)):
+        g.settle(q)
+
+
+def rope_table(length):
+    half = HEAD // 2
+    freq = (10000.0 ** (-np.arange(half, dtype=np.float32) / half)).astype(np.float32)
+    angles = np.arange(length, dtype=np.float32)[:, None] * freq[None, :]
+    cosine, sine = np.cos(angles), np.sin(angles)
+    table = np.concatenate([cosine] * 4 + [-sine, sine] * 2, 1)
+    return table.astype(np.float32).reshape(4, -1, 2 * LANES)
+
+
+def column_halves(v):
+    return v[:, : v.shape[1] // 2], v[:, v.shape[1] // 2 :]
+
+
+def shard_halves(w_qkv, w_cross_kv, w_out, w_cross_q, w_cross_out, w_up, gains, shifts, nz):
+    rows = w_qkv.shape[0]
+    up = jnp.swapaxes(w_up.reshape(rows, nz * 4, 2, -1), 1, 2).reshape(rows, -1)
+    pads = [jnp.pad(jnp.stack(v, 1), ((0, 0), (0, LANES - 3))) for v in (gains, shifts)]
+    parts = [column_halves(v) for v in (w_qkv, w_cross_kv, w_out, w_cross_q, w_cross_out, up)]
+    return jnp.stack(
+        [jnp.concatenate([parts[0][h], pads[h], *(v[h] for v in parts[1:])], 1) for h in range(2)]
+    ).astype(f32)
+
+
+def joined_halves(w):
+    return jnp.concatenate([w[h].reshape(-1, w.shape[-1]) for h in range(2)], 1)
+
+
+def local_fast(
+    tokens,
+    prefix_len,
+    neighbours,
+    neighbour_index,
+    w_qkv,
+    w_out,
+    w_cross_q,
+    w_cross_kv,
+    w_cross_out,
+    w_up,
+    w_down,
+    gain_one,
+    shift_one,
+    gain_two,
+    shift_two,
+    gain_three,
+    shift_three,
+    cotangent,
+):
+    nz = lax.axis_size("dp") // 2
+    quarter, width = tokens.shape[1:]
+    hidden = w_up.shape[1]
+    slots, rows_n = neighbours.shape[1:3]
+    length = quarter * 4
+    shards = shard_halves(
+        w_qkv, w_cross_kv, w_out, w_cross_q, w_cross_out, w_up,
+        (gain_one, gain_two, gain_three), (shift_one, shift_two, shift_three), nz,
+    )
+    weights, acts = buffers(nz, quarter, length, width, hidden, slots, rows_n, 2 * w_qkv.shape[0])
+    names = tuple(acts)
+    vmem, smem = pl.BlockSpec(memory_space=pltpu.VMEM), pl.BlockSpec(memory_space=pltpu.SMEM)
+    outs = pl.pallas_call(
+        functools.partial(forward_kernel, nz, names),
+        out_shape=[jax.ShapeDtypeStruct(*v) for v in [*weights, *acts.values()]],
+        in_specs=[vmem, vmem, vmem, smem, vmem, smem, vmem],
+        out_specs=[vmem] * (len(weights) + len(acts)),
+        scratch_shapes=[
+            pltpu.VMEM(shards.shape[1:], f32),
+            pltpu.SemaphoreType.DMA((2,)),
+            pltpu.SemaphoreType.DMA((len(CHUNKS), 12)),
+            pltpu.SemaphoreType.DMA((len(CHUNKS), 12)),
+            pltpu.SemaphoreType.DMA((6,)),
+        ],
+        compiler_params=pltpu.CompilerParams(
+            collective_id=0, has_side_effects=True, vmem_limit_bytes=60 * 2**20
+        ),
+    )(
+        shards, w_down, tokens[0], prefix_len, neighbours[0],
+        neighbour_index.reshape(-1), jnp.asarray(rope_table(length)),
+    )
+    w, a = outs[:7], dict(zip(names, outs[7:]))
+    full_qkv = jnp.concatenate([w[0][h].reshape(width, -1)[:, : 3 * width // 2] for h in range(2)], 1)
+    full_cross_kv, full_out, full_cross_q, full_cross_out, full_up = (joined_halves(w[k]) for k in range(1, 6))
+    full_down = w[6].reshape(hidden, width)
+    gain_f1, gain_f2, gain_f3 = (a["vec"][0, i] for i in range(3))
+    seq_here, heads = 1, width // HEAD
+    seq_index = lax.axis_index("seq")
+    query_pos = seq_index * quarter + jnp.arange(quarter)
+    key_pos = jnp.arange(length)
+    visible = (key_pos[None, None, :] <= query_pos[None, :, None]) | (
+        key_pos[None, None, :] < prefix_len[:, None, None]
+    )
+    cosine, sine_part = rotary_tables(query_pos)
+    unit_one, inv_one = plain_norm_parts(tokens.astype(f32))
+    unit_two, inv_two = plain_norm_parts(a["first"][None])
+    unit_three, inv_three = plain_norm_parts(a["second"][None])
+    grad_act = input_grad(cotangent, full_down)
+    grad_hidden = (grad_act * a["slope"]).astype(bf16)
+    grad_normed_three = input_grad(grad_hidden, full_up)
+    back_three, grad_gain_three, grad_shift_three = norm_back(grad_normed_three, unit_three, inv_three, gain_f3)
+    grad_second = cotangent.astype(f32) + back_three
+    grad_cross_branch = grad_second.astype(bf16)
+    spans = slots // 2
+    span_len = quarter // spans
+    grad_mixed = input_grad(grad_cross_branch, full_cross_out).astype(bf16).reshape(1, spans, span_len, heads, HEAD)
+    local_index = neighbour_index.reshape(1, slots) - seq_index * slots
+    picked = pick_slots(a["pool"][None], local_index)
+    picked = picked.reshape(1, spans, 2 * rows_n, 2 * width)
+    cross_keys = picked[..., :width].reshape(1, spans, 2 * rows_n, heads, HEAD)
+    cross_values = picked[..., width:].reshape(1, spans, 2 * rows_n, heads, HEAD)
+    cross_queries = a["cq"].reshape(1, spans, span_len, heads, HEAD)
+    cross_probs = jax.nn.softmax(
+        jnp.einsum("scqhd,sckhd->schqk", cross_queries, cross_keys, preferred_element_type=f32) * HEAD ** (-0.5), -1
+    )
+    grad_cross_probs = jnp.einsum("scqhd,sckhd->schqk", grad_mixed, cross_values, preferred_element_type=f32)
+    grad_cross_scores = (
+        cross_probs * (grad_cross_probs - jnp.sum(cross_probs * grad_cross_probs, -1, keepdims=True))
+    ).astype(bf16)
+    grad_cross_query = (
+        (jnp.einsum("schqk,sckhd->scqhd", grad_cross_scores, cross_keys, preferred_element_type=f32) * HEAD ** (-0.5))
+        .astype(bf16)
+        .reshape(1, quarter, width)
+    )
+    grad_cross_keys = jnp.einsum(
+        "schqk,scqhd->sckhd", grad_cross_scores, cross_queries, preferred_element_type=f32
+    ) * HEAD ** (-0.5)
+    grad_cross_values = jnp.einsum(
+        "schqk,scqhd->sckhd", cross_probs.astype(bf16), grad_mixed, preferred_element_type=f32
+    )
+    grad_picked = jnp.concatenate(
+        [v.reshape(1, spans, 2 * rows_n, width) for v in (grad_cross_keys, grad_cross_values)], -1
+    ).astype(bf16).reshape(slots, rows_n, 2 * width)
+    grad_pool_kv = pick_slots(grad_picked[None], slot_places(local_index))
+    grad_neighbours = input_grad(grad_pool_kv, full_cross_kv)
+    grad_normed_two = input_grad(grad_cross_query, full_cross_q)
+    back_two, grad_gain_two, grad_shift_two = norm_back(grad_normed_two, unit_two, inv_two, gain_f2)
+    grad_first = grad_second + back_two
+    grad_self_branch = grad_first.astype(bf16)
+    grad_attended = input_grad(grad_self_branch, full_out).astype(bf16).reshape(1, quarter, heads, HEAD)
+    key_heads = a["kv"].reshape(1, length, 2 * heads, HEAD)[:, :, :heads]
+    value_heads = a["kv"].reshape(1, length, 2 * heads, HEAD)[:, :, heads:]
+    logsum = jnp.swapaxes(a["lse"].reshape(heads // 2, 2, quarter).reshape(heads // 4, 1, 4, quarter), 0, 0)
+    grad_query, grad_key_all, grad_value_all = lax.map(
+        functools.partial(attend_back, visible),
+        (
+            grouped(a["q"].reshape(1, quarter, heads, HEAD)),
+            grouped(key_heads),
+            grouped(value_heads),
+            grouped(grad_attended),
+            logsum,
+        ),
+    )
+    grad_query = ungrouped(grad_query)
+    grad_key_all = ungrouped(grad_key_all).reshape(1, length, width)
+    grad_value_all = ungrouped(grad_value_all).reshape(1, length, width)
+    both = lax.psum_scatter(
+        jnp.concatenate([grad_key_all, grad_value_all], -1).astype(bf16), "seq", scatter_dimension=1, tiled=True
+    ).astype(f32)
+    grad_joined = jnp.concatenate(
+        [
+            unrotate(grad_query, cosine, sine_part).reshape(1, quarter, width),
+            unrotate(both[..., :width].reshape(1, quarter, heads, HEAD), cosine, sine_part).reshape(1, quarter, width),
+            both[..., width:],
+        ],
+        -1,
+    ).astype(bf16)
+    grad_normed_one = input_grad(grad_joined, full_qkv)
+    back_one, grad_gain_one, grad_shift_one = norm_back(grad_normed_one, unit_one, inv_one, gain_f1)
+    grad_tokens = grad_first + back_one
+    norm_grads = jnp.stack(
+        [grad_gain_one, grad_shift_one, grad_gain_two, grad_shift_two, grad_gain_three, grad_shift_three], 1
+    )
+    width_owned = lax.psum_scatter(
+        jnp.concatenate(
+            [
+                weight_grad(a["n1"], grad_joined).astype(bf16),
+                weight_grad(a["att"], grad_self_branch).astype(bf16),
+                weight_grad(a["n2"], grad_cross_query).astype(bf16),
+                weight_grad(neighbours, grad_pool_kv).astype(bf16),
+                weight_grad(a["cm"], grad_cross_branch).astype(bf16),
+                weight_grad(a["n3"], grad_hidden).astype(bf16),
+                norm_grads.astype(bf16),
+            ],
+            1,
+        ),
+        ("dp", "seq"),
+        scatter_dimension=0,
+        tiled=True,
+    ).astype(f32)
+    grad_down = weight_grad(a["act"], cotangent).astype(bf16)
+    grad_down = jnp.swapaxes(grad_down.reshape(2, nz * 4, -1, width), 0, 1).reshape(hidden, width)
+    down_owned = lax.psum_scatter(grad_down, ("dp", "seq"), scatter_dimension=0, tiled=True).astype(f32)
+    column = 8 * width + hidden
+    rows = width_owned.shape[0]
+    grad_up = width_owned[:, 8 * width : column].reshape(rows, 2, nz * 4, -1)
+    return (
+        a["out"][None],
+        grad_tokens,
+        grad_neighbours,
+        width_owned[:, : 3 * width],
+        width_owned[:, 3 * width : 4 * width],
+        width_owned[:, 4 * width : 5 * width],
+        width_owned[:, 5 * width : 7 * width],
+        width_owned[:, 7 * width : 8 * width],
+        jnp.swapaxes(grad_up, 1, 2).reshape(rows, hidden),
+        down_owned,
+        *(width_owned[:, column + i] for i in range(6)),
+    )
+
+
+def pick_slots(pool, index):
+    return jnp.stack(
+        [
+            jnp.concatenate([lax.dynamic_slice_in_dim(pool[s], index[s, j], 1, 0) for j in range(index.shape[1])], 0)
+            for s in range(index.shape[0])
+        ]
+    )
+
+
+def slot_places(index):
+    slots = index.shape[1]
+    same = index[:, :, None] == jnp.arange(slots)[None, None, :]
+    return jnp.sum(jnp.where(same, jnp.arange(slots)[None, :, None], 0), 1)
 
 
 def dense_dot(left_side, weight):
@@ -33,7 +649,7 @@
     )
 
 
-def norm_parts(array_in):
+def plain_norm_parts(array_in):
     avg_value = jnp.mean(array_in, -1, keepdims=True)
     centred = array_in - avg_value
     inv_std = lax.rsqrt(jnp.mean(centred * centred, -1, keepdims=True) + eps)
@@ -57,7 +673,7 @@
     return (jnp.cos(angles)[:, None, :], jnp.sin(angles)[:, None, :])
 
 
-def rotate(array_in, cosine, sine_part):
+def plain_rotate(array_in, cosine, sine_part):
     half_size = HEAD // 2
     first_half = array_in[..., :half_size]
     second = array_in[..., half_size:]
@@ -132,7 +748,7 @@
     return (grad_query, grad_key, grad_value)
 
 
-def local(
+def local_plain(
     tokens,
     prefix_len,
     neighbours,
@@ -197,14 +813,14 @@
     gain_f2 = full_gain_two.astype(jnp.float32)
     gain_f3 = full_gain_three.astype(jnp.float32)
     resid_in = tokens.astype(jnp.float32)
-    unit_one, inv_one = norm_parts(resid_in)
+    unit_one, inv_one = plain_norm_parts(resid_in)
     normed_one = (unit_one * gain_f1 + full_shift_one.astype(jnp.float32)).astype(jnp.bfloat16)
     joined = dense_dot(normed_one, full_qkv)
-    query_rot = rotate(
+    query_rot = plain_rotate(
         joined[..., :width].reshape(seq_here, quarter, heads, HEAD), cosine, sine_part
     ).astype(jnp.bfloat16)
     key_local = (
-        rotate(
+        plain_rotate(
             joined[..., width : 2 * width].reshape(seq_here, quarter, heads, HEAD),
             cosine,
             sine_part,
@@ -220,12 +836,12 @@
     key_heads = key_all.reshape(seq_here, length, heads, HEAD)
     value_heads = value_all.reshape(seq_here, length, heads, HEAD)
     attended, logsum = lax.map(
-        partial(attend_group, visible),
+        functools.partial(attend_group, visible),
         (grouped(query_rot), grouped(key_heads), grouped(value_heads)),
     )
     attended = ungrouped(attended).reshape(seq_here, quarter, width).astype(jnp.bfloat16)
     first_sum = resid_in + dense_dot(attended, full_out)
-    unit_two, inv_two = norm_parts(first_sum)
+    unit_two, inv_two = plain_norm_parts(first_sum)
     normed_two = (unit_two * gain_f2 + full_shift_two.astype(jnp.float32)).astype(jnp.bfloat16)
     cross_query = dense_dot(normed_two, full_cross_q).astype(jnp.bfloat16)
     pool_kv = dense_dot(neighbours, full_cross_kv).astype(jnp.bfloat16)
@@ -234,7 +850,7 @@
     span_len = quarter // spans
     neighbour_rows = 2 * neighbours.shape[2]
     local_index = neighbour_index.reshape(seq_here, slots) - seq_index * slots
-    picked = jnp.take_along_axis(pool_kv, local_index[:, :, None, None], axis=1)
+    picked = pick_slots(pool_kv, local_index)
     picked = picked.reshape(seq_here, spans, neighbour_rows, 2 * width)
     cross_keys = picked[..., :width].reshape(seq_here, spans, neighbour_rows, heads, HEAD)
     cross_values = picked[..., width:].reshape(seq_here, spans, neighbour_rows, heads, HEAD)
@@ -249,54 +865,24 @@
     )
     cross_mixed = cross_mixed.reshape(seq_here, quarter, width).astype(jnp.bfloat16)
     second_sum = first_sum + dense_dot(cross_mixed, full_cross_out)
-    unit_three, inv_three = norm_parts(second_sum)
+    unit_three, inv_three = plain_norm_parts(second_sum)
     normed_three = (unit_three * gain_f3 + full_shift_three.astype(jnp.float32)).astype(
         jnp.bfloat16
     )
     hidden_pre = dense_dot(normed_three, full_up)
     activated = jax.nn.gelu(hidden_pre, approximate=False).astype(jnp.bfloat16)
     output = (second_sum + dense_dot(activated, full_down)).astype(jnp.bfloat16)
-    backward_set = (
-        lax.all_gather(w_qkv, ("dp", "seq"), axis=0, tiled=True),
-        lax.all_gather(w_out, ("dp", "seq"), axis=0, tiled=True),
-        lax.all_gather(w_cross_q, ("dp", "seq"), axis=0, tiled=True),
-        lax.all_gather(w_cross_kv, ("dp", "seq"), axis=0, tiled=True),
-        lax.all_gather(w_cross_out, ("dp", "seq"), axis=0, tiled=True),
-        lax.all_gather(w_up, ("dp", "seq"), axis=0, tiled=True),
-        lax.all_gather(w_down, ("dp", "seq"), axis=0, tiled=True),
-        lax.all_gather(gain_one, ("dp", "seq"), axis=0, tiled=True),
-        lax.all_gather(shift_one, ("dp", "seq"), axis=0, tiled=True),
-        lax.all_gather(gain_two, ("dp", "seq"), axis=0, tiled=True),
-        lax.all_gather(shift_two, ("dp", "seq"), axis=0, tiled=True),
-        lax.all_gather(gain_three, ("dp", "seq"), axis=0, tiled=True),
-        lax.all_gather(shift_three, ("dp", "seq"), axis=0, tiled=True),
-    )
-    (
-        back_qkv,
-        back_out,
-        back_cross_q,
-        back_cross_kv,
-        back_cross_out,
-        back_up,
-        back_down,
-        back_gain_one,
-        back_shift_one,
-        back_gain_two,
-        back_shift_two,
-        back_gain_three,
-        back_shift_three,
-    ) = backward_set
-    grad_act = input_grad(cotangent, back_down)
-    _, gelu_back = jax.vjp(partial(jax.nn.gelu, approximate=False), hidden_pre)
+    grad_act = input_grad(cotangent, full_down)
+    _, gelu_back = jax.vjp(functools.partial(jax.nn.gelu, approximate=False), hidden_pre)
     grad_hidden = gelu_back(grad_act)[0].astype(jnp.bfloat16)
-    grad_normed_three = input_grad(grad_hidden, back_up)
+    grad_normed_three = input_grad(grad_hidden, full_up)
     back_three, grad_gain_three, grad_shift_three = norm_back(
-        grad_normed_three, unit_three, inv_three, back_gain_three.astype(jnp.float32)
+        grad_normed_three, unit_three, inv_three, full_gain_three.astype(jnp.float32)
     )
     grad_second = cotangent.astype(jnp.float32) + back_three
     grad_cross_branch = grad_second.astype(jnp.bfloat16)
     grad_mixed = (
-        input_grad(grad_cross_branch, back_cross_out)
+        input_grad(grad_cross_branch, full_cross_out)
         .astype(jnp.bfloat16)
         .reshape(seq_here, spans, span_len, heads, HEAD)
     )
@@ -334,27 +920,21 @@
         -1,
     )
     grad_picked = grad_picked.reshape(seq_here, slots, neighbours.shape[2], 2 * width)
-    seq_rows = jnp.arange(seq_here)[:, None]
-    grad_pool_kv = (
-        jnp.zeros(pool_kv.shape, jnp.float32)
-        .at[seq_rows, local_index]
-        .add(grad_picked)
-        .astype(jnp.bfloat16)
-    )
-    grad_neighbours = input_grad(grad_pool_kv, back_cross_kv)
-    grad_normed_two = input_grad(grad_cross_query, back_cross_q)
+    grad_pool_kv = pick_slots(grad_picked.astype(jnp.bfloat16), slot_places(local_index))
+    grad_neighbours = input_grad(grad_pool_kv, full_cross_kv)
+    grad_normed_two = input_grad(grad_cross_query, full_cross_q)
     back_two, grad_gain_two, grad_shift_two = norm_back(
-        grad_normed_two, unit_two, inv_two, back_gain_two.astype(jnp.float32)
+        grad_normed_two, unit_two, inv_two, full_gain_two.astype(jnp.float32)
     )
     grad_first = grad_second + back_two
     grad_self_branch = grad_first.astype(jnp.bfloat16)
     grad_attended = (
-        input_grad(grad_self_branch, back_out)
+        input_grad(grad_self_branch, full_out)
         .astype(jnp.bfloat16)
         .reshape(seq_here, quarter, heads, HEAD)
     )
     grad_query, grad_key_all, grad_value_all = lax.map(
-        partial(attend_back, visible),
+        functools.partial(attend_back, visible),
         (
             grouped(query_rot),
             grouped(key_heads),
@@ -384,9 +964,9 @@
         ],
         -1,
     ).astype(jnp.bfloat16)
-    grad_normed_one = input_grad(grad_joined, back_qkv)
+    grad_normed_one = input_grad(grad_joined, full_qkv)
     back_one, grad_gain_one, grad_shift_one = norm_back(
-        grad_normed_one, unit_one, inv_one, back_gain_one.astype(jnp.float32)
+        grad_normed_one, unit_one, inv_one, full_gain_one.astype(jnp.float32)
     )
     grad_tokens = grad_first + back_one
     norm_grads = jnp.stack(
@@ -442,8 +1022,10 @@
 
 
 def solution(mesh):
+    sizes = dict(mesh.shape)
+    fits = sizes == {"dp": 8, "seq": 4}
     return jax.shard_map(
-        local,
+        local_fast if fits else local_plain,
         mesh=mesh,
         in_specs=(
             P("dp", "seq", None),

time: 1260 us -> 640 us (0.51)
  waiting for transfers between devices: 875 us -> 204 us
  Pallas kernels: 0 us -> 134 us
  matrix products: 133 us -> 64.9 us
  blocking collectives: 40.9 us -> 0 us
  between operations: 15.9 us -> 46.7 us
  other arithmetic: 53.4 us -> 26.3 us
  local copies, waits for them, and re-layouts: 131 us -> 152 us
    all_gather x9 -> x0, waiting for transfers between devices: 327 us -> none  [the longest x1 62.1 us: local(): lax.all_gather(w_up, ('dp', 'seq'), axis=0, tiled=True)]
    unnamed x14 -> x4, waiting for transfers between devices: 415 us -> 167 us
    pallas_call x0 -> x1, Pallas kernels: none -> 134 us  [local_fast(): pl.pallas_call(functools.partial(forward_kernel, nz, names), out_shape=[j...]
    reduce_scatter x3 -> x2, waiting for transfers between devices: 133 us -> 36.1 us  [the longest x1 36.1 us: local_fast(): lax.psum_scatter(grad_down, ('dp', 'seq'), scatter_dimension=0, tiled=True)]
    unnamed x1 -> x0, blocking collectives: 40.9 us -> none
    dot_general x15 -> x4, matrix products: 47.4 us -> 8.91 us  [the longest x1 3.79 us: local_fast(): jnp.einsum('scqhd,sckhd->schqk', grad_mixed, cross_values, preferred_elem...]
    unnamed x144 -> x141, local copies, waits for them, and re-layouts: 9.8 us -> 31.4 us
    concatenate x5 -> x7, local copies, waits for them, and re-layouts: 48.7 us -> 31.5 us  [the longest x1 23.6 us: local_fast(): jnp.concatenate([weight_grad(a['n1'], grad_joined).astype(bf16), weight_g...]
  transfers between devices with their start and end apart: 13 -> 3, of which waited for: 11 -> 2; matrix products, arithmetic and copies ran while one was open for 17% -> 15% of each run, Pallas kernels for 0% -> 0%
where the time goes in v1:
time: 640 us; the launch traced here: 628 us
  waiting for transfers between devices  204 us (32%)
  local copies, waits for them, and re-layouts  152 us (24%)
  Pallas kernels  134 us (21%)
  matrix products  64.9 us (10%)
  between operations  46.7 us (7%)
  other arithmetic  26.3 us (4%)
    unnamed x4, waiting for transfers between devices  167 us
    pallas_call x1, Pallas kernels, local_fast(): pl.pallas_call(functools.partial(forward_kernel, nz, names), out_shape=[j...  134 us
    reduce_scatter x1, waiting for transfers between devices, local_fast(): lax.psum_scatter(grad_down, ('dp', 'seq'), scatter_dimension=0, tiled=True)  36.1 us
    unnamed x141, local copies, waits for them, and re-layouts  31.4 us
    concatenate x1, local copies, waits for them, and re-layouts, local_fast(): jnp.concatenate([weight_grad(a['n1'], grad_joined).astype(bf16), weight_g...  23.6 us
    dot_general x7, matrix products, weight_grad(): lax.dot_general(flat_left, flat_grad, (((0,), (0,)), ((), ())), preferred...  18.6 us
    dot_general x7, matrix products, input_grad(): lax.dot_general(grad_out, weight, (((grad_out.ndim - 1,), (1,)), ((), ())...  14.5 us
  transfers between devices with their start and end apart: 3, of which 2 were waited for; matrix products, arithmetic and copies ran while one was open for 15% of the time, Pallas kernels for 0%

profile of v1, /device:TPU:1, one launch (start us, length us, event | category | flops | bytes accessed | tf_op | source)
XLA Modules:
  0.0 628.0 jit_solution(8779644304069997436)
XLA Ops:
  29.0 133.6 %shard_map.306 = (bf16[2,4,4,48,1280]{4,3,2,1,0:T(8,128)(2,1)}, bf16[2,4,4,48,768]{4,3,2,1,0:T(8,128)(2,1)}, bf16[2,4,4,48,384]{4,3,2,1,0:T(8,128)(2,1)}, bf16[2...) custom-call(f32[2,24,4736]{2,1,0:T(8,128)} %maximum_convert_fusion.a, ...), custom_call_target="tpu_custom_call" | custom-call | tf_op jit(solution)/shard_map/pallas_call | solution.py:467
  163.9 1.5 multiply_reduce_fusion.8
  165.4 1.5 slice_reduce_fusion.6
  166.9 3.0 fusion.126
  170.0 1.5 fusion.47
  171.5 3.0 multiply_reduce_fusion.3
  177.2 1.8 dynamic-slice_dynamic-update-slice_fusion.7
  179.6 1.8 dynamic-slice_dynamic-update-slice_fusion.6
  182.0 1.8 dynamic-slice_dynamic-update-slice_fusion.5
  184.4 1.8 dynamic-slice_dynamic-update-slice_fusion.4
  186.8 1.8 dynamic-slice_dynamic-update-slice_fusion.3
  189.3 1.8 dynamic-slice_dynamic-update-slice_fusion.2
  191.7 1.8 dynamic-slice_dynamic-update-slice_fusion.1
  194.1 1.8 dynamic-slice_dynamic-update-slice_fusion
  195.9 3.7 fusion.129
  199.6 1.8 copy.150
  201.4 1.6 reshape.724
  203.0 1.8 copy.165
  204.8 1.7 fusion.133
  208.3 1.6 reshape.725
  209.9 1.8 copy.167
  211.7 3.3 copy.154
  215.0 2.7 fusion.138
  217.6 3.8 multiply_reduce_fusion.1
  224.2 1.5 fusion.132
  225.7 2.2 multiply_reduce_fusion.4
  229.0 5.9 copy.157
  234.9 6.1 reshape.695
  241.0 3.5 fusion.128
  247.1 1.5 fusion.131
  252.1 1.9 copy.160
  255.2 31.5 %while.15 = (s32[]{:T(128)}, f32[3,1,256,4,64]{2,4,3,1,0:T(8,128)}, bf16[3,1,1024,4,64]{2,4,3,1,0:T(8,128)(2,1)}, bf16[3,1,1024,4,64]{2,4,3,1,0:T(8,128)(2,1)}, ...) while((s32[]{:T(128)}, f32[3,1,256,4,64]{2,4,3,1,0:T(8,128)}, ...), condition=%wide.region_15.16_spmd.clone, body=%wide.region_13.15_spmd.clone.sunk | while | flops 687668224 | bytes 63741224 | solution.py:548
  256.4 2.8 multiply_reduce_fusion.13
  266.8 2.8 multiply_reduce_fusion.13
  270.8 1.5 fusion.189
  277.3 2.8 multiply_reduce_fusion.13
  286.7 3.8 pad_maximum_fusion
  293.4 2.5 copy.182
  296.7 2.8 fusion.63
  299.6 1.7 fusion.62
  302.6 1.6 fusion.127
  304.3 1.5 convolution_convert_fusion.7
  316.9 2.9 slice.283
  324.4 2.6 copy.166
  327.0 2.0 concatenate.100
  329.0 2.2 copy.169
  331.2 2.4 copy.171
  333.5 2.5 convolution_convert_fusion.5
  336.0 2.4 copy.172
  344.0 1.7 copy-done.44
  346.4 3.9 fusion.52
  350.3 2.9 copy.173
  353.3 2.6 convolution_convert_fusion.6
  355.9 2.5 copy.174
  363.1 3.6 convolution_convert_fusion.1
  370.1 1.9 fusion.86
  373.8 3.0 convolution_convert_fusion.2
  376.8 23.6 %concatenate.105 = bf16[768,9222]{1,0:T(8,128)(2,1)} concatenate(bf16[768,2304]{1,0:T(8,128)(2,1)} %convolution_convert_fusion.2, bf16[768,768]{1,0:T(8,128)(2,1)} %copy.171, bf16[768,768]{1,0:T(8,128)(2,1)} %copy.172, bf16[768,1536]{1,0:T(8,128)(2,1)S(1)} %copy.173, bf16[768,768]{1,0:T(8,128)(2,1)} %copy.174, bf16[768,3072]{1,0:T(8,128)(2,1)} %convolution_convert_fusion.1, ...), dimensions={1} | concatenate | bytes 28329984 | tf_op jit(solution)/shard_map/concatenate | solution.py:579
  400.5 1.7 copy-done.18
  402.4 1.7 copy-done.45
  404.1 4.3 fusion.59
  408.4 36.1 %reduce-scatter.8.cloned.1.call-done = bf16[96,768]{1,0:T(8,128)(2,1)} async-done(((bf16[3072,768]{1,0:T(8,128)(2,1)}), bf16[96,768]{1,0:T(8,128)(2,1)}) %reduce-scatter.8.cloned.1.call-update) | async-done | bytes 147472 | tf_op jit(solution)/shard_map/reduce_scatter | solution.py:597
  444.5 1.6 convert_element_type.147
  447.4 167.4 %reduce-scatter.10.cloned.1.call-done = bf16[24,9222]{1,0:T(8,128)(2,1)} async-done(((bf16[768,9222]{1,0:T(8,128)(2,1)}), bf16[24,9222]{1,0:T(8,128)(2,1)}) %reduce-scatter.10.cloned.1.call-update) | async-done | bytes 442672
  (283 shorter events, 77.0 us)
Async XLA Ops:
  7.2 359.5 %reduce-scatter.6.cloned.1.call-start = ((), (), s32[]{:S(2)}) async-start(), calls=%async_computation.3 | async-start | bytes 3932160 | tf_op jit(solution)/shard_map/reduce_scatter | solution.py:561
  163.8 6.0 slice-start
  165.4 6.1 copy-start.54
  166.9 3.0 copy-start.21
  166.9 3.0 slice-start.1
  166.9 3.1 copy-start.65
  170.0 1.5 copy-start.4
  171.4 3.0 copy-start.23
  171.5 4.1 copy-start.1
  175.7 50.0 %copy-start.49 = (f32[256]{0:T(256)}, f32[256]{0:T(256)S(1)}, u32[]{:S(2)}) copy-start(f32[256]{0:T(256)S(1)} %broadcast_multiply_fusion.5) | copy-start | bytes 3076
  199.6 1.8 copy-start.39
  204.8 10.2 %copy-start.11 = (bf16[4,64,12,64]{1,3,2,0:T(8,128)(2,1)}, bf16[4,64,12,64]{1,3,2,0:T(8,128)(2,1)S(1)}, u32[]{:S(2)}) copy-start(bf16[4,64,12,64]{1,3,2,0:T(8,128)(2,1)S(1)} %copy.165) | copy-start | bytes 1179652
  204.8 1.8 copy-start.34
  204.8 1.8 copy-start.55
  204.8 1.8 copy-start.56
  204.8 1.7 copy-start.57
  211.7 6.0 copy-start.32
  217.6 3.8 copy-start.40
  217.6 3.8 copy-start
  223.0 2.7 copy-start.2
  223.0 2.7 copy-start.52
  224.2 3.7 copy-start.30
  241.0 4.7 copy-start.48
  247.0 1.6 copy-start.3
  247.0 1.7 copy-start.9
  247.0 1.9 copy-start.35
  247.0 1.9 copy-start.50
  247.0 1.9 copy-start.53
  247.1 1.9 copy-start.58
  260.4 1.5 copy-start.26
  262.4 2.2 copy-start.27
  270.8 1.5 copy-start.26
  272.8 2.2 copy-start.27
  281.3 1.5 copy-start.26
  283.2 2.2 copy-start.27
  290.5 1.5 copy-start.22
  290.5 154.0 %reduce-scatter.8.cloned.1.call-start = ((), (), s32[]{:S(2)}) async-start(), calls=%async_computation.4 | async-start | bytes 4866048 | tf_op jit(solution)/shard_map/reduce_scatter | solution.py:597
  296.0 318.8 %reduce-scatter.10.cloned.1.call-start = ((), (), s32[]{:S(2)}) async-start(), calls=%async_computation.5 | async-start | bytes 14800896
  296.7 2.9 copy-start.12
  299.6 3.0 copy-start.15
  302.6 1.6 copy-start.6
  302.6 1.7 copy-start.37
  329.0 4.5 copy-start.31
  343.9 2.5 copy-start.25
  344.0 1.7 copy-start.44
  350.3 3.0 copy-start.10
  353.3 6.0 copy-start.61
  353.3 6.8 %copy-start.60 = (bf16[768]{0:T(1024)(128)(2,1)S(1)}, bf16[768]{0:T(1024)(128)(2,1)}, u32[]{:S(2)}) copy-start(bf16[768]{0:T(1024)(128)(2,1)} %get-tuple-element.189) | copy-start | bytes 4612
  353.3 7.7 %copy-start.59 = (bf16[768]{0:T(1024)(128)(2,1)S(1)}, bf16[768]{0:T(1024)(128)(2,1)}, u32[]{:S(2)}) copy-start(bf16[768]{0:T(1024)(128)(2,1)} %get-tuple-element.203) | copy-start | bytes 4612
  353.3 8.5 %copy-start.13 = (bf16[1,256,768]{2,1,0:T(8,128)(2,1)S(1)}, bf16[1,256,768]{2,1,0:T(8,128)(2,1)}, u32[]{:S(2)}) copy-start(bf16[1,256,768]{2,1,0:T(8,128)(2,1)} %param.21) | copy-start | bytes 1179652
  355.9 2.5 copy-start.62
  355.9 6.3 %copy-start.51 = (f32[256]{0:T(256)S(1)}, f32[256]{0:T(256)}, u32[]{:S(2)}) copy-start(f32[256]{0:T(256)} %get-tuple-element.301) | copy-start | bytes 3076
  355.9 7.1 %copy-start.36 = (bf16[256,768]{1,0:T(8,128)(2,1)S(1)}, bf16[256,768]{1,0:T(8,128)(2,1)}, u32[]{:S(2)}) copy-start(bf16[256,768]{1,0:T(8,128)(2,1)} %get-tuple-element.117) | copy-start | bytes 1179652
  358.4 4.7 copy-start.24
  368.0 1.6 copy-start.19
  368.0 2.1 copy-start.20
  368.0 2.1 copy-start.46
  370.1 3.7 copy-start.66
  400.4 1.8 copy-start.18
  402.2 1.9 copy-start.45
  404.1 42.0 %copy-start.64 = (f32[256]{0:T(256)S(1)}, f32[256]{0:T(256)}, u32[]{:S(2)}) copy-start(f32[256]{0:T(256)} %get-tuple-element.194) | copy-start | bytes 3076
  404.1 42.1 %copy-start.7 = (f32[1,256,768]{2,1,0:T(8,128)S(1)}, f32[1,256,768]{2,1,0:T(8,128)}, u32[]{:S(2)}) copy-start(f32[1,256,768]{2,1,0:T(8,128)} %copy-done.5) | copy-start | bytes 2359300
  614.7 2.6 copy-start.14
  615.7 4.5 copy-start.38
  (20 other events, 22.2 us)
Sparse Core Ops, SparseCore 0:
  290.7 41.9 reduce-scatter.5
  339.0 105.4 reduce-scatter.7
  450.7 164.0 reduce-scatter.9

commit v2 on v1

--- a/solution.py
+++ b/solution.py
@@ -155,7 +155,7 @@
     return v * cosine + swap_halves(v) * signed
 
 
-def forward(p, r, g, kv_sem):
+def forward(p, r, g, swap, kv_sem, pairs):
     n = len(g.chunks)
     c, z = p.c, p.z
     w = r.w
@@ -172,6 +172,8 @@
 
     first = remote(r.shards.at[p.o], r.beside, r.pair_sem.at[0], r.pair_sem.at[1], p.to_c)
     first.start()
+    rope = pltpu.make_async_copy(r.rope_table.at[p.s], r.rope, r.rope_sem)
+    rope.start()
     w[6][c, z, p.own] = r.w_down[...]
     first.wait_recv()
     start = 0
@@ -185,6 +187,9 @@
             if g.chunks[q][0] == k:
                 g.along_z(q)
     step(0)
+    swap.send("cot", r.cotangent, r.by_cot)
+    swap.send("nb", r.neighbours, r.by_neighbours)
+    rope.wait()
     tokens = r.tokens[...].astype(f32)
     unit, _ = norm_parts(tokens)
     step(1)
@@ -198,7 +203,8 @@
         return (v * r.vec[0, i : i + 1] + r.vec[1, i : i + 1]).astype(bf16)
 
     r.n1[...] = affine(unit, 0)
-    cosine, signed = r.rope[p.s, :, :LANES], r.rope[p.s, :, LANES:]
+    swap.send("n1", r.n1, r.by_n1)
+    cosine, signed = r.rope[:, :LANES], r.rope[:, LANES:]
     for i in (2, 3, 4, 5, 0, 1):
         joined = dot(r.n1[...], half_of(w[0], i // 3, (i % 3) * 384, 384))
         if i < 4:
@@ -260,17 +266,19 @@
         r.att[:, cols] = jnp.where(low_lane, mixed[:quarter], mixed[quarter:]).astype(bf16)
         return carry
 
-    lax.fori_loop(0, 3, self_pair, 0)
+    lax.fori_loop(0, pairs // 2, self_pair, 0)
     step(5)
-    lax.fori_loop(3, 6, self_pair, 0)
+    lax.fori_loop(pairs // 2, pairs, self_pair, 0)
     g.ready(2)
 
     def project(v, k):
         return jnp.concatenate([dot(v, half_of(w[k], h)) for h in range(2)], 1)
 
+    swap.send("att", r.att, r.by_att)
     first_sum = tokens + project(r.att[...], 2)
     r.first[...] = first_sum
     r.n2[...] = affine(norm_parts(first_sum)[0], 1)
+    swap.send("n2", r.n2, r.by_n2)
     step(6)
     g.ready(3)
     r.cq[...] = project(r.n2[...], 3).astype(bf16)
@@ -296,12 +304,14 @@
             r.cm[rows, cols] = jnp.where(low_lane, mixed[:span], mixed[span:]).astype(bf16)
         return carry
 
-    lax.fori_loop(0, 6, cross_pair, 0)
+    lax.fori_loop(0, pairs, cross_pair, 0)
     step(7)
     g.ready(4)
+    swap.send("cm", r.cm, r.by_cm)
     second_sum = r.first[...] + project(r.cm[...], 4)
     r.second[...] = second_sum
     r.n3[...] = affine(norm_parts(second_sum)[0], 2)
+    swap.send("n3", r.n3, r.by_n3)
     step(8)
     hidden_half = w[5].shape[-1]
 
@@ -324,6 +334,7 @@
     step(9)
     g.ready(6)
     up_tiles(768, 768, 256)
+    swap.send("act", r.act.at[:, pl.ds(pl.multiple_of(p.o * hidden_half, LANES), hidden_half)], r.by_act)
     step(10)
     for q in (7, 8):
         g.ready(q)
@@ -336,41 +347,400 @@
         cp.wait_send()
 
 
+class Reduce:
+    def __init__(self, place, r, chunks, send, recv):
+        self.p, self.r, self.w, self.chunks, self.ss, self.rs = place, r, r.w, chunks, send, recv
+        self.sent, self.open, self.under_way = [], set(), {}
+        self.starts = [sum(v.shape[-1] for v in r.w[:k]) for k in range(6)]
+
+    def free(self, k):
+        p = self.p
+        for device in (p.to_x, p.to_y, *p.to_z):
+            pl.semaphore_signal(self.r.credit.at[k], inc=1, device_id=device, device_id_type=MESH)
+
+    def at(self, q, half, z, xy):
+        k, start, width, _ = self.chunks[q]
+        return self.w[k].at[half, z, xy, :, pl.ds(start, width)]
+
+    def load(self, q, half, z, xy):
+        k, start, width, _ = self.chunks[q]
+        return self.w[k][half, z, xy, :, start : start + width].astype(f32)
+
+    def save(self, q, half, z, xy, v):
+        k, start, width, _ = self.chunks[q]
+        self.w[k][half, z, xy, :, start : start + width] = v.astype(bf16)
+
+    def copy(self, q, j, src, dst, device):
+        cp = remote(src, dst, self.ss.at[q, j], self.rs.at[q, j], device)
+        cp.start()
+        self.sent.append(cp)
+
+    def wait(self, q, j, ref):
+        remote(ref, ref, self.ss.at[q, j], self.rs.at[q, j], self.p.to_c).wait_recv()
+
+    def diagonal(self, q):
+        p, (k, _, _, cut) = self.p, self.chunks[q]
+        if k not in self.open:
+            pl.semaphore_wait(self.r.credit.at[k], 1 + p.nz)
+            self.open.add(k)
+        for j, z, device in ((0, pl.ds(0, cut), p.to_y), (1, pl.ds(cut, p.nz - cut), p.to_x)):
+            self.copy(q, j, self.at(q, p.c, z, p.at_d), self.at(q, p.o, z, 0), device)
+
+    def across(self, q):
+        p, cut, allz = self.p, self.chunks[q][3], slice(None)
+        for j, zs, to in ((0, range(cut), p.at_x), (1, range(cut, p.nz), p.at_y)):
+            self.wait(q, j, self.at(q, p.o, pl.ds(zs[0], len(zs)), 0))
+            for z in zs:
+                self.save(q, p.c, z, to, self.load(q, p.c, z, to) + self.load(q, p.o, z, 0))
+        self.copy(q, 2, self.at(q, p.c, allz, p.at_x), self.at(q, p.o, allz, 1), p.to_x)
+        self.copy(q, 3, self.at(q, p.c, allz, p.at_y), self.at(q, p.o, allz, 2), p.to_y)
+
+    def along_z(self, q):
+        p, allz = self.p, slice(None)
+        self.wait(q, 2, self.at(q, p.o, allz, 1))
+        self.wait(q, 3, self.at(q, p.o, allz, 2))
+        for z in range(p.nz):
+            total = self.load(q, p.c, z, p.own) + self.load(q, p.o, z, 1) + self.load(q, p.o, z, 2)
+            self.save(q, p.c, z, p.own, total)
+        for j, device in enumerate(p.to_z):
+            self.copy(q, 4 + j, self.at(q, p.c, p.z_of[j], p.own), self.at(q, p.o, j, 3), device)
+
+    def last(self, q):
+        p, r, (k, start, width, _) = self.p, self.r, self.chunks[q]
+        total = self.load(q, p.c, p.z, p.own)
+        for j in range(p.nz - 1):
+            self.wait(q, 4 + j, self.at(q, p.o, j, 3))
+            total = total + self.load(q, p.o, j, 3)
+        cols = slice(start, start + width)
+        if k == 6:
+            r.sums[6][:, cols] = total
+            return
+        rows = total.shape[0] // 2
+        r.sums[k][p.c, :, cols] = jnp.where(p.c == 0, total[:rows], total[rows:])
+        there = slice(self.starts[k] + start, self.starts[k] + start + width)
+        r.beside[:, there] = jnp.where(p.c == 0, total[rows:], total[:rows])
+        self.copy(q, 7, r.beside.at[:, there], r.sums[k].at[p.c, :, cols], p.to_c)
+
+    def finish(self, q):
+        p, (k, start, width, _) = self.p, self.chunks[q]
+        if k != 6:
+            self.wait(q, 7, self.r.sums[k].at[p.o, :, pl.ds(start, width)])
+
+    def push(self, q=None):
+        if q is not None:
+            self.diagonal(q)
+        for other in sorted(self.under_way, reverse=True):
+            (self.across, self.along_z, self.last)[self.under_way[other]](other)
+            self.under_way[other] += 1
+            if self.under_way[other] == 3:
+                del self.under_way[other]
+        if q is not None:
+            self.under_way[q] = 0
+
+    def drain(self):
+        while self.under_way:
+            self.push()
+        for q in range(len(self.chunks)):
+            self.finish(q)
+
+
+class Swap:
+    def __init__(self, place, sems):
+        self.p, self.sems, self.n, self.sent, self.landed = place, sems, 0, [], {}
+
+    def send(self, name, src, dst):
+        cp = remote(src, dst, self.sems.at[0, self.n], self.sems.at[1, self.n], self.p.to_c)
+        cp.start()
+        self.sent.append(cp)
+        self.landed[name] = cp
+        self.n += 1
+
+    def wait(self, name):
+        self.landed.pop(name).wait_recv()
+
+
+def norm_back_at(grad, v, gain):
+    unit, inv = norm_parts(v)
+    scaled = grad * gain
+    back = inv * (
+        scaled - jnp.mean(scaled, -1, keepdims=True) - unit * jnp.mean(scaled * unit, -1, keepdims=True)
+    )
+    return back, jnp.sum(grad * unit, 0, keepdims=True), jnp.sum(grad, 0, keepdims=True)
+
+
+def backward(p, r, g, swap, red, kv_sem, pairs):
+    w, c, o = r.w, p.c, p.o
+    quarter, width = r.tokens.shape
+    hidden_half, pool_half = w[5].shape[-1], w[1].shape[-1]
+    slots, rows_n = r.neighbours.shape[:2]
+    low_lane, low, high = lane_masks()
+    r.vec_sum[...] = jnp.zeros_like(r.vec_sum)
+
+    def half(ref, h, size):
+        return ref.at[:, pl.ds(pl.multiple_of(h * size, LANES), size)]
+
+    def input_grad(ref, k, size):
+        return sum(dot(ref[:, h * size : (h + 1) * size], half_of(w[k], h, 0, size), NT) for h in range(2))
+
+    def weight_grad(k, left, left_beside, right, right_beside, size, tile=384, base=0, tiles=2):
+        rows, per = w[k].shape[3], tile // (4 * w[k].shape[3])
+        cut = size // 2 if size > 768 and size % 256 == 0 else size
+        if size == 1152:
+            cut = 384
+
+        def body(i, carry):
+            cols = pl.ds(pl.multiple_of(base + i * tile, LANES), tile)
+            beside = pl.ds(pl.multiple_of(i * tile, LANES), tile)
+            for start in range(0, size, cut):
+                part = dot(left(cols), right(start, cut), TN) + dot(left_beside(beside), right_beside(start, cut), TN)
+                w[k][c, pl.ds(i * per, per), :, :, start : start + cut] = part.astype(bf16).reshape(per, 4, rows, cut)
+            return carry
+
+        lax.fori_loop(0, tiles, body, 0)
+
+    def plain_grad(k, left, left_beside, right, right_beside, size):
+        weight_grad(
+            k,
+            lambda cols: left[:, cols],
+            lambda cols: left_beside[:, cols],
+            lambda start, n: right[:, pl.ds(pl.multiple_of(c * size + start, LANES), n)],
+            lambda start, n: right_beside[:, start : start + n],
+            size,
+        )
+
+    def gain(i):
+        return r.vec[0, i : i + 1]
+
+    def keep_vec(i, gain_sum, shift_sum):
+        r.vec_sum[0, i : i + 1] = gain_sum
+        r.vec_sum[1, i : i + 1] = shift_sum
+
+    def act_tile(i, carry):
+        h, z = lax.div(i, p.nz), lax.rem(i, p.nz)
+        rows = w[6][h, z].reshape(-1, width)
+        cols = pl.ds(pl.multiple_of(i * rows.shape[0], LANES), rows.shape[0])
+        r.slope[:, cols] = (dot(r.cotangent[...], rows, NT) * r.slope[:, cols].astype(f32)).astype(bf16)
+        return carry
+
+    lax.fori_loop(0, 2 * p.nz, act_tile, 0)
+    gh = r.slope
+    red.free(6)
+    swap.send("gh", half(gh, o, hidden_half), r.by_hidden_grad)
+    for name in ("act", "cot"):
+        swap.wait(name)
+    for q in (7, 8):
+        g.settle(q)
+    down_rows = 4 * w[6].shape[3]
+    weight_grad(
+        6,
+        lambda cols: r.act[:, cols],
+        lambda cols: r.by_act[:, cols],
+        lambda start, n: r.cotangent[:, start : start + n],
+        lambda start, n: r.by_cot[:, start : start + n],
+        width,
+        tile=down_rows,
+        base=c * hidden_half,
+        tiles=p.nz,
+    )
+    red.push(0)
+    red.push(1)
+    grad_three = input_grad(gh, 5, hidden_half)
+    red.free(5)
+    for q in (5, 6):
+        g.settle(q)
+    back, dg, db = norm_back_at(grad_three, r.second[...], gain(2))
+    keep_vec(2, dg, db)
+    grad_second = r.cotangent[...].astype(f32) + back
+    r.second[...] = grad_second
+    r.branch[...] = grad_second.astype(bf16)
+    swap.send("gcb", half(r.branch, o, width // 2), r.by_branch)
+    r.mixed_grad[...] = input_grad(r.branch, 4, width // 2).astype(bf16)
+    red.free(4)
+    g.settle(4)
+    for name in ("gh", "n3"):
+        swap.wait(name)
+    plain_grad(5, r.n3, r.by_n3, gh, r.by_hidden_grad, hidden_half)
+    red.push(2)
+    red.push(3)
+
+    span = quarter // (slots // 2)
+
+    def cross_pair(i, carry):
+        cols = pl.ds(pl.multiple_of(i * LANES, LANES), LANES)
+        vcols = pl.ds(pl.multiple_of(i * LANES + pool_half, LANES), LANES)
+        for b in range(slots // 2):
+            two = [lax.rem(r.index[2 * b + j], slots) for j in range(2)]
+            rows = slice(b * span, (b + 1) * span)
+            queries = stacked(r.cq[rows, cols], low, high) * bf16(HEAD**-0.5)
+            grads = stacked(r.mixed_grad[rows, cols], low, high)
+            keys = jnp.concatenate([r.pool[t, :, cols] for t in two], 0)
+            values = jnp.concatenate([r.pool[t, :, vcols] for t in two], 0)
+            probs = jnp.exp(dot(keys, queries, NT) - r.lse_cross[i, b : b + 1])
+            grad_probs = dot(values, grads, NT)
+            score_grad = (probs * (grad_probs - jnp.sum(probs * grad_probs, 0, keepdims=True))).astype(bf16)
+            r.gkv[b, :, cols] = dot(score_grad, queries).astype(bf16)
+            r.gkv[b, :, vcols] = dot(probs.astype(bf16), grads).astype(bf16)
+            gq = dot(score_grad, keys, TN) * HEAD**-0.5
+            r.cq_grad[rows, cols] = jnp.where(low_lane, gq[:span], gq[span:]).astype(bf16)
+        return carry
+
+    lax.fori_loop(0, pairs, cross_pair, 0)
+    swap.send("gcq", half(r.cq_grad, o, width // 2), r.by_cq_grad)
+    grad_two = input_grad(r.cq_grad, 3, width // 2)
+    red.free(3)
+    g.settle(3)
+    back, dg, db = norm_back_at(grad_two, r.first[...], gain(1))
+    keep_vec(1, dg, db)
+    grad_first = r.second[...] + back
+    r.first[...] = grad_first
+    r.self_branch[...] = grad_first.astype(bf16)
+    swap.send("gsb", half(r.self_branch, o, width // 2), r.by_self_branch)
+    r.att_grad[...] = input_grad(r.self_branch, 2, width // 2).astype(bf16)
+    red.free(2)
+    g.settle(2)
+    for s in range(slots):
+        j = 0
+        for k in range(slots):
+            j = jnp.where(lax.rem(r.index[k], slots) == s, k, j)
+        b, odd = lax.div(j, 2), lax.rem(j, 2)
+        r.pool_grad[s] = jnp.where(odd == 0, r.gkv[b, :rows_n], r.gkv[b, rows_n:])
+    swap.send("gp", r.pool_grad.at[:, :, pl.ds(pl.multiple_of(o * pool_half, LANES), pool_half)], r.by_pool_grad)
+    swap.wait("gcb")
+    swap.wait("cm")
+    plain_grad(4, r.cm, r.by_cm, r.branch, r.by_branch, width // 2)
+    red.push(4)
+
+    cosine, signed = r.rope[:, :LANES], r.rope[:, LANES:]
+    place = lax.rem(lax.broadcasted_iota(jnp.int32, (1, 2 * quarter), 1), quarter) + p.s * quarter
+    limit = jnp.maximum(place, r.prefix[0] - 1)
+
+    def self_pair(i, carry):
+        cols = pl.ds(pl.multiple_of(i * LANES, LANES), LANES)
+        vcols = pl.ds(pl.multiple_of(i * LANES + pool_half, LANES), LANES)
+        queries = stacked(r.q[:, cols], low, high) * bf16(HEAD**-0.5)
+        grads = stacked(r.att_grad[:, cols], low, high)
+        keys = r.kv[:, :, cols].reshape(-1, LANES)
+        values = r.kv[:, :, vcols].reshape(-1, LANES)
+        scores = dot(keys, queries, NT)
+        key_place = lax.broadcasted_iota(jnp.int32, scores.shape, 0)
+        probs = jnp.exp(jnp.where(key_place <= limit, scores, masked) - r.lse[i])
+        grad_probs = dot(values, grads, NT)
+        score_grad = (probs * (grad_probs - jnp.sum(probs * grad_probs, 0, keepdims=True))).astype(bf16)
+        r.gkv[:, :, cols] = dot(score_grad, queries).astype(bf16).reshape(4, quarter, LANES)
+        r.gkv[:, :, vcols] = dot(probs.astype(bf16), grads).astype(bf16).reshape(4, quarter, LANES)
+        gq = dot(score_grad, keys, TN) * HEAD**-0.5
+        gq = jnp.where(low_lane, gq[:quarter], gq[quarter:])
+        r.joined_grad[:, cols] = rotate(gq, cosine, -signed).astype(bf16)
+        return carry
+
+    lax.fori_loop(0, pairs // 2, self_pair, 0)
+    red.push()
+    lax.fori_loop(pairs // 2, pairs, self_pair, 0)
+    swap.send("far", r.gkv.at[p.s_d], r.kv_far)
+    swap.send("near", r.gkv.at[p.s_c], r.kv_near)
+    swap.wait("gcq")
+    swap.wait("n2")
+    plain_grad(3, r.n2, r.by_n2, r.cq_grad, r.by_cq_grad, width // 2)
+    swap.wait("far")
+    r.gkv[p.s_y] = (r.gkv[p.s_y].astype(f32) + r.kv_far[...].astype(f32)).astype(bf16)
+    far = remote(r.gkv.at[p.s_y], r.kv_y, kv_sem.at[6], kv_sem.at[7], p.to_y)
+    far.start()
+    red.push(5)
+    swap.wait("gsb")
+    swap.wait("att")
+    plain_grad(2, r.att, r.by_att, r.self_branch, r.by_self_branch, width // 2)
+    red.push(6)
+
+    out = [None, None]
+    for s in range(slots):
+        rows = r.pool_grad[s]
+        part = sum(
+            dot(rows[:, h * pool_half : (h + 1) * pool_half], half_of(w[1], h), NT) for h in range(2)
+        )
+        if out[s % 2] is not None:
+            out[s % 2].wait()
+        r.stage[s % 2] = part
+        out[s % 2] = pltpu.make_async_copy(r.stage.at[s % 2], r.neighbours_grad.at[s], r.out_sem.at[s % 2])
+        out[s % 2].start()
+    red.free(1)
+    g.settle(1)
+    swap.wait("gp")
+    swap.wait("nb")
+    size = slots * rows_n
+    weight_grad(
+        1,
+        lambda cols: r.neighbours[:, :, cols].reshape(size, -1),
+        lambda cols: r.by_neighbours[:, :, cols].reshape(size, -1),
+        lambda start, n: r.pool_grad[:, :, pl.ds(pl.multiple_of(c * pool_half + start, LANES), n)].reshape(size, -1),
+        lambda start, n: r.by_pool_grad[:, :, start : start + n].reshape(size, -1),
+        pool_half,
+    )
+    red.push(7)
+    remote(r.gkv.at[p.s_y], r.kv_y, kv_sem.at[6], kv_sem.at[7], p.to_y).wait_recv()
+    swap.wait("near")
+    for start in range(0, 2 * width, LANES):
+        cols = slice(start, start + LANES)
+        total = r.gkv[p.s, :, cols].astype(f32) + r.kv_near[:, cols].astype(f32) + r.kv_y[:, cols].astype(f32)
+        if start < width:
+            total = rotate(total, cosine, -signed)
+        r.joined_grad[:, width + start : width + start + LANES] = total.astype(bf16)
+    joined_half = 3 * width // 2
+    swap.send("gj", half(r.joined_grad, o, joined_half), r.by_joined_grad)
+    grad_one = input_grad(r.joined_grad, 0, joined_half)
+    red.free(0)
+    g.settle(0)
+    back, dg, db = norm_back_at(grad_one, r.tokens[...].astype(f32), gain(0))
+    keep_vec(0, dg, db)
+    r.tokens_grad[...] = r.first[...] + back
+    swap.send("vec", r.vec_sum.at[o], r.by_vec)
+    swap.wait("gj")
+    swap.wait("n1")
+    plain_grad(0, r.n1, r.by_n1, r.joined_grad, r.by_joined_grad, joined_half)
+    swap.wait("vec")
+    vec = r.vec_sum[c] + r.by_vec[...]
+    vec = jnp.concatenate([vec, jnp.zeros((LANES - 8, width), f32)], 0)
+    w[0][c, :, :, :, joined_half:] = jnp.transpose(vec).astype(bf16).reshape(p.nz, 4, -1, LANES)
+    for q in range(8, len(red.chunks)):
+        red.push(q)
+    red.drain()
+    for cp in (*red.sent, *swap.sent, far):
+        cp.wait_send()
+    for cp in out:
+        cp.wait()
+
+
+def rope_table(length):
+    half = HEAD // 2
+    freq = (10000.0 ** (-np.arange(half, dtype=np.float32) / half)).astype(np.float32)
+    angles = np.arange(length, dtype=np.float32)[:, None] * freq[None, :]
+    cosine, sine = np.cos(angles), np.sin(angles)
+    table = np.concatenate([cosine] * 4 + [-sine, sine] * 2, 1)
+    return table.astype(np.float32).reshape(4, -1, 2 * LANES)
+
+
+def column_halves(v):
+    return v[:, : v.shape[1] // 2], v[:, v.shape[1] // 2 :]
+
+
+def shard_halves(w_qkv, w_cross_kv, w_out, w_cross_q, w_cross_out, w_up, gains, shifts, nz):
+    rows = w_qkv.shape[0]
+    up = jnp.swapaxes(w_up.reshape(rows, nz * 4, 2, -1), 1, 2).reshape(rows, -1)
+    pads = [jnp.pad(jnp.stack(v, 1), ((0, 0), (0, LANES - 3))) for v in (gains, shifts)]
+    parts = [column_halves(v) for v in (w_qkv, w_cross_kv, w_out, w_cross_q, w_cross_out, up)]
+    return jnp.stack(
+        [jnp.concatenate([parts[0][h], pads[h], *(v[h] for v in parts[1:])], 1) for h in range(2)]
+    ).astype(f32)
+
+
 class Refs:
-    pass
-
-
-NAMES_IN = ("shards", "w_down", "tokens", "prefix", "neighbours", "index", "rope")
-
-
-def buffers(nz, quarter, length, width, hidden, slots, rows_n, row_block):
-    heads2 = width // LANES
-    halves = (3 * width // 2 + LANES, width, width // 2, width // 2, width // 2, hidden // 2)
-    weights = [((2, nz, 4, row_block, h), bf16) for h in halves]
-    weights.append(((2, nz, 4, hidden // (8 * nz), width), bf16))
-    acts = dict(
-        n1=((quarter, width), bf16),
-        q=((quarter, width), bf16),
-        kv=((4, quarter, 2 * width), bf16),
-        att=((quarter, width), bf16),
-        lse=((heads2, 1, 2 * quarter), f32),
-        first=((quarter, width), f32),
-        n2=((quarter, width), bf16),
-        cq=((quarter, width), bf16),
-        pool=((slots, rows_n, 2 * width), bf16),
-        lse_cross=((heads2, 8, LANES), f32),
-        cm=((quarter, width), bf16),
-        second=((quarter, width), f32),
-        n3=((quarter, width), bf16),
-        act=((quarter, hidden), bf16),
-        slope=((quarter, hidden), bf16),
-        out=((quarter, width), bf16),
-        vec=((2, 8, width), f32),
-    )
-    return weights, acts
-
-
-CHUNKS = (
+    def take(self, names, refs):
+        for name, ref in zip(names, refs, strict=True):
+            setattr(self, name, ref)
+
+
+NAMES_IN = ("shards", "w_down", "tokens", "cotangent", "prefix", "neighbours", "index", "rope_table")
+NAMES_OUT = ("out", "tokens_grad", "neighbours_grad")
+GATHER = (
     (0, 0, 1280, 2),
     (1, 0, 768, 2),
     (2, 0, 384, 2),
@@ -381,55 +751,107 @@
     (6, 0, 384, 2),
     (6, 384, 384, 2),
 )
-
-
-def forward_kernel(nz, names, *args):
-    n_in = len(NAMES_IN)
+REDUCE = (
+    (6, 0, 384, 2),
+    (6, 384, 384, 2),
+    (5, 0, 768, 2),
+    (5, 768, 768, 2),
+    (4, 0, 384, 2),
+    (3, 0, 384, 2),
+    (2, 0, 384, 2),
+    (1, 0, 768, 2),
+    (0, 0, 640, 2),
+    (0, 640, 640, 2),
+)
+
+
+def memory(nz, quarter, width, hidden, slots, rows_n, rows):
+    halves = (3 * width // 2 + LANES, width, width // 2, width // 2, width // 2, hidden // 2)
+    weights = [((2, nz, 4, 2 * rows, h), bf16) for h in halves]
+    weights.append(((2, nz, 4, hidden // (8 * nz), width), bf16))
+    sums = [((2, rows, h), f32) for h in halves]
+    sums.append(((hidden // (8 * nz), width), f32))
+    tok, half_tok = ((quarter, width), bf16), ((quarter, width // 2), bf16)
+    half_hidden = ((quarter, hidden // 2), bf16)
+    pool_half = ((slots, rows_n, width), bf16)
+    kv = ((quarter, 2 * width), bf16)
+    arrays = dict(
+        beside=((rows, sum(halves)), f32),
+        rope=((quarter, 2 * LANES), f32),
+        n1=tok,
+        q=tok,
+        kv=((4, *kv[0]), bf16),
+        att=tok,
+        lse=((width // LANES, 1, 2 * quarter), f32),
+        first=((quarter, width), f32),
+        n2=tok,
+        cq=tok,
+        pool=((slots, rows_n, 2 * width), bf16),
+        lse_cross=((width // LANES, 8, LANES), f32),
+        cm=tok,
+        second=((quarter, width), f32),
+        n3=tok,
+        act=((quarter, hidden), bf16),
+        slope=((quarter, hidden), bf16),
+        vec=((2, 8, width), f32),
+        branch=tok,
+        mixed_grad=tok,
+        cq_grad=tok,
+        self_branch=tok,
+        att_grad=tok,
+        joined_grad=((quarter, 3 * width), bf16),
+        pool_grad=((slots, rows_n, 2 * width), bf16),
+        gkv=((4, *kv[0]), bf16),
+        kv_far=kv,
+        kv_near=kv,
+        kv_y=kv,
+        stage=((2, rows_n, width), f32),
+        vec_sum=((2, 8, width), f32),
+        by_act=half_hidden,
+        by_cot=tok,
+        by_n3=tok,
+        by_hidden_grad=half_hidden,
+        by_cm=tok,
+        by_branch=half_tok,
+        by_neighbours=pool_half,
+        by_pool_grad=pool_half,
+        by_n2=tok,
+        by_cq_grad=half_tok,
+        by_att=tok,
+        by_self_branch=half_tok,
+        by_n1=tok,
+        by_joined_grad=((quarter, 3 * width // 2), bf16),
+        by_vec=((8, width), f32),
+    )
+    return weights, arrays, sums
+
+
+def layer_kernel(nz, names, *refs):
+    refs = list(refs)
     r = Refs()
-    for name, ref in zip(NAMES_IN, args[:n_in]):
-        setattr(r, name, ref)
-    r.w = args[n_in : n_in + 7]
-    outs = args[n_in + 7 : n_in + 7 + len(names)]
-    for name, ref in zip(names, outs):
-        setattr(r, name, ref)
-    r.beside, r.pair_sem, send, recv, kv_sem = args[n_in + 7 + len(names) :]
+
+    def some(n):
+        taken = refs[:n]
+        del refs[:n]
+        return taken
+
+    r.take(NAMES_IN, some(len(NAMES_IN)))
+    r.take(NAMES_OUT, some(len(NAMES_OUT)))
+    r.sums, r.w = some(7), some(7)
+    r.take(names, some(len(names)))
+    r.pair_sem, r.rope_sem, r.out_sem, kv_sem, swap_sem, g_send, g_recv, r_send, r_recv, r.credit = refs
     p = Place(nz)
     barrier = pltpu.get_barrier_semaphore()
     friends = [*p.to_z, p.to_x, p.to_y, p.to_c]
     for device in friends:
         pl.semaphore_signal(barrier, inc=1, device_id=device, device_id_type=MESH)
     pl.semaphore_wait(barrier, len(friends))
-    g = Gather(p, r.w, CHUNKS, send, recv)
-    forward(p, r, g, kv_sem)
-    for q in range(len(CHUNKS)):
-        g.settle(q)
-
-
-def rope_table(length):
-    half = HEAD // 2
-    freq = (10000.0 ** (-np.arange(half, dtype=np.float32) / half)).astype(np.float32)
-    angles = np.arange(length, dtype=np.float32)[:, None] * freq[None, :]
-    cosine, sine = np.cos(angles), np.sin(angles)
-    table = np.concatenate([cosine] * 4 + [-sine, sine] * 2, 1)
-    return table.astype(np.float32).reshape(4, -1, 2 * LANES)
-
-
-def column_halves(v):
-    return v[:, : v.shape[1] // 2], v[:, v.shape[1] // 2 :]
-
-
-def shard_halves(w_qkv, w_cross_kv, w_out, w_cross_q, w_cross_out, w_up, gains, shifts, nz):
-    rows = w_qkv.shape[0]
-    up = jnp.swapaxes(w_up.reshape(rows, nz * 4, 2, -1), 1, 2).reshape(rows, -1)
-    pads = [jnp.pad(jnp.stack(v, 1), ((0, 0), (0, LANES - 3))) for v in (gains, shifts)]
-    parts = [column_halves(v) for v in (w_qkv, w_cross_kv, w_out, w_cross_q, w_cross_out, up)]
-    return jnp.stack(
-        [jnp.concatenate([parts[0][h], pads[h], *(v[h] for v in parts[1:])], 1) for h in range(2)]
-    ).astype(f32)
-
-
-def joined_halves(w):
-    return jnp.concatenate([w[h].reshape(-1, w.shape[-1]) for h in range(2)], 1)
+    g = Gather(p, r.w, GATHER, g_send, g_recv)
+    swap = Swap(p, swap_sem)
+    pairs = r.tokens.shape[1] // LANES
+    forward(p, r, g, swap, kv_sem, pairs)
+    red = Reduce(p, r, REDUCE, r_send, r_recv)
+    backward(p, r, g, swap, red, kv_sem, pairs)
 
 
 def local_fast(
@@ -454,162 +876,57 @@
 ):
     nz = lax.axis_size("dp") // 2
     quarter, width = tokens.shape[1:]
-    hidden = w_up.shape[1]
+    rows, hidden = w_up.shape
     slots, rows_n = neighbours.shape[1:3]
-    length = quarter * 4
     shards = shard_halves(
         w_qkv, w_cross_kv, w_out, w_cross_q, w_cross_out, w_up,
         (gain_one, gain_two, gain_three), (shift_one, shift_two, shift_three), nz,
     )
-    weights, acts = buffers(nz, quarter, length, width, hidden, slots, rows_n, 2 * w_qkv.shape[0])
-    names = tuple(acts)
-    vmem, smem = pl.BlockSpec(memory_space=pltpu.VMEM), pl.BlockSpec(memory_space=pltpu.SMEM)
-    outs = pl.pallas_call(
-        functools.partial(forward_kernel, nz, names),
-        out_shape=[jax.ShapeDtypeStruct(*v) for v in [*weights, *acts.values()]],
-        in_specs=[vmem, vmem, vmem, smem, vmem, smem, vmem],
-        out_specs=[vmem] * (len(weights) + len(acts)),
-        scratch_shapes=[
-            pltpu.VMEM(shards.shape[1:], f32),
-            pltpu.SemaphoreType.DMA((2,)),
-            pltpu.SemaphoreType.DMA((len(CHUNKS), 12)),
-            pltpu.SemaphoreType.DMA((len(CHUNKS), 12)),
-            pltpu.SemaphoreType.DMA((6,)),
+    weights, arrays, sums = memory(nz, quarter, width, hidden, slots, rows_n, rows)
+    vmem, smem, anywhere = (pl.BlockSpec(memory_space=m) for m in (pltpu.VMEM, pltpu.SMEM, pl.ANY))
+    made = [((quarter, width), bf16), ((quarter, width), f32), ((slots, rows_n, width), f32), *sums]
+    dma = pltpu.SemaphoreType.DMA
+    out, tokens_grad, neighbours_grad, *summed = pl.pallas_call(
+        functools.partial(layer_kernel, nz, tuple(arrays)),
+        out_shape=[jax.ShapeDtypeStruct(*v) for v in made],
+        in_specs=[vmem, vmem, vmem, vmem, smem, vmem, smem, anywhere],
+        out_specs=[vmem, vmem, anywhere] + [vmem] * len(sums),
+        scratch_shapes=[pltpu.VMEM(*v) for v in (*weights, *arrays.values())]
+        + [
+            dma((2,)),
+            dma,
+            dma((2,)),
+            dma((8,)),
+            dma((2, 20)),
+            dma((len(GATHER), 12)),
+            dma((len(GATHER), 12)),
+            dma((len(REDUCE), 8)),
+            dma((len(REDUCE), 8)),
+            pltpu.SemaphoreType.REGULAR((7,)),
         ],
         compiler_params=pltpu.CompilerParams(
-            collective_id=0, has_side_effects=True, vmem_limit_bytes=60 * 2**20
+            collective_id=0, has_side_effects=True, vmem_limit_bytes=64 * 2**20 - 2**17
         ),
     )(
-        shards, w_down, tokens[0], prefix_len, neighbours[0],
-        neighbour_index.reshape(-1), jnp.asarray(rope_table(length)),
-    )
-    w, a = outs[:7], dict(zip(names, outs[7:]))
-    full_qkv = jnp.concatenate([w[0][h].reshape(width, -1)[:, : 3 * width // 2] for h in range(2)], 1)
-    full_cross_kv, full_out, full_cross_q, full_cross_out, full_up = (joined_halves(w[k]) for k in range(1, 6))
-    full_down = w[6].reshape(hidden, width)
-    gain_f1, gain_f2, gain_f3 = (a["vec"][0, i] for i in range(3))
-    seq_here, heads = 1, width // HEAD
-    seq_index = lax.axis_index("seq")
-    query_pos = seq_index * quarter + jnp.arange(quarter)
-    key_pos = jnp.arange(length)
-    visible = (key_pos[None, None, :] <= query_pos[None, :, None]) | (
-        key_pos[None, None, :] < prefix_len[:, None, None]
-    )
-    cosine, sine_part = rotary_tables(query_pos)
-    unit_one, inv_one = plain_norm_parts(tokens.astype(f32))
-    unit_two, inv_two = plain_norm_parts(a["first"][None])
-    unit_three, inv_three = plain_norm_parts(a["second"][None])
-    grad_act = input_grad(cotangent, full_down)
-    grad_hidden = (grad_act * a["slope"]).astype(bf16)
-    grad_normed_three = input_grad(grad_hidden, full_up)
-    back_three, grad_gain_three, grad_shift_three = norm_back(grad_normed_three, unit_three, inv_three, gain_f3)
-    grad_second = cotangent.astype(f32) + back_three
-    grad_cross_branch = grad_second.astype(bf16)
-    spans = slots // 2
-    span_len = quarter // spans
-    grad_mixed = input_grad(grad_cross_branch, full_cross_out).astype(bf16).reshape(1, spans, span_len, heads, HEAD)
-    local_index = neighbour_index.reshape(1, slots) - seq_index * slots
-    picked = pick_slots(a["pool"][None], local_index)
-    picked = picked.reshape(1, spans, 2 * rows_n, 2 * width)
-    cross_keys = picked[..., :width].reshape(1, spans, 2 * rows_n, heads, HEAD)
-    cross_values = picked[..., width:].reshape(1, spans, 2 * rows_n, heads, HEAD)
-    cross_queries = a["cq"].reshape(1, spans, span_len, heads, HEAD)
-    cross_probs = jax.nn.softmax(
-        jnp.einsum("scqhd,sckhd->schqk", cross_queries, cross_keys, preferred_element_type=f32) * HEAD ** (-0.5), -1
-    )
-    grad_cross_probs = jnp.einsum("scqhd,sckhd->schqk", grad_mixed, cross_values, preferred_element_type=f32)
-    grad_cross_scores = (
-        cross_probs * (grad_cross_probs - jnp.sum(cross_probs * grad_cross_probs, -1, keepdims=True))
-    ).astype(bf16)
-    grad_cross_query = (
-        (jnp.einsum("schqk,sckhd->scqhd", grad_cross_scores, cross_keys, preferred_element_type=f32) * HEAD ** (-0.5))
-        .astype(bf16)
-        .reshape(1, quarter, width)
-    )
-    grad_cross_keys = jnp.einsum(
-        "schqk,scqhd->sckhd", grad_cross_scores, cross_queries, preferred_element_type=f32
-    ) * HEAD ** (-0.5)
-    grad_cross_values = jnp.einsum(
-        "schqk,scqhd->sckhd", cross_probs.astype(bf16), grad_mixed, preferred_element_type=f32
-    )
-    grad_picked = jnp.concatenate(
-        [v.reshape(1, spans, 2 * rows_n, width) for v in (grad_cross_keys, grad_cross_values)], -1
-    ).astype(bf16).reshape(slots, rows_n, 2 * width)
-    grad_pool_kv = pick_slots(grad_picked[None], slot_places(local_index))
-    grad_neighbours = input_grad(grad_pool_kv, full_cross_kv)
-    grad_normed_two = input_grad(grad_cross_query, full_cross_q)
-    back_two, grad_gain_two, grad_shift_two = norm_back(grad_normed_two, unit_two, inv_two, gain_f2)
-    grad_first = grad_second + back_two
-    grad_self_branch = grad_first.astype(bf16)
-    grad_attended = input_grad(grad_self_branch, full_out).astype(bf16).reshape(1, quarter, heads, HEAD)
-    key_heads = a["kv"].reshape(1, length, 2 * heads, HEAD)[:, :, :heads]
-    value_heads = a["kv"].reshape(1, length, 2 * heads, HEAD)[:, :, heads:]
-    logsum = jnp.swapaxes(a["lse"].reshape(heads // 2, 2, quarter).reshape(heads // 4, 1, 4, quarter), 0, 0)
-    grad_query, grad_key_all, grad_value_all = lax.map(
-        functools.partial(attend_back, visible),
-        (
-            grouped(a["q"].reshape(1, quarter, heads, HEAD)),
-            grouped(key_heads),
-            grouped(value_heads),
-            grouped(grad_attended),
-            logsum,
-        ),
-    )
-    grad_query = ungrouped(grad_query)
-    grad_key_all = ungrouped(grad_key_all).reshape(1, length, width)
-    grad_value_all = ungrouped(grad_value_all).reshape(1, length, width)
-    both = lax.psum_scatter(
-        jnp.concatenate([grad_key_all, grad_value_all], -1).astype(bf16), "seq", scatter_dimension=1, tiled=True
-    ).astype(f32)
-    grad_joined = jnp.concatenate(
-        [
-            unrotate(grad_query, cosine, sine_part).reshape(1, quarter, width),
-            unrotate(both[..., :width].reshape(1, quarter, heads, HEAD), cosine, sine_part).reshape(1, quarter, width),
-            both[..., width:],
-        ],
-        -1,
-    ).astype(bf16)
-    grad_normed_one = input_grad(grad_joined, full_qkv)
-    back_one, grad_gain_one, grad_shift_one = norm_back(grad_normed_one, unit_one, inv_one, gain_f1)
-    grad_tokens = grad_first + back_one
-    norm_grads = jnp.stack(
-        [grad_gain_one, grad_shift_one, grad_gain_two, grad_shift_two, grad_gain_three, grad_shift_three], 1
-    )
-    width_owned = lax.psum_scatter(
-        jnp.concatenate(
-            [
-                weight_grad(a["n1"], grad_joined).astype(bf16),
-                weight_grad(a["att"], grad_self_branch).astype(bf16),
-                weight_grad(a["n2"], grad_cross_query).astype(bf16),
-                weight_grad(neighbours, grad_pool_kv).astype(bf16),
-                weight_grad(a["cm"], grad_cross_branch).astype(bf16),
-                weight_grad(a["n3"], grad_hidden).astype(bf16),
-                norm_grads.astype(bf16),
-            ],
-            1,
-        ),
-        ("dp", "seq"),
-        scatter_dimension=0,
-        tiled=True,
-    ).astype(f32)
-    grad_down = weight_grad(a["act"], cotangent).astype(bf16)
-    grad_down = jnp.swapaxes(grad_down.reshape(2, nz * 4, -1, width), 0, 1).reshape(hidden, width)
-    down_owned = lax.psum_scatter(grad_down, ("dp", "seq"), scatter_dimension=0, tiled=True).astype(f32)
-    column = 8 * width + hidden
-    rows = width_owned.shape[0]
-    grad_up = width_owned[:, 8 * width : column].reshape(rows, 2, nz * 4, -1)
+        shards, w_down, tokens[0], cotangent[0], prefix_len, neighbours[0],
+        neighbour_index.reshape(-1), jnp.asarray(rope_table(4 * quarter)),
+    )
+    whole = [jnp.concatenate([v[0], v[1]], 1) for v in summed[1:5]]
+    half = 3 * width // 2
+    up = jnp.concatenate([v.reshape(rows, 4 * nz, 1, -1) for v in summed[5]], 2)
+    vectors = [summed[0][h, :, half + i] for i in range(3) for h in range(2)]
     return (
-        a["out"][None],
-        grad_tokens,
-        grad_neighbours,
-        width_owned[:, : 3 * width],
-        width_owned[:, 3 * width : 4 * width],
-        width_owned[:, 4 * width : 5 * width],
-        width_owned[:, 5 * width : 7 * width],
-        width_owned[:, 7 * width : 8 * width],
-        jnp.swapaxes(grad_up, 1, 2).reshape(rows, hidden),
-        down_owned,
-        *(width_owned[:, column + i] for i in range(6)),
+        out[None],
+        tokens_grad[None],
+        neighbours_grad[None],
+        jnp.concatenate([summed[0][0, :, :half], summed[0][1, :, :half]], 1),
+        whole[1],
+        whole[2],
+        whole[0],
+        whole[3],
+        up.reshape(rows, hidden),
+        summed[6],
+        *vectors,
     )
 
 

time: 640 us -> 290 us (0.45); the launches traced: 628 us -> 289 us
  waiting for transfers between devices: 204 us -> 0 us
  local copies, waits for them, and re-layouts: 152 us -> 23.6 us
  Pallas kernels: 134 us -> 258 us
  matrix products: 64.9 us -> 0 us
  between operations: 46.7 us -> 1.39 us
  other arithmetic: 26.3 us -> 5.7 us
    unnamed x4 -> x0, waiting for transfers between devices: 167 us -> none
    pallas_call x1, Pallas kernels: 134 us -> 258 us  [local_fast(): pl.pallas_call(functools.partial(layer_kernel, nz, tuple(arrays)), out_sh...]
    dot_general x33 -> x0, matrix products: 62.2 us -> none  [the longest x7 18.6 us: weight_grad(): lax.dot_general(flat_left, flat_grad, (((0,), (0,)), ((), ())), preferred...]
    reduce_scatter x2 -> x0, waiting for transfers between devices: 36.1 us -> none  [the longest x1 36.1 us: local_fast(): lax.psum_scatter(grad_down, ('dp', 'seq'), scatter_dimension=0, tiled=True)]
    slice x21 -> x1, local copies, waits for them, and re-layouts: 33.8 us -> 1.65 us  [local_fast(): vectors = [summed[0][h, :, half + i] for i in range(3) for h in range(2)]]
    concatenate x6 -> x1, local copies, waits for them, and re-layouts: 31.5 us -> 0.31 us  [local_fast(): up = jnp.concatenate([v.reshape(rows, 4 * nz, 1, -1) for v in summed[5]], 2)]
    unnamed x141 -> x15, local copies, waits for them, and re-layouts: 31.4 us -> 10.9 us
    convert_element_type x6 -> x0, local copies, waits for them, and re-layouts: 12.7 us -> none  [the longest x1 2.95 us: local_fast(): weight_grad(neighbours, grad_pool_kv).astype(bf16)]
  transfers between devices with their start and end apart: 3 -> 0, of which waited for: 2 -> 0; matrix products, arithmetic and copies ran while one was open for 15% -> 0% of each run, Pallas kernels for 0% -> 0%
where the time goes in v2:
time: 290 us; the launch traced here: 289 us
  Pallas kernels  258 us (89%)
  local copies, waits for them, and re-layouts  23.6 us (8%)
  other arithmetic  5.7 us (2%)
    pallas_call x1, Pallas kernels, local_fast(): pl.pallas_call(functools.partial(layer_kernel, nz, tuple(arrays)), out_sh...  258 us
    unnamed x15, local copies, waits for them, and re-layouts  10.9 us

profile of v2, /device:TPU:1, one launch (start us, length us, event | category | flops | bytes accessed | tf_op | source)
XLA Modules:
  0.0 288.9 jit_solution(11642970038865150676)
XLA Ops:
  1.3 0.7 pad_maximum_fusion.6
  2.0 0.7 pad_maximum_fusion.7
  2.7 0.8 copy.56
  3.5 0.6 reshape.46.refs_6_
  4.0 0.1 copy.55
  4.1 0.1 copy.53
  4.2 1.1 reshape.44
  5.4 0.2 reshape.45
  5.7 0.9 slice_dynamic-update-slice_fusion.3
  6.5 0.8 slice_dynamic-update-slice_fusion.5
  7.3 0.7 constant_dynamic-update-slice_fusion.2
  8.1 0.8 constant_dynamic-update-slice_fusion.1
  8.8 0.7 constant_dynamic-update-slice_fusion
  9.6 1.0 maximum_convert_fusion.refs_0_
  10.6 258.2 %shard_map.306 = (bf16[256,768]{1,0:T(8,128)(2,1)}, f32[256,768]{1,0:T(8,128)}, f32[8,128,768]{2,1,0:T(8,128)}, f32[2,24,1280]{2,1,0:T(8,128)}, f32[2,24,768]{2,...) custom-call(f32[2,24,4736]{2,1,0:T(8,128)} %maximum_convert_fusion.r, ...), custom_call_target="tpu_custom_call" | custom-call | tf_op jit(solution)/shard_map/pallas_call | solution.py:889
  268.8 1.6 slice_reduce_fusion
  270.5 1.0 slice_bitcast_fusion.1
  271.4 0.7 pad_maximum_fusion.1
  272.1 0.8 slice_bitcast_fusion.9
  272.9 0.6 pad_maximum_fusion.3
  273.6 0.8 slice_bitcast_fusion.7
  274.3 0.6 pad_maximum_fusion.4
  275.0 0.8 slice_bitcast_fusion.5
  275.8 0.6 pad_maximum_fusion.5
  276.4 0.9 slice_bitcast_fusion.3
  277.3 0.0 copy-start
  277.4 0.7 pad_maximum_fusion.2
  278.0 2.0 fusion
  280.0 0.1 reshape_unstack.6
  280.1 1.0 reshape_unstack.7
  281.2 0.3 copy.57
  281.5 1.2 reshape.47
  282.7 1.8 copy.77
  284.5 2.1 copy.78
  286.5 0.0 copy-done
  286.6 0.0 copy-start.1
  286.6 1.7 copy.79
  288.2 0.0 copy-done.1
  288.2 0.7 copy.80
  (4 shorter events, 0.1 us)
Async XLA Ops:
  277.3 9.2 %copy-start = (f32[8,128,768]{2,1,0:T(8,128)S(1)}, f32[8,128,768]{2,1,0:T(8,128)}, u32[]{:S(2)}) copy-start(f32[8,128,768]{2,1,0:T(8,128)} %get-tuple-element.28) | copy-start | bytes 9437188
  286.6 1.7 copy-start.1

commit v3 on v2

--- a/solution.py
+++ b/solution.py
@@ -19,6 +19,8 @@
 NT = (((1,), (1,)), ((), ()))
 TN = (((0,), (0,)), ((), ()))
 LANES = 128
+AHEAD = 2
+TICKS_KV = 0
 
 
 def dot(a, b, dims=NN):
@@ -55,6 +57,13 @@
         self.s_c = y * 2 + 1 - c
         self.s_d = (1 - y) * 2 + 1 - c
 
+    def meet(self):
+        barrier = pltpu.get_barrier_semaphore()
+        friends = [*self.to_z, self.to_x, self.to_y, self.to_c]
+        for device in friends:
+            pl.semaphore_signal(barrier, inc=1, device_id=device, device_id_type=MESH)
+        pl.semaphore_wait(barrier, len(friends))
+
 
 def remote(src, dst, send, recv, device):
     return pltpu.make_async_remote_copy(
@@ -66,6 +75,37 @@
     def __init__(self, place, weights, chunks, send, recv):
         self.p, self.w, self.chunks, self.ss, self.rs = place, weights, chunks, send, recv
         self.sent = [[] for _ in chunks]
+        self.t, self.have = 0, set()
+
+    def chunks_of(self, k):
+        return [q for q, v in enumerate(self.chunks) if v[0] == k]
+
+    def begin(self):
+        self.along_z(0)
+
+    def tick(self):
+        t, n = self.t, len(self.chunks)
+        if t >= n + 2:
+            return
+        if t == 0:
+            for q in range(1, AHEAD):
+                self.along_z(q)
+        if t < n:
+            self.along_xy(t)
+        if t + AHEAD < n:
+            self.along_z(t + AHEAD)
+        if 0 <= t - 1 < n:
+            self.across(t - 1)
+        if 0 <= t - 2 < n:
+            self.last(t - 2)
+        self.t += 1
+
+    def need(self, q):
+        while self.t <= q + 2:
+            self.tick()
+        if q not in self.have:
+            self.have.add(q)
+            self.ready(q)
 
     def part(self, q, half, z, xy):
         k, start, width, _ = self.chunks[q]
@@ -160,70 +200,101 @@
     c, z = p.c, p.z
     w = r.w
 
-    def step(t):
-        if t < n:
-            g.along_xy(t)
-        if t + 3 < n:
-            g.along_z(t + 3)
-        if 0 <= t - 1 < n:
-            g.across(t - 1)
-        if 0 <= t - 2 < n:
-            g.last(t - 2)
-
-    first = remote(r.shards.at[p.o], r.beside, r.pair_sem.at[0], r.pair_sem.at[1], p.to_c)
+    vectors = r.vectors[...].astype(f32)
+    start = 0
+    for k, ref in enumerate((r.w_qkv, r.w_cross_kv, r.w_out, r.w_cross_q, r.w_cross_out, r.w_up)):
+        rows = ref[...].astype(f32)
+        size = rows.shape[1] // 2
+        for h in range(2):
+            parts = 3 if k == 0 else 1
+            part = size // parts
+            for i in range(parts):
+                source = i * 2 * part + h * part
+                r.pack[h, :, start + i * part : start + (i + 1) * part] = rows[:, source : source + part]
+            if k == 0:
+                r.pack[h, :, start + size : start + size + LANES] = jnp.zeros((rows.shape[0], LANES), f32)
+                r.pack[h, :, start + size : start + size + vectors.shape[1]] = vectors
+        start += w[k].shape[-1]
+    p.meet()
+    first = remote(r.pack.at[p.o], r.beside, r.pair_sem.at[0], r.pair_sem.at[1], p.to_c)
     first.start()
-    rope = pltpu.make_async_copy(r.rope_table.at[p.s], r.rope, r.rope_sem)
-    rope.start()
-    w[6][c, z, p.own] = r.w_down[...]
+    down_rows, down_half = r.w_down.shape[0], w[6].shape[-1]
+    down_at = pl.ds(pl.multiple_of(c * down_rows, 16), down_rows)
+    down = remote(
+        r.w_down.at[:, pl.ds(pl.multiple_of(p.o * down_half, LANES), down_half)],
+        w[6].at[p.o, z, p.own, down_at],
+        r.pair_sem.at[2],
+        r.pair_sem.at[3],
+        p.to_c,
+    )
+    down.start()
+    tokens_y = remote(r.tokens, r.branch, r.pair_sem.at[4], r.pair_sem.at[5], p.to_y)
+    tokens_y.start()
+    ropes = [pltpu.make_async_copy(r.rope_table.at[s], r.rope.at[i], r.rope_sem.at[i]) for i, s in enumerate((p.s, p.s_y))]
+    for rope in ropes:
+        rope.start()
+    w[6][c, z, p.own, down_at] = r.w_down[:, pl.ds(pl.multiple_of(c * down_half, LANES), down_half)]
     first.wait_recv()
     start = 0
     for k in range(6):
         width = w[k].shape[-1]
-        mine, other = r.shards[c, :, start : start + width], r.beside[:, start : start + width]
+        mine, other = r.pack[c, :, start : start + width], r.beside[:, start : start + width]
         top, low = jnp.where(c == 0, mine, other), jnp.where(c == 0, other, mine)
         w[k][c, z, p.own] = jnp.concatenate([top, low], 0).astype(bf16)
         start += width
-        for q in range(3):
-            if g.chunks[q][0] == k:
-                g.along_z(q)
-    step(0)
-    swap.send("cot", r.cotangent, r.by_cot)
+        if k == 0:
+            g.begin()
+    down.wait_recv()
+    g.tick()
+    swap.send("cot", r.cotangent.at[:, pl.ds(pl.multiple_of(p.o * down_half, LANES), down_half)], r.by_cot)
     swap.send("nb", r.neighbours, r.by_neighbours)
-    rope.wait()
+    for rope in ropes:
+        rope.wait()
     tokens = r.tokens[...].astype(f32)
+    quarter, width = tokens.shape
     unit, _ = norm_parts(tokens)
-    step(1)
-    step(2)
-    g.ready(0)
-    qkv_half = 3 * 384
+    g.tick()
+    tokens_y.wait_recv()
+    unit_y, _ = norm_parts(r.branch[...].astype(f32))
+    g.need(0)
+    part = width // 2
+    r.vec[...] = jnp.transpose(half_of(w[0], 0, 3 * part, LANES).astype(f32))[:8]
+
+    def affine(v, i):
+        return (v * r.vec[i : i + 1] + r.vec[3 + i : 4 + i]).astype(bf16)
+
+    r.n1[:quarter] = affine(unit, 0)
+    r.n1[quarter:] = affine(unit_y, 0)
+    swap.send("n1", r.n1, r.by_n1)
     for h in range(2):
-        r.vec[h] = jnp.transpose(half_of(w[0], h, qkv_half, LANES).astype(f32))[:8]
-
-    def affine(v, i):
-        return (v * r.vec[0, i : i + 1] + r.vec[1, i : i + 1]).astype(bf16)
-
-    r.n1[...] = affine(unit, 0)
-    swap.send("n1", r.n1, r.by_n1)
-    cosine, signed = r.rope[:, :LANES], r.rope[:, LANES:]
-    for i in (2, 3, 4, 5, 0, 1):
-        joined = dot(r.n1[...], half_of(w[0], i // 3, (i % 3) * 384, 384))
-        if i < 4:
-            joined = jnp.concatenate(
-                [rotate(joined[:, b : b + LANES], cosine, signed) for b in range(0, 384, LANES)], 1
-            )
-        part = joined.astype(bf16)
-        if i < 2:
-            r.q[:, i * 384 : (i + 1) * 384] = part
-        else:
-            r.kv[p.s, :, (i - 2) * 384 : (i - 1) * 384] = part
-            if i == 5:
-                kv_c = remote(r.kv.at[p.s], r.kv.at[p.s], kv_sem.at[0], kv_sem.at[1], p.to_c)
-                kv_y = remote(r.kv.at[p.s], r.kv.at[p.s], kv_sem.at[2], kv_sem.at[3], p.to_y)
-                kv_y.start()
-                kv_c.start()
-    step(3)
-
-    g.ready(1)
+        value = dot(r.n1[...], half_of(w[0], h, 2 * part, part)).astype(bf16)
+        cols = slice(width + h * part, width + (h + 1) * part)
+        r.kv[p.s, :, cols] = value[:quarter]
+        r.kv[p.s_y, :, cols] = value[quarter:]
+
+    def turned(v, i, sign=1):
+        cosine, signed = r.rope[i, :, :LANES], r.rope[i, :, LANES:]
+        return jnp.concatenate(
+            [rotate(v[:, b : b + LANES], cosine, sign * signed) for b in range(0, v.shape[1], LANES)], 1
+        )
+
+    g.need(1)
+    for h in range(2):
+        key = dot(r.n1[...], half_of(w[0], h, part, part))
+        cols = slice(h * part, (h + 1) * part)
+        r.kv[p.s, :, cols] = turned(key[:quarter], 0).astype(bf16)
+        r.kv[p.s_y, :, cols] = turned(key[quarter:], 1).astype(bf16)
+    kv_sent = [
+        remote(r.kv.at[s], r.kv.at[s], kv_sem.at[0, i], kv_sem.at[1, i], p.to_c) for i, s in enumerate((p.s, p.s_y))
+    ]
+    for cp in kv_sent:
+        cp.start()
+    g.need(2)
+    for h in range(2):
+        query = dot(r.n1[:quarter], half_of(w[0], h, 0, part))
+        r.q[:, h * part : (h + 1) * part] = turned(query, 0).astype(bf16)
+    g.need(3)
+    g.need(4)
 
     def pool_rows(i, carry):
         rows = r.neighbours[pl.ds(i * 2, 2)].reshape(-1, r.neighbours.shape[2])
@@ -234,17 +305,13 @@
             )
         return carry
 
-    lax.fori_loop(0, r.neighbours.shape[0] // 2, pool_rows, 0)
-    landed = r.kv.at[p.s_y]
-    remote(landed, landed, kv_sem.at[2], kv_sem.at[3], p.to_y).wait_recv()
-    kv_d = remote(landed, landed, kv_sem.at[4], kv_sem.at[5], p.to_c)
-    kv_d.start()
-    step(4)
-    for ref, j in ((r.kv.at[p.s_c], 1), (r.kv.at[p.s_d], 5)):
-        remote(ref, ref, kv_sem.at[j - 1], kv_sem.at[j], p.to_c).wait_recv()
+    lax.fori_loop(0, 2, pool_rows, 0)
+    g.tick()
+    lax.fori_loop(2, r.neighbours.shape[0] // 2, pool_rows, 0)
+    for i, s in enumerate((p.s_c, p.s_d)):
+        remote(r.kv.at[s], r.kv.at[s], kv_sem.at[0, i], kv_sem.at[1, i], p.to_c).wait_recv()
 
     low_lane, low, high = lane_masks()
-    quarter = tokens.shape[0]
     place = lax.rem(lax.broadcasted_iota(jnp.int32, (1, 2 * quarter), 1), quarter) + p.s * quarter
     limit = jnp.maximum(place, r.prefix[0] - 1)
 
@@ -266,10 +333,10 @@
         r.att[:, cols] = jnp.where(low_lane, mixed[:quarter], mixed[quarter:]).astype(bf16)
         return carry
 
-    lax.fori_loop(0, pairs // 2, self_pair, 0)
-    step(5)
-    lax.fori_loop(pairs // 2, pairs, self_pair, 0)
-    g.ready(2)
+    for i in range(0, pairs, 2):
+        lax.fori_loop(i, i + 2, self_pair, 0)
+        g.tick()
+    g.need(5)
 
     def project(v, k):
         return jnp.concatenate([dot(v, half_of(w[k], h)) for h in range(2)], 1)
@@ -279,8 +346,7 @@
     r.first[...] = first_sum
     r.n2[...] = affine(norm_parts(first_sum)[0], 1)
     swap.send("n2", r.n2, r.by_n2)
-    step(6)
-    g.ready(3)
+    g.need(6)
     r.cq[...] = project(r.n2[...], 3).astype(bf16)
     slots = r.neighbours.shape[0]
     span = quarter // (slots // 2)
@@ -304,71 +370,75 @@
             r.cm[rows, cols] = jnp.where(low_lane, mixed[:span], mixed[span:]).astype(bf16)
         return carry
 
-    lax.fori_loop(0, pairs, cross_pair, 0)
-    step(7)
-    g.ready(4)
+    lax.fori_loop(0, pairs // 2, cross_pair, 0)
+    g.tick()
+    lax.fori_loop(pairs // 2, pairs, cross_pair, 0)
+    g.need(7)
     swap.send("cm", r.cm, r.by_cm)
     second_sum = r.first[...] + project(r.cm[...], 4)
     r.second[...] = second_sum
     r.n3[...] = affine(norm_parts(second_sum)[0], 2)
     swap.send("n3", r.n3, r.by_n3)
-    step(8)
     hidden_half = w[5].shape[-1]
 
-    def up_tiles(start, width, tile):
-        def body(i, carry):
-            h, col = lax.div(i, width // tile), start + lax.rem(i, width // tile) * tile
-            col = pl.multiple_of(col, tile)
-            hidden = dot(r.n3[...], half_of(w[5], h, col, tile))
+    def up_tile(start, size):
+        def body(h, carry):
+            hidden = dot(r.n3[...], half_of(w[5], h, start, size))
             cdf = 0.5 * (1.0 + lax.erf(hidden * (0.5**0.5)))
             density = jnp.exp(-0.5 * hidden * hidden) * ((2 * math.pi) ** -0.5)
-            cols = pl.ds(pl.multiple_of(h * hidden_half + col, tile), tile)
+            cols = pl.ds(pl.multiple_of(h * hidden_half + start, LANES), size)
             r.act[:, cols] = (hidden * cdf).astype(bf16)
             r.slope[:, cols] = (cdf + hidden * density).astype(bf16)
             return carry
 
-        lax.fori_loop(0, 2 * (width // tile), body, 0)
-
-    g.ready(5)
-    up_tiles(0, 768, 256)
-    step(9)
-    g.ready(6)
-    up_tiles(768, 768, 256)
-    swap.send("act", r.act.at[:, pl.ds(pl.multiple_of(p.o * hidden_half, LANES), hidden_half)], r.by_act)
-    step(10)
-    for q in (7, 8):
-        g.ready(q)
-        col = g.chunks[q][1]
-        cols = slice(col, col + 384)
-        down = sum(dot(r.act[:, h * hidden_half : (h + 1) * hidden_half], half_of(w[6], h, col, 384)) for h in range(2))
-        r.out[:, cols] = (r.second[:, cols] + down).astype(bf16)
-    first.wait_send()
-    for cp in (kv_c, kv_y, kv_d):
-        cp.wait_send()
+        lax.fori_loop(0, 2, body, 0)
+
+    for q, (k, start, size, _) in enumerate(g.chunks):
+        if k == 5:
+            g.need(q)
+            up_tile(start, size)
+    swap.send("act", r.act, r.by_act)
+
+    def down_part(q):
+        _, start, size, _ = g.chunks[q]
+        for h in range(2):
+            cols = slice(h * down_half + start, h * down_half + start + size)
+            r.out[:, cols] = (r.second[:, cols] + dot(r.act[...], half_of(w[6], h, start, size))).astype(bf16)
+
+    return down_part, turned, (first, down, tokens_y, *kv_sent)
+
+
+LAG = 3
 
 
 class Reduce:
     def __init__(self, place, r, chunks, send, recv):
         self.p, self.r, self.w, self.chunks, self.ss, self.rs = place, r, r.w, chunks, send, recv
-        self.sent, self.open, self.under_way = [], set(), {}
-        self.starts = [sum(v.shape[-1] for v in r.w[:k]) for k in range(6)]
+        self.sent, self.open, self.under_way, self.next = [], set(), {}, 0
+        self.starts = [sum(v.shape[-1] for v in r.w[:k]) for k in range(7)]
 
     def free(self, k):
         p = self.p
         for device in (p.to_x, p.to_y, *p.to_z):
             pl.semaphore_signal(self.r.credit.at[k], inc=1, device_id=device, device_id_type=MESH)
 
+    def array(self, k, half):
+        return (self.r.down_sum, 0) if k == 6 and half is self.p.c else (self.w[k], half)
+
     def at(self, q, half, z, xy):
         k, start, width, _ = self.chunks[q]
-        return self.w[k].at[half, z, xy, :, pl.ds(start, width)]
+        ref, lead = self.array(k, half)
+        return ref.at[lead, z, xy, :, pl.ds(start, width)]
 
     def load(self, q, half, z, xy):
         k, start, width, _ = self.chunks[q]
-        return self.w[k][half, z, xy, :, start : start + width].astype(f32)
+        ref, lead = self.array(k, half)
+        return ref[lead, z, xy, :, start : start + width].astype(f32)
 
     def save(self, q, half, z, xy, v):
         k, start, width, _ = self.chunks[q]
-        self.w[k][half, z, xy, :, start : start + width] = v.astype(bf16)
+        ref, lead = self.array(k, half)
+        ref[lead, z, xy, :, start : start + width] = v.astype(bf16)
 
     def copy(self, q, j, src, dst, device):
         cp = remote(src, dst, self.ss.at[q, j], self.rs.at[q, j], device)
@@ -412,34 +482,39 @@
             self.wait(q, 4 + j, self.at(q, p.o, j, 3))
             total = total + self.load(q, p.o, j, 3)
         cols = slice(start, start + width)
-        if k == 6:
-            r.sums[6][:, cols] = total
-            return
         rows = total.shape[0] // 2
         r.sums[k][p.c, :, cols] = jnp.where(p.c == 0, total[:rows], total[rows:])
-        there = slice(self.starts[k] + start, self.starts[k] + start + width)
-        r.beside[:, there] = jnp.where(p.c == 0, total[rows:], total[:rows])
-        self.copy(q, 7, r.beside.at[:, there], r.sums[k].at[p.c, :, cols], p.to_c)
+        if k == 6:
+            mine = r.down_beside.at[:, cols]
+        else:
+            mine = r.beside.at[:, self.starts[k] + start : self.starts[k] + start + width]
+        mine[...] = jnp.where(p.c == 0, total[rows:], total[:rows])
+        self.copy(q, 7, mine, r.sums[k].at[p.c, :, cols], p.to_c)
 
     def finish(self, q):
         p, (k, start, width, _) = self.p, self.chunks[q]
-        if k != 6:
-            self.wait(q, 7, self.r.sums[k].at[p.o, :, pl.ds(start, width)])
-
-    def push(self, q=None):
+        self.wait(q, 7, self.r.sums[k].at[p.o, :, pl.ds(start, width)])
+
+    def push(self, q=None, lag=LAG):
+        for other in list(self.under_way):
+            stage, age = self.under_way[other]
+            if age + 1 < lag:
+                self.under_way[other] = stage, age + 1
+                continue
+            (self.across, self.along_z, self.last)[stage](other)
+            self.under_way[other] = stage + 1, 0
+            if stage == 2:
+                del self.under_way[other]
         if q is not None:
             self.diagonal(q)
-        for other in sorted(self.under_way, reverse=True):
-            (self.across, self.along_z, self.last)[self.under_way[other]](other)
-            self.under_way[other] += 1
-            if self.under_way[other] == 3:
-                del self.under_way[other]
-        if q is not None:
-            self.under_way[q] = 0
+            self.under_way[q] = 0, 0
+
+    def chunks_of(self, k):
+        return [q for q, v in enumerate(self.chunks) if v[0] == k]
 
     def drain(self):
         while self.under_way:
-            self.push()
+            self.push(None, 1)
         for q in range(len(self.chunks)):
             self.finish(q)
 
@@ -468,7 +543,7 @@
     return back, jnp.sum(grad * unit, 0, keepdims=True), jnp.sum(grad, 0, keepdims=True)
 
 
-def backward(p, r, g, swap, red, kv_sem, pairs):
+def backward(p, r, g, swap, red, kv_sem, pairs, down_part, turned):
     w, c, o = r.w, p.c, p.o
     quarter, width = r.tokens.shape
     hidden_half, pool_half = w[5].shape[-1], w[1].shape[-1]
@@ -482,23 +557,25 @@
     def input_grad(ref, k, size):
         return sum(dot(ref[:, h * size : (h + 1) * size], half_of(w[k], h, 0, size), NT) for h in range(2))
 
-    def weight_grad(k, left, left_beside, right, right_beside, size, tile=384, base=0, tiles=2):
-        rows, per = w[k].shape[3], tile // (4 * w[k].shape[3])
-        cut = size // 2 if size > 768 and size % 256 == 0 else size
-        if size == 1152:
-            cut = 384
-
-        def body(i, carry):
-            cols = pl.ds(pl.multiple_of(base + i * tile, LANES), tile)
-            beside = pl.ds(pl.multiple_of(i * tile, LANES), tile)
-            for start in range(0, size, cut):
-                part = dot(left(cols), right(start, cut), TN) + dot(left_beside(beside), right_beside(start, cut), TN)
-                w[k][c, pl.ds(i * per, per), :, :, start : start + cut] = part.astype(bf16).reshape(per, 4, rows, cut)
-            return carry
-
-        lax.fori_loop(0, tiles, body, 0)
-
-    def plain_grad(k, left, left_beside, right, right_beside, size):
+    def weight_grad(k, left, left_beside, right, right_beside, size, tile=384, chunks=None, push=True):
+        into, lead = red.array(k, c)
+        rows = into.shape[3]
+        per = tile // (4 * rows)
+        for q in red.chunks_of(k) if chunks is None else chunks:
+            _, start, n, _ = red.chunks[q]
+            n = min(n, size - start)
+
+            def body(i, carry, start=start, n=n):
+                cols = pl.ds(pl.multiple_of(i * tile, LANES), tile)
+                part = dot(left(cols), right(start, n), TN) + dot(left_beside(cols), right_beside(start, n), TN)
+                into[lead, pl.ds(i * per, per), :, :, start : start + n] = part.astype(bf16).reshape(per, 4, rows, n)
+                return carry
+
+            lax.fori_loop(0, p.nz // per, body, 0)
+            if push:
+                red.push(q)
+
+    def plain_grad(k, left, left_beside, right, right_beside, size, tile=384, chunks=None, push=True):
         weight_grad(
             k,
             lambda cols: left[:, cols],
@@ -506,47 +583,50 @@
             lambda start, n: right[:, pl.ds(pl.multiple_of(c * size + start, LANES), n)],
             lambda start, n: right_beside[:, start : start + n],
             size,
+            tile,
+            chunks,
+            push,
         )
 
     def gain(i):
-        return r.vec[0, i : i + 1]
+        return r.vec[i : i + 1]
 
     def keep_vec(i, gain_sum, shift_sum):
-        r.vec_sum[0, i : i + 1] = gain_sum
-        r.vec_sum[1, i : i + 1] = shift_sum
-
-    def act_tile(i, carry):
-        h, z = lax.div(i, p.nz), lax.rem(i, p.nz)
-        rows = w[6][h, z].reshape(-1, width)
-        cols = pl.ds(pl.multiple_of(i * rows.shape[0], LANES), rows.shape[0])
-        r.slope[:, cols] = (dot(r.cotangent[...], rows, NT) * r.slope[:, cols].astype(f32)).astype(bf16)
+        r.vec_sum[i : i + 1] = gain_sum
+        r.vec_sum[3 + i : 4 + i] = shift_sum
+
+    for q in g.chunks_of(6):
+        g.tick()
+    for name in ("cot", "act"):
+        swap.wait(name)
+    plain_grad(6, r.act, r.by_act, r.cotangent, r.by_cot, w[6].shape[-1], 4 * w[6].shape[3], push=False)
+    for q in g.chunks_of(6):
+        g.need(q)
+    down_half = w[6].shape[-1]
+
+    def act_tile(z, carry):
+        rows = 4 * w[6].shape[3]
+        cols = pl.ds(pl.multiple_of(z * rows, LANES), rows)
+        act_grad = sum(
+            dot(r.cotangent[:, h * down_half : (h + 1) * down_half], w[6][h, z].reshape(rows, down_half), NT)
+            for h in range(2)
+        )
+        r.slope[:, cols] = (act_grad * r.slope[:, cols].astype(f32)).astype(bf16)
         return carry
 
-    lax.fori_loop(0, 2 * p.nz, act_tile, 0)
+    lax.fori_loop(0, p.nz, act_tile, 0)
     gh = r.slope
+    swap.send("gh", half(gh, o, hidden_half), r.by_hidden_grad)
+    for q in g.chunks_of(6):
+        down_part(q)
+        g.settle(q)
     red.free(6)
-    swap.send("gh", half(gh, o, hidden_half), r.by_hidden_grad)
-    for name in ("act", "cot"):
-        swap.wait(name)
-    for q in (7, 8):
-        g.settle(q)
-    down_rows = 4 * w[6].shape[3]
-    weight_grad(
-        6,
-        lambda cols: r.act[:, cols],
-        lambda cols: r.by_act[:, cols],
-        lambda start, n: r.cotangent[:, start : start + n],
-        lambda start, n: r.by_cot[:, start : start + n],
-        width,
-        tile=down_rows,
-        base=c * hidden_half,
-        tiles=p.nz,
-    )
-    red.push(0)
-    red.push(1)
+    for q in red.chunks_of(6):
+        red.push(q)
     grad_three = input_grad(gh, 5, hidden_half)
     red.free(5)
-    for q in (5, 6):
+    red.push()
+    for q in g.chunks_of(5):
         g.settle(q)
     back, dg, db = norm_back_at(grad_three, r.second[...], gain(2))
     keep_vec(2, dg, db)
@@ -554,14 +634,13 @@
     r.second[...] = grad_second
     r.branch[...] = grad_second.astype(bf16)
     swap.send("gcb", half(r.branch, o, width // 2), r.by_branch)
-    r.mixed_grad[...] = input_grad(r.branch, 4, width // 2).astype(bf16)
-    red.free(4)
-    g.settle(4)
     for name in ("gh", "n3"):
         swap.wait(name)
     plain_grad(5, r.n3, r.by_n3, gh, r.by_hidden_grad, hidden_half)
-    red.push(2)
-    red.push(3)
+    r.mixed_grad[...] = input_grad(r.branch, 4, width // 2).astype(bf16)
+    red.free(4)
+    for q in g.chunks_of(4):
+        g.settle(q)
 
     span = quarter // (slots // 2)
 
@@ -584,41 +663,47 @@
             r.cq_grad[rows, cols] = jnp.where(low_lane, gq[:span], gq[span:]).astype(bf16)
         return carry
 
-    lax.fori_loop(0, pairs, cross_pair, 0)
+    for i in range(0, pairs, 2):
+        lax.fori_loop(i, i + 2, cross_pair, 0)
+        red.push()
     swap.send("gcq", half(r.cq_grad, o, width // 2), r.by_cq_grad)
     grad_two = input_grad(r.cq_grad, 3, width // 2)
     red.free(3)
-    g.settle(3)
+    for q in g.chunks_of(3):
+        g.settle(q)
     back, dg, db = norm_back_at(grad_two, r.first[...], gain(1))
     keep_vec(1, dg, db)
     grad_first = r.second[...] + back
     r.first[...] = grad_first
     r.self_branch[...] = grad_first.astype(bf16)
     swap.send("gsb", half(r.self_branch, o, width // 2), r.by_self_branch)
-    r.att_grad[...] = input_grad(r.self_branch, 2, width // 2).astype(bf16)
+    r.mixed_grad[...] = input_grad(r.self_branch, 2, width // 2).astype(bf16)
     red.free(2)
-    g.settle(2)
+    for q in g.chunks_of(2):
+        g.settle(q)
+    swap.wait("gcb")
+    swap.wait("cm")
+    plain_grad(4, r.cm, r.by_cm, r.branch, r.by_branch, width // 2)
     for s in range(slots):
         j = 0
         for k in range(slots):
             j = jnp.where(lax.rem(r.index[k], slots) == s, k, j)
         b, odd = lax.div(j, 2), lax.rem(j, 2)
-        r.pool_grad[s] = jnp.where(odd == 0, r.gkv[b, :rows_n], r.gkv[b, rows_n:])
-    swap.send("gp", r.pool_grad.at[:, :, pl.ds(pl.multiple_of(o * pool_half, LANES), pool_half)], r.by_pool_grad)
-    swap.wait("gcb")
-    swap.wait("cm")
-    plain_grad(4, r.cm, r.by_cm, r.branch, r.by_branch, width // 2)
-    red.push(4)
-
-    cosine, signed = r.rope[:, :LANES], r.rope[:, LANES:]
+        r.pool[s] = jnp.where(odd == 0, r.gkv[b, :rows_n], r.gkv[b, rows_n:])
+    swap.send("gp", r.pool.at[:, :, pl.ds(pl.multiple_of(o * pool_half, LANES), pool_half)], r.by_pool_grad)
+
+    cosine, signed = r.rope[0, :, :LANES], r.rope[0, :, LANES:]
     place = lax.rem(lax.broadcasted_iota(jnp.int32, (1, 2 * quarter), 1), quarter) + p.s * quarter
     limit = jnp.maximum(place, r.prefix[0] - 1)
+    group, groups = width, 2
+    each = pairs // groups
 
     def self_pair(i, carry):
         cols = pl.ds(pl.multiple_of(i * LANES, LANES), LANES)
         vcols = pl.ds(pl.multiple_of(i * LANES + pool_half, LANES), LANES)
+        start = lax.div(i, each) * group + lax.rem(i, each) * LANES
         queries = stacked(r.q[:, cols], low, high) * bf16(HEAD**-0.5)
-        grads = stacked(r.att_grad[:, cols], low, high)
+        grads = stacked(r.mixed_grad[:, cols], low, high)
         keys = r.kv[:, :, cols].reshape(-1, LANES)
         values = r.kv[:, :, vcols].reshape(-1, LANES)
         scores = dot(keys, queries, NT)
@@ -626,44 +711,85 @@
         probs = jnp.exp(jnp.where(key_place <= limit, scores, masked) - r.lse[i])
         grad_probs = dot(values, grads, NT)
         score_grad = (probs * (grad_probs - jnp.sum(probs * grad_probs, 0, keepdims=True))).astype(bf16)
-        r.gkv[:, :, cols] = dot(score_grad, queries).astype(bf16).reshape(4, quarter, LANES)
-        r.gkv[:, :, vcols] = dot(probs.astype(bf16), grads).astype(bf16).reshape(4, quarter, LANES)
+        for offset, part in ((0, dot(score_grad, queries)), (group // 2, dot(probs.astype(bf16), grads))):
+            there = pl.ds(pl.multiple_of(start + offset, LANES), LANES)
+            r.gkv[:, :, there] = part.astype(bf16).reshape(4, quarter, LANES)
         gq = dot(score_grad, keys, TN) * HEAD**-0.5
         gq = jnp.where(low_lane, gq[:quarter], gq[quarter:])
-        r.joined_grad[:, cols] = rotate(gq, cosine, -signed).astype(bf16)
+        r.q_grad[:, cols] = rotate(gq, cosine, -signed).astype(bf16)
         return carry
 
-    lax.fori_loop(0, pairs // 2, self_pair, 0)
-    red.push()
-    lax.fori_loop(pairs // 2, pairs, self_pair, 0)
-    swap.send("far", r.gkv.at[p.s_d], r.kv_far)
-    swap.send("near", r.gkv.at[p.s_c], r.kv_near)
+    for i in range(groups):
+        for j in range(each):
+            lax.fori_loop(i * each + j, i * each + j + 1, self_pair, 0)
+            red.push()
+        cols = pl.ds(i * group, group)
+        swap.send(f"far{i}", r.gkv.at[p.s_d, :, cols], r.by_act.at[:, cols])
+        swap.send(f"near{i}", r.gkv.at[p.s_c, :, cols], r.by_act.at[:, pl.ds((groups + i) * group, group)])
+    swap.send("gq", half(r.q_grad, o, width // 2), r.by_q_grad)
     swap.wait("gcq")
     swap.wait("n2")
     plain_grad(3, r.n2, r.by_n2, r.cq_grad, r.by_cq_grad, width // 2)
-    swap.wait("far")
-    r.gkv[p.s_y] = (r.gkv[p.s_y].astype(f32) + r.kv_far[...].astype(f32)).astype(bf16)
-    far = remote(r.gkv.at[p.s_y], r.kv_y, kv_sem.at[6], kv_sem.at[7], p.to_y)
-    far.start()
-    red.push(5)
+    for i in range(groups):
+        cols = slice(i * group, (i + 1) * group)
+        for j, (name, s, other) in enumerate((("near", p.s, groups + i), ("far", p.s_y, i))):
+            swap.wait(f"{name}{i}")
+            total = r.gkv[s, :, cols].astype(f32) + r.by_act[:, other * group : (other + 1) * group].astype(f32)
+            total = jnp.concatenate([turned(total[:, : group // 2], j, -1), total[:, group // 2 :]], 1)
+            r.gkv[s, :, cols] = total.astype(bf16)
+    half_kv = pl.ds(pl.multiple_of(o * group, LANES), group)
+    for j, (name, s) in enumerate((("gkv", p.s), ("gkvy", p.s_y))):
+        swap.send(name, r.gkv.at[s, :, half_kv], r.by_kv_grad.at[pl.ds(j * quarter, quarter)])
+    red.push()
+    part = width // 2
+
+    def kv_grads(cols):
+        return jnp.concatenate([r.gkv[s, :, cols] for s in (p.s, p.s_y)], 0)
+
+    grad_one = sum(dot(kv_grads(slice(h * group, (h + 1) * group)), half_of(w[0], h, part, group), NT) for h in range(2))
+    r.mixed_grad[...] = grad_one[quarter:].astype(bf16)
+    to_y = remote(r.mixed_grad, r.one_y, kv_sem.at[0], kv_sem.at[1], p.to_y)
+    to_y.start()
+    r.second[...] = grad_one[:quarter] + sum(
+        dot(r.q_grad[:, h * part : (h + 1) * part], half_of(w[0], h, 0, part), NT) for h in range(2)
+    )
+    red.free(0)
+    for q in g.chunks_of(0):
+        g.settle(q)
+    for name in ("gq", "n1", "gkv", "gkvy"):
+        swap.wait(name)
+    first_chunk, *kv_chunks, vec_chunk = red.chunks_of(0)
+    plain_grad(0, r.n1.at[:quarter], r.by_n1.at[:quarter], r.q_grad, r.by_q_grad, part, chunks=[first_chunk])
+    weight_grad(
+        0,
+        lambda cols: r.n1[:, cols],
+        lambda cols: r.by_n1[:, cols],
+        lambda start, n: kv_grads(pl.ds(pl.multiple_of(c * group + start - part, LANES), n)),
+        lambda start, n: r.by_kv_grad[:, start - part : start - part + n],
+        3 * part,
+        chunks=kv_chunks,
+    )
     swap.wait("gsb")
     swap.wait("att")
     plain_grad(2, r.att, r.by_att, r.self_branch, r.by_self_branch, width // 2)
-    red.push(6)
 
     out = [None, None]
     for s in range(slots):
-        rows = r.pool_grad[s]
-        part = sum(
+        rows = r.pool[s]
+        slot_grad = sum(
             dot(rows[:, h * pool_half : (h + 1) * pool_half], half_of(w[1], h), NT) for h in range(2)
         )
         if out[s % 2] is not None:
             out[s % 2].wait()
-        r.stage[s % 2] = part
-        out[s % 2] = pltpu.make_async_copy(r.stage.at[s % 2], r.neighbours_grad.at[s], r.out_sem.at[s % 2])
+        stage = r.stage.at[s % 2]
+        stage[...] = slot_grad
+        out[s % 2] = pltpu.make_async_copy(stage, r.neighbours_grad.at[s], r.out_sem.at[s % 2])
         out[s % 2].start()
+        if s == slots // 2:
+            red.push()
     red.free(1)
-    g.settle(1)
+    for q in g.chunks_of(1):
+        g.settle(q)
     swap.wait("gp")
     swap.wait("nb")
     size = slots * rows_n
@@ -671,39 +797,22 @@
         1,
         lambda cols: r.neighbours[:, :, cols].reshape(size, -1),
         lambda cols: r.by_neighbours[:, :, cols].reshape(size, -1),
-        lambda start, n: r.pool_grad[:, :, pl.ds(pl.multiple_of(c * pool_half + start, LANES), n)].reshape(size, -1),
+        lambda start, n: r.pool[:, :, pl.ds(pl.multiple_of(c * pool_half + start, LANES), n)].reshape(size, -1),
         lambda start, n: r.by_pool_grad[:, :, start : start + n].reshape(size, -1),
         pool_half,
     )
-    red.push(7)
-    remote(r.gkv.at[p.s_y], r.kv_y, kv_sem.at[6], kv_sem.at[7], p.to_y).wait_recv()
-    swap.wait("near")
-    for start in range(0, 2 * width, LANES):
-        cols = slice(start, start + LANES)
-        total = r.gkv[p.s, :, cols].astype(f32) + r.kv_near[:, cols].astype(f32) + r.kv_y[:, cols].astype(f32)
-        if start < width:
-            total = rotate(total, cosine, -signed)
-        r.joined_grad[:, width + start : width + start + LANES] = total.astype(bf16)
-    joined_half = 3 * width // 2
-    swap.send("gj", half(r.joined_grad, o, joined_half), r.by_joined_grad)
-    grad_one = input_grad(r.joined_grad, 0, joined_half)
-    red.free(0)
-    g.settle(0)
+    to_y.wait_recv()
+    grad_one = r.second[...] + r.one_y[...].astype(f32)
     back, dg, db = norm_back_at(grad_one, r.tokens[...].astype(f32), gain(0))
     keep_vec(0, dg, db)
     r.tokens_grad[...] = r.first[...] + back
-    swap.send("vec", r.vec_sum.at[o], r.by_vec)
-    swap.wait("gj")
-    swap.wait("n1")
-    plain_grad(0, r.n1, r.by_n1, r.joined_grad, r.by_joined_grad, joined_half)
+    swap.send("vec", r.vec_sum, r.by_vec)
     swap.wait("vec")
-    vec = r.vec_sum[c] + r.by_vec[...]
-    vec = jnp.concatenate([vec, jnp.zeros((LANES - 8, width), f32)], 0)
-    w[0][c, :, :, :, joined_half:] = jnp.transpose(vec).astype(bf16).reshape(p.nz, 4, -1, LANES)
-    for q in range(8, len(red.chunks)):
-        red.push(q)
+    vec = jnp.concatenate([r.vec_sum[...] + r.by_vec[...], jnp.zeros((LANES - 8, width), f32)], 0)
+    w[0][c, :, :, :, 3 * part :] = jnp.transpose(vec).astype(bf16).reshape(p.nz, 4, -1, LANES)
+    red.push(vec_chunk)
     red.drain()
-    for cp in (*red.sent, *swap.sent, far):
+    for cp in (*red.sent, *swap.sent, to_y):
         cp.wait_send()
     for cp in out:
         cp.wait()
@@ -718,18 +827,60 @@
     return table.astype(np.float32).reshape(4, -1, 2 * LANES)
 
 
-def column_halves(v):
-    return v[:, : v.shape[1] // 2], v[:, v.shape[1] // 2 :]
-
-
-def shard_halves(w_qkv, w_cross_kv, w_out, w_cross_q, w_cross_out, w_up, gains, shifts, nz):
-    rows = w_qkv.shape[0]
-    up = jnp.swapaxes(w_up.reshape(rows, nz * 4, 2, -1), 1, 2).reshape(rows, -1)
-    pads = [jnp.pad(jnp.stack(v, 1), ((0, 0), (0, LANES - 3))) for v in (gains, shifts)]
-    parts = [column_halves(v) for v in (w_qkv, w_cross_kv, w_out, w_cross_q, w_cross_out, up)]
-    return jnp.stack(
-        [jnp.concatenate([parts[0][h], pads[h], *(v[h] for v in parts[1:])], 1) for h in range(2)]
-    ).astype(f32)
+def deliver_kernel(*refs):
+    n = 3
+    plain, sums = refs[:n], refs[n : n + 7]
+    outs, sem = refs[n + 7 : -1], refs[-1]
+    copies = [(src, dst) for src, dst in zip(plain, outs[:n])]
+    for k, dst in zip(range(7), outs[n : n + 7]):
+        parts = 3 if k == 0 else 1
+        part = dst.shape[1] // (2 * parts)
+        for h in range(2):
+            for i in range(parts):
+                source, there = i * part, i * 2 * part + h * part
+                copies.append((sums[k].at[h, :, source : source + part], dst.at[:, there : there + part]))
+    copies = [pltpu.make_async_copy(src, dst, sem.at[i]) for i, (src, dst) in enumerate(copies)]
+    for cp in copies:
+        cp.start()
+    half = outs[n].shape[1] // 2
+    turned = jnp.transpose(
+        jnp.concatenate([sums[0][0, :, half:], jnp.zeros((LANES - sums[0].shape[1], LANES), f32)], 0)
+    )
+    outs[n + 7][...] = turned[:8, : outs[n + 7].shape[1]]
+    for cp in copies:
+        cp.wait()
+
+
+def deliver(out, tokens_grad, neighbours_grad, summed):
+    rows = summed[0].shape[1]
+    widths = [2 * v.shape[2] for v in summed]
+    widths[0] -= 2 * LANES
+    shapes = [out, tokens_grad, neighbours_grad] + [
+        jax.ShapeDtypeStruct((v.shape[1], n), f32) for v, n in zip(summed, widths)
+    ]
+    vmem, anywhere = pl.BlockSpec(memory_space=pltpu.VMEM), pl.BlockSpec(memory_space=pl.ANY)
+    out, tokens_grad, neighbours_grad, *grads, vectors = pl.pallas_call(
+        deliver_kernel,
+        out_shape=[jax.ShapeDtypeStruct(v.shape, v.dtype) for v in shapes] + [jax.ShapeDtypeStruct((8, rows), f32)],
+        in_specs=[vmem] * 10,
+        out_specs=[anywhere] * 10 + [vmem],
+        scratch_shapes=[pltpu.SemaphoreType.DMA((21,))],
+        compiler_params=pltpu.CompilerParams(vmem_limit_bytes=32 * 2**20),
+        name="deliver",
+    )(out, tokens_grad, neighbours_grad, *summed)
+    return (
+        out[None],
+        tokens_grad[None],
+        neighbours_grad[None],
+        grads[0],
+        grads[2],
+        grads[3],
+        grads[1],
+        grads[4],
+        grads[5],
+        grads[6],
+        *(vectors[i] for i in (0, 3, 1, 4, 2, 5)),
+    )
 
 
 class Refs:
@@ -738,47 +889,75 @@
             setattr(self, name, ref)
 
 
-NAMES_IN = ("shards", "w_down", "tokens", "cotangent", "prefix", "neighbours", "index", "rope_table")
+NAMES_IN = (
+    "w_qkv",
+    "w_cross_kv",
+    "w_out",
+    "w_cross_q",
+    "w_cross_out",
+    "w_up",
+    "w_down",
+    "vectors",
+    "tokens",
+    "cotangent",
+    "prefix",
+    "neighbours",
+    "index",
+    "rope_table",
+)
 NAMES_OUT = ("out", "tokens_grad", "neighbours_grad")
 GATHER = (
-    (0, 0, 1280, 2),
-    (1, 0, 768, 2),
+    (0, 768, 512, 2),
+    (0, 384, 384, 2),
+    (0, 0, 384, 2),
+    (1, 0, 384, 2),
+    (1, 384, 384, 2),
     (2, 0, 384, 2),
     (3, 0, 384, 2),
     (4, 0, 384, 2),
-    (5, 0, 768, 2),
-    (5, 768, 768, 2),
-    (6, 0, 384, 2),
-    (6, 384, 384, 2),
+    (5, 0, 384, 2),
+    (5, 384, 384, 2),
+    (5, 768, 384, 2),
+    (5, 1152, 384, 2),
+    (6, 0, 128, 2),
+    (6, 128, 128, 2),
+    (6, 256, 128, 2),
 )
 REDUCE = (
-    (6, 0, 384, 2),
-    (6, 384, 384, 2),
-    (5, 0, 768, 2),
-    (5, 768, 768, 2),
+    (6, 0, 256, 2),
+    (6, 256, 128, 2),
+    (5, 0, 512, 2),
+    (5, 512, 512, 2),
+    (5, 1024, 512, 2),
     (4, 0, 384, 2),
     (3, 0, 384, 2),
     (2, 0, 384, 2),
-    (1, 0, 768, 2),
-    (0, 0, 640, 2),
-    (0, 640, 640, 2),
+    (1, 0, 384, 2),
+    (1, 384, 384, 2),
+    (0, 0, 384, 2),
+    (0, 384, 384, 2),
+    (0, 768, 384, 2),
+    (0, 1152, 128, 2),
 )
 
 
 def memory(nz, quarter, width, hidden, slots, rows_n, rows):
     halves = (3 * width // 2 + LANES, width, width // 2, width // 2, width // 2, hidden // 2)
     weights = [((2, nz, 4, 2 * rows, h), bf16) for h in halves]
-    weights.append(((2, nz, 4, hidden // (8 * nz), width), bf16))
+    weights.append(((2, nz, 4, hidden // (4 * nz), width // 2), bf16))
     sums = [((2, rows, h), f32) for h in halves]
-    sums.append(((hidden // (8 * nz), width), f32))
+    sums.append(((2, hidden // (8 * nz), width // 2), f32))
     tok, half_tok = ((quarter, width), bf16), ((quarter, width // 2), bf16)
     half_hidden = ((quarter, hidden // 2), bf16)
     pool_half = ((slots, rows_n, width), bf16)
     kv = ((quarter, 2 * width), bf16)
     arrays = dict(
+        pack=((2, rows, sum(halves)), f32),
         beside=((rows, sum(halves)), f32),
-        rope=((quarter, 2 * LANES), f32),
-        n1=tok,
+        down_sum=((1, *weights[6][0][1:]), bf16),
+        down_beside=((hidden // (8 * nz), width // 2), f32),
+        rope=((2, quarter, 2 * LANES), f32),
+        n1=((2 * quarter, width), bf16),
         q=tok,
         kv=((4, *kv[0]), bf16),
         att=tok,
@@ -793,22 +972,18 @@
         n3=tok,
         act=((quarter, hidden), bf16),
         slope=((quarter, hidden), bf16),
-        vec=((2, 8, width), f32),
+        vec=((8, width), f32),
         branch=tok,
         mixed_grad=tok,
         cq_grad=tok,
         self_branch=tok,
-        att_grad=tok,
-        joined_grad=((quarter, 3 * width), bf16),
-        pool_grad=((slots, rows_n, 2 * width), bf16),
+        q_grad=tok,
+        one_y=tok,
+        stage=((2, rows_n, width), f32),
         gkv=((4, *kv[0]), bf16),
-        kv_far=kv,
-        kv_near=kv,
-        kv_y=kv,
-        stage=((2, rows_n, width), f32),
-        vec_sum=((2, 8, width), f32),
-        by_act=half_hidden,
-        by_cot=tok,
+        vec_sum=((8, width), f32),
+        by_act=((quarter, hidden), bf16),
+        by_cot=half_tok,
         by_n3=tok,
         by_hidden_grad=half_hidden,
         by_cm=tok,
@@ -819,8 +994,9 @@
         by_cq_grad=half_tok,
         by_att=tok,
         by_self_branch=half_tok,
-        by_n1=tok,
-        by_joined_grad=((quarter, 3 * width // 2), bf16),
+        by_n1=((2 * quarter, width), bf16),
+        by_q_grad=half_tok,
+        by_kv_grad=((2 * quarter, width), bf16),
         by_vec=((8, width), f32),
     )
     return weights, arrays, sums
@@ -839,19 +1015,16 @@
     r.take(NAMES_OUT, some(len(NAMES_OUT)))
     r.sums, r.w = some(7), some(7)
     r.take(names, some(len(names)))
-    r.pair_sem, r.rope_sem, r.out_sem, kv_sem, swap_sem, g_send, g_recv, r_send, r_recv, r.credit = refs
+    r.pair_sem, r.rope_sem, r.out_sem, fkv_sem, kv_sem, swap_sem, g_send, g_recv, r_send, r_recv, r.credit = refs
     p = Place(nz)
-    barrier = pltpu.get_barrier_semaphore()
-    friends = [*p.to_z, p.to_x, p.to_y, p.to_c]
-    for device in friends:
-        pl.semaphore_signal(barrier, inc=1, device_id=device, device_id_type=MESH)
-    pl.semaphore_wait(barrier, len(friends))
     g = Gather(p, r.w, GATHER, g_send, g_recv)
     swap = Swap(p, swap_sem)
     pairs = r.tokens.shape[1] // LANES
-    forward(p, r, g, swap, kv_sem, pairs)
+    down_part, turned, sent = forward(p, r, g, swap, fkv_sem, pairs)
     red = Reduce(p, r, REDUCE, r_send, r_recv)
-    backward(p, r, g, swap, red, kv_sem, pairs)
+    backward(p, r, g, swap, red, kv_sem, pairs, down_part, turned)
+    for cp in sent:
+        cp.wait_send()
 
 
 def local_fast(
@@ -878,10 +1051,7 @@
     quarter, width = tokens.shape[1:]
     rows, hidden = w_up.shape
     slots, rows_n = neighbours.shape[1:3]
-    shards = shard_halves(
-        w_qkv, w_cross_kv, w_out, w_cross_q, w_cross_out, w_up,
-        (gain_one, gain_two, gain_three), (shift_one, shift_two, shift_three), nz,
-    )
+    vectors = jnp.stack([gain_one, gain_two, gain_three, shift_one, shift_two, shift_three], 1)
     weights, arrays, sums = memory(nz, quarter, width, hidden, slots, rows_n, rows)
     vmem, smem, anywhere = (pl.BlockSpec(memory_space=m) for m in (pltpu.VMEM, pltpu.SMEM, pl.ANY))
     made = [((quarter, width), bf16), ((quarter, width), f32), ((slots, rows_n, width), f32), *sums]
@@ -889,15 +1059,16 @@
     out, tokens_grad, neighbours_grad, *summed = pl.pallas_call(
         functools.partial(layer_kernel, nz, tuple(arrays)),
         out_shape=[jax.ShapeDtypeStruct(*v) for v in made],
-        in_specs=[vmem, vmem, vmem, vmem, smem, vmem, smem, anywhere],
+        in_specs=[vmem] * 10 + [smem, vmem, smem, anywhere],
         out_specs=[vmem, vmem, anywhere] + [vmem] * len(sums),
         scratch_shapes=[pltpu.VMEM(*v) for v in (*weights, *arrays.values())]
         + [
+            dma((6,)),
             dma((2,)),
-            dma,
             dma((2,)),
-            dma((8,)),
-            dma((2, 20)),
+            dma((2, 2)),
+            dma((2,)),
+            dma((2, 28)),
             dma((len(GATHER), 12)),
             dma((len(GATHER), 12)),
             dma((len(REDUCE), 8)),
@@ -908,26 +1079,11 @@
             collective_id=0, has_side_effects=True, vmem_limit_bytes=64 * 2**20 - 2**17
         ),
     )(
-        shards, w_down, tokens[0], cotangent[0], prefix_len, neighbours[0],
+        w_qkv, w_cross_kv, w_out, w_cross_q, w_cross_out, w_up, w_down, vectors,
+        tokens[0], cotangent[0], prefix_len, neighbours[0],
         neighbour_index.reshape(-1), jnp.asarray(rope_table(4 * quarter)),
     )
-    whole = [jnp.concatenate([v[0], v[1]], 1) for v in summed[1:5]]
-    half = 3 * width // 2
-    up = jnp.concatenate([v.reshape(rows, 4 * nz, 1, -1) for v in summed[5]], 2)
-    vectors = [summed[0][h, :, half + i] for i in range(3) for h in range(2)]
-    return (
-        out[None],
-        tokens_grad[None],
-        neighbours_grad[None],
-        jnp.concatenate([summed[0][0, :, :half], summed[0][1, :, :half]], 1),
-        whole[1],
-        whole[2],
-        whole[0],
-        whole[3],
-        up.reshape(rows, hidden),
-        summed[6],
-        *vectors,
-    )
+    return deliver(out, tokens_grad, neighbours_grad, summed)
 
 
 def pick_slots(pool, index):

time: 290 us -> 243 us (0.84); the launches traced: 289 us -> 239 us
  Pallas kernels: 258 us -> 223 us
  local copies, waits for them, and re-layouts: 23.6 us -> 13.8 us
  other arithmetic: 5.7 us -> 0 us
    pallas_call x1, Pallas kernels: 258 us -> 221 us  [local_fast(): pl.pallas_call(functools.partial(layer_kernel, nz, tuple(arrays)), out_sh...]
    squeeze x5 -> x1, local copies, waits for them, and re-layouts: 4.27 us -> 0.54 us  [deliver(): vectors[i]]
    concatenate x6 -> x0, other arithmetic: 3.32 us -> none  [the longest x4 2.59 us: local_fast(): whole = [jnp.concatenate([v[0], v[1]], 1) for v in summed[1:5]]]
    unnamed x15 -> x21, local copies, waits for them, and re-layouts: 10.9 us -> 11.2 us
where the time goes in v3:
time: 243 us; the launch traced here: 239 us
  Pallas kernels  223 us (92%)
  local copies, waits for them, and re-layouts  13.8 us (6%)
    pallas_call x1, Pallas kernels, local_fast(): pl.pallas_call(functools.partial(layer_kernel, nz, tuple(arrays)), out_sh...  221 us
    unnamed x21, local copies, waits for them, and re-layouts  11.2 us

profile of v3, /device:TPU:1, one launch (start us, length us, event | category | flops | bytes accessed | tf_op | source)
XLA Modules:
  0.0 238.6 jit_solution(12419623729123510221)
XLA Ops:
  1.3 0.8 copy.49
  2.1 0.6 reshape.35.refs_12_
  2.7 0.8 stack.27
  3.4 0.7 copy.50.refs_7_
  4.1 220.7 %shard_map.306 = (bf16[256,768]{1,0:T(8,128)(2,1)}, f32[256,768]{1,0:T(8,128)}, f32[8,128,768]{2,1,0:T(8,128)}, f32[2,24,1280]{2,1,0:T(8,128)}, f32[2,24,768]{2,...) custom-call(bf16[24,2304]{1,0:T(8,128)(2,1)} %refs_0_.1, ...), custom_call_target="tpu_custom_call" | custom-call | tf_op jit(solution)/shard_map/pallas_call | solution.py:1059
  224.8 0.0 copy-start
  224.8 1.9 copy-done
  226.7 0.0 copy-start.1
  226.7 1.1 copy-done.1
  227.8 0.0 copy-start.2
  227.8 1.0 copy-done.2
  228.8 0.0 copy-start.3
  228.8 1.0 copy-done.3
  229.8 0.0 copy-start.4
  229.8 1.0 copy-done.4
  230.7 0.0 copy-start.5
  230.7 0.9 copy-done.5
  231.7 0.0 copy-start.6
  231.7 0.9 copy-done.6
  232.6 0.0 copy-start.7
  232.6 0.9 copy-done.7
  233.5 0.0 copy-start.8
  233.5 0.9 copy-done.8
  234.4 0.0 copy-start.9
  234.4 0.9 copy-done.9
  235.3 2.6 %deliver.1 = (bf16[256,768]{1,0:T(8,128)(2,1)}, f32[256,768]{1,0:T(8,128)}, f32[8,128,768]{2,1,0:T(8,128)}, f32[24,2304]{1,0:T(8,128)}, f32[24,1536]{1,0:T(8,128...) custom-call(bf16[256,768]{1,0:T(8,128)(2,1)S(1)} %copy-done.2, ...), custom_call_target="tpu_custom_call" | custom-call | tf_op jit(solution)/shard_map/deliver/pallas_call | solution.py:862
  237.8 0.5 slice_bitcast_fusion
Async XLA Ops:
  224.8 1.9 copy-start
  226.7 1.1 copy-start.1
  227.8 1.0 copy-start.2
  228.8 1.0 copy-start.3
  229.8 1.0 copy-start.4
  230.7 0.9 copy-start.5
  231.7 0.9 copy-start.6
  232.6 0.9 copy-start.7
  233.5 0.9 copy-start.8
  234.4 0.9 copy-start.9

commit v4 on v3

--- a/solution.py
+++ b/solution.py
@@ -19,8 +19,9 @@
 NT = (((1,), (1,)), ((), ()))
 TN = (((0,), (0,)), ((), ()))
 LANES = 128
-AHEAD = 2
-TICKS_KV = 0
+AHEAD = 3
+SPREAD = 3
+ACROSS, LAST = 2, 4
 
 
 def dot(a, b, dims=NN):
@@ -76,36 +77,94 @@
         self.p, self.w, self.chunks, self.ss, self.rs = place, weights, chunks, send, recv
         self.sent = [[] for _ in chunks]
         self.t, self.have = 0, set()
+        self.z_first = [q for q, v in enumerate(chunks) if v[3] > 0]
+        self.plane_first = [q for q, v in enumerate(chunks) if v[3] <= 0]
 
     def chunks_of(self, k):
         return [q for q, v in enumerate(self.chunks) if v[0] == k]
 
     def begin(self):
-        self.along_z(0)
+        self.along_z(self.z_first[0])
 
     def tick(self):
-        t, n = self.t, len(self.chunks)
-        if t >= n + 2:
+        t, order = self.t, self.z_first
+        n = len(order)
+        if t >= n + LAST:
             return
         if t == 0:
-            for q in range(1, AHEAD):
+            for q in order[1:AHEAD]:
                 self.along_z(q)
+            for q in self.plane_first:
+                self.plane_out(q)
         if t < n:
-            self.along_xy(t)
+            self.along_xy(order[t])
         if t + AHEAD < n:
-            self.along_z(t + AHEAD)
-        if 0 <= t - 1 < n:
-            self.across(t - 1)
-        if 0 <= t - 2 < n:
-            self.last(t - 2)
+            self.along_z(order[t + AHEAD])
+        if t == 1:
+            for q in self.plane_first:
+                self.plane_across(q)
+        if t >= 2 and (t - 2) % SPREAD == 0 and (t - 2) // SPREAD < len(self.plane_first):
+            self.plane_z(self.plane_first[(t - 2) // SPREAD])
+        if 0 <= t - ACROSS < n:
+            self.across(order[t - ACROSS])
+        if 0 <= t - LAST < n:
+            self.last(order[t - LAST])
         self.t += 1
 
     def need(self, q):
-        while self.t <= q + 2:
-            self.tick()
+        if q in self.plane_first:
+            while self.t <= SPREAD * self.plane_first.index(q) + 2:
+                self.tick()
+        else:
+            while self.t <= self.z_first.index(q) + LAST:
+                self.tick()
         if q not in self.have:
             self.have.add(q)
-            self.ready(q)
+            if q in self.plane_first:
+                self.plane_last(q)
+                self.plane_ready(q)
+            else:
+                self.ready(q)
+
+    def plane_out(self, q):
+        p = self.p
+        mine = self.part(q, p.c, p.z, p.own)
+        for j, device in ((3, p.to_x), (4, p.to_y), (7, p.to_c)):
+            self.send(q, j, mine, device)
+
+    def plane_across(self, q):
+        p = self.p
+        from_x, from_y = self.part(q, p.c, p.z, p.at_x), self.part(q, p.c, p.z, p.at_y)
+        self.wait(q, 3, from_x)
+        self.send(q, 8, from_x, p.to_c)
+        self.wait(q, 4, from_y)
+        self.send(q, 9, from_y, p.to_c)
+        if self.chunks[q][3] == 0:
+            self.send(q, 5, from_y, p.to_x)
+        else:
+            self.send(q, 5, from_x, p.to_y)
+
+    def plane_z(self, q):
+        p, every = self.p, slice(None)
+        diag = self.part(q, p.c, p.z, p.at_d)
+        self.wait(q, 5, diag)
+        self.send(q, 10, diag, p.to_c)
+        for j, device in enumerate(p.to_z):
+            self.send(q, j, self.part(q, p.c, p.z, every), device)
+
+    def plane_last(self, q):
+        p, every = self.p, slice(None)
+        for j, z in enumerate(p.z_from):
+            ref = self.part(q, p.c, z, every)
+            self.wait(q, j, ref)
+            self.send(q, 11 + j, ref, p.to_c)
+
+    def plane_ready(self, q):
+        p, every = self.p, slice(None)
+        for j, xy in ((7, p.own), (8, p.at_x), (9, p.at_y), (10, p.at_d)):
+            self.wait(q, j, self.part(q, p.o, p.z, xy))
+        for j, z in enumerate(p.z_from):
+            self.wait(q, 11 + j, self.part(q, p.o, z, every))
 
     def part(self, q, half, z, xy):
         k, start, width, _ = self.chunks[q]
@@ -201,6 +260,10 @@
     w = r.w
 
     vectors = r.vectors[...].astype(f32)
+    count, rows = vectors.shape
+    vectors = jnp.concatenate([vectors, jnp.zeros((count, LANES - rows), f32)], 1)
+    vectors = jnp.concatenate([vectors, jnp.zeros((LANES - count, LANES), f32)], 0)
+    vectors = jnp.transpose(vectors)[:rows]
     start = 0
     for k, ref in enumerate((r.w_qkv, r.w_cross_kv, r.w_out, r.w_cross_q, r.w_cross_out, r.w_up)):
         rows = ref[...].astype(f32)
@@ -212,8 +275,7 @@
                 source = i * 2 * part + h * part
                 r.pack[h, :, start + i * part : start + (i + 1) * part] = rows[:, source : source + part]
             if k == 0:
-                r.pack[h, :, start + size : start + size + LANES] = jnp.zeros((rows.shape[0], LANES), f32)
-                r.pack[h, :, start + size : start + size + vectors.shape[1]] = vectors
+                r.pack[h, :, start + size : start + size + LANES] = vectors
         start += w[k].shape[-1]
     p.meet()
     first = remote(r.pack.at[p.o], r.beside, r.pair_sem.at[0], r.pair_sem.at[1], p.to_c)
@@ -312,25 +374,26 @@
         remote(r.kv.at[s], r.kv.at[s], kv_sem.at[0, i], kv_sem.at[1, i], p.to_c).wait_recv()
 
     low_lane, low, high = lane_masks()
-    place = lax.rem(lax.broadcasted_iota(jnp.int32, (1, 2 * quarter), 1), quarter) + p.s * quarter
+    place = lax.broadcasted_iota(jnp.int32, (1, quarter), 1) + p.s * quarter
     limit = jnp.maximum(place, r.prefix[0] - 1)
 
     def self_pair(i, carry):
         cols = pl.ds(pl.multiple_of(i * LANES, LANES), LANES)
         vcols = pl.ds(pl.multiple_of(i * LANES + w[1].shape[-1], LANES), LANES)
-        queries = stacked(r.q[:, cols], low, high) * bf16(HEAD**-0.5)
         keys = r.kv[:, :, cols].reshape(-1, LANES)
         values = r.kv[:, :, vcols].reshape(-1, LANES)
-        scores = dot(keys, queries, NT)
-        key_place = lax.broadcasted_iota(jnp.int32, scores.shape, 0)
-        scores = jnp.where(key_place <= limit, scores, masked)
-        top = jnp.max(scores, 0, keepdims=True)
-        e = jnp.exp(scores - top)
-        total = jnp.sum(e, 0, keepdims=True)
-        weights = (e * (1.0 / total)).astype(bf16)
-        r.lse[i] = top + jnp.log(total)
-        mixed = dot(weights, values, TN)
-        r.att[:, cols] = jnp.where(low_lane, mixed[:quarter], mixed[quarter:]).astype(bf16)
+        mixed = []
+        for e, lanes in enumerate((low, high)):
+            scores = dot(keys, r.q[:, cols] * (lanes * bf16(HEAD**-0.5)), NT)
+            key_place = lax.broadcasted_iota(jnp.int32, scores.shape, 0)
+            scores = jnp.where(key_place <= limit, scores, masked)
+            top = jnp.max(scores, 0, keepdims=True)
+            exped = jnp.exp(scores - top)
+            total = jnp.sum(exped, 0, keepdims=True)
+            weights = (exped * (1.0 / total)).astype(bf16)
+            r.lse[i, :, e * quarter : (e + 1) * quarter] = top + jnp.log(total)
+            mixed.append(dot(weights, values, TN))
+        r.att[:, cols] = jnp.where(low_lane, *mixed).astype(bf16)
         return carry
 
     for i in range(0, pairs, 2):
@@ -355,7 +418,7 @@
         cols = pl.ds(pl.multiple_of(i * LANES, LANES), LANES)
         vcols = pl.ds(pl.multiple_of(i * LANES + w[1].shape[-1], LANES), LANES)
         for b in range(slots // 2):
-            two = [lax.rem(r.index[2 * b + j], slots) for j in range(2)]
+            two = [lax.rem(r.index[b, j], slots) for j in range(2)]
             rows = slice(b * span, (b + 1) * span)
             queries = stacked(r.cq[rows, cols], low, high) * bf16(HEAD**-0.5)
             keys = jnp.concatenate([r.pool[t, :, cols] for t in two], 0)
@@ -408,7 +471,7 @@
     return down_part, turned, (first, down, tokens_y, *kv_sent)
 
 
-LAG = 3
+LAG = 4
 
 
 class Reduce:
@@ -423,7 +486,9 @@
             pl.semaphore_signal(self.r.credit.at[k], inc=1, device_id=device, device_id_type=MESH)
 
     def array(self, k, half):
-        return (self.r.down_sum, 0) if k == 6 and half is self.p.c else (self.w[k], half)
+        if k == 6:
+            return self.r.down_sum, 0 if half is self.p.c else 1
+        return self.w[k], half
 
     def at(self, q, half, z, xy):
         k, start, width, _ = self.chunks[q]
@@ -449,10 +514,7 @@
         remote(ref, ref, self.ss.at[q, j], self.rs.at[q, j], self.p.to_c).wait_recv()
 
     def diagonal(self, q):
-        p, (k, _, _, cut) = self.p, self.chunks[q]
-        if k not in self.open:
-            pl.semaphore_wait(self.r.credit.at[k], 1 + p.nz)
-            self.open.add(k)
+        p, cut = self.p, self.chunks[q][3]
         for j, z, device in ((0, pl.ds(0, cut), p.to_y), (1, pl.ds(cut, p.nz - cut), p.to_x)):
             self.copy(q, j, self.at(q, p.c, z, p.at_d), self.at(q, p.o, z, 0), device)
 
@@ -475,12 +537,54 @@
         for j, device in enumerate(p.to_z):
             self.copy(q, 4 + j, self.at(q, p.c, p.z_of[j], p.own), self.at(q, p.o, j, 3), device)
 
+    def steps(self, q):
+        if self.chunks[q][3] > 0:
+            return self.diagonal, self.across, self.along_z, self.last
+        return self.z_out, self.plane_diagonal, self.plane_across, self.plane_last
+
+    def z_out(self, q):
+        p, every = self.p, slice(None)
+        for j, device in enumerate(p.to_z):
+            self.copy(q, 4 + j, self.at(q, p.c, p.z_of[j], every), self.at(q, p.o, j, every), device)
+
+    def plane_diagonal(self, q):
+        p, every = self.p, slice(None)
+        for j in range(p.nz - 1):
+            self.wait(q, 4 + j, self.at(q, p.o, j, every))
+        for xy in range(4):
+            total = self.load(q, p.c, p.z, xy)
+            for j in range(p.nz - 1):
+                total = total + self.load(q, p.o, j, xy)
+            self.save(q, p.c, p.z, xy, total)
+        device = p.to_x if self.chunks[q][3] == 0 else p.to_y
+        self.copy(q, 0, self.at(q, p.c, p.z, p.at_d), self.at(q, p.o, p.nz - 1, 0), device)
+
+    def plane_across(self, q):
+        p, there = self.p, self.p.nz - 1
+        to = p.at_y if self.chunks[q][3] == 0 else p.at_x
+        self.wait(q, 0, self.at(q, p.o, there, 0))
+        self.save(q, p.c, p.z, to, self.load(q, p.c, p.z, to) + self.load(q, p.o, there, 0))
+        self.copy(q, 2, self.at(q, p.c, p.z, p.at_x), self.at(q, p.o, there, 1), p.to_x)
+        self.copy(q, 3, self.at(q, p.c, p.z, p.at_y), self.at(q, p.o, there, 2), p.to_y)
+
+    def plane_last(self, q):
+        p, there = self.p, self.p.nz - 1
+        total = self.load(q, p.c, p.z, p.own)
+        for j in (1, 2):
+            self.wait(q, 1 + j, self.at(q, p.o, there, j))
+            total = total + self.load(q, p.o, there, j)
+        self.hand_over(q, total)
+
     def last(self, q):
-        p, r, (k, start, width, _) = self.p, self.r, self.chunks[q]
+        p = self.p
         total = self.load(q, p.c, p.z, p.own)
         for j in range(p.nz - 1):
             self.wait(q, 4 + j, self.at(q, p.o, j, 3))
             total = total + self.load(q, p.o, j, 3)
+        self.hand_over(q, total)
+
+    def hand_over(self, q, total):
+        p, r, (k, start, width, _) = self.p, self.r, self.chunks[q]
         cols = slice(start, start + width)
         rows = total.shape[0] // 2
         r.sums[k][p.c, :, cols] = jnp.where(p.c == 0, total[:rows], total[rows:])
@@ -501,12 +605,16 @@
             if age + 1 < lag:
                 self.under_way[other] = stage, age + 1
                 continue
-            (self.across, self.along_z, self.last)[stage](other)
+            self.steps(other)[stage + 1](other)
             self.under_way[other] = stage + 1, 0
             if stage == 2:
                 del self.under_way[other]
         if q is not None:
-            self.diagonal(q)
+            k = self.chunks[q][0]
+            if k not in self.open:
+                pl.semaphore_wait(self.r.credit.at[k], 1 + self.p.nz)
+                self.open.add(k)
+            self.steps(q)[0](q)
             self.under_way[q] = 0, 0
 
     def chunks_of(self, k):
@@ -595,13 +703,15 @@
         r.vec_sum[i : i + 1] = gain_sum
         r.vec_sum[3 + i : 4 + i] = shift_sum
 
-    for q in g.chunks_of(6):
-        g.tick()
     for name in ("cot", "act"):
         swap.wait(name)
-    plain_grad(6, r.act, r.by_act, r.cotangent, r.by_cot, w[6].shape[-1], 4 * w[6].shape[3], push=False)
+    red.free(6)
+    plain_grad(6, r.act, r.by_act, r.cotangent, r.by_cot, w[6].shape[-1], 4 * w[6].shape[3])
     for q in g.chunks_of(6):
         g.need(q)
+        down_part(q)
+        g.settle(q)
+        red.push()
     down_half = w[6].shape[-1]
 
     def act_tile(z, carry):
@@ -617,12 +727,7 @@
     lax.fori_loop(0, p.nz, act_tile, 0)
     gh = r.slope
     swap.send("gh", half(gh, o, hidden_half), r.by_hidden_grad)
-    for q in g.chunks_of(6):
-        down_part(q)
-        g.settle(q)
-    red.free(6)
-    for q in red.chunks_of(6):
-        red.push(q)
+    red.push()
     grad_three = input_grad(gh, 5, hidden_half)
     red.free(5)
     red.push()
@@ -648,7 +753,7 @@
         cols = pl.ds(pl.multiple_of(i * LANES, LANES), LANES)
         vcols = pl.ds(pl.multiple_of(i * LANES + pool_half, LANES), LANES)
         for b in range(slots // 2):
-            two = [lax.rem(r.index[2 * b + j], slots) for j in range(2)]
+            two = [lax.rem(r.index[b, j], slots) for j in range(2)]
             rows = slice(b * span, (b + 1) * span)
             queries = stacked(r.cq[rows, cols], low, high) * bf16(HEAD**-0.5)
             grads = stacked(r.mixed_grad[rows, cols], low, high)
@@ -687,13 +792,13 @@
     for s in range(slots):
         j = 0
         for k in range(slots):
-            j = jnp.where(lax.rem(r.index[k], slots) == s, k, j)
+            j = jnp.where(lax.rem(r.index[k // 2, k % 2], slots) == s, k, j)
         b, odd = lax.div(j, 2), lax.rem(j, 2)
         r.pool[s] = jnp.where(odd == 0, r.gkv[b, :rows_n], r.gkv[b, rows_n:])
     swap.send("gp", r.pool.at[:, :, pl.ds(pl.multiple_of(o * pool_half, LANES), pool_half)], r.by_pool_grad)
 
     cosine, signed = r.rope[0, :, :LANES], r.rope[0, :, LANES:]
-    place = lax.rem(lax.broadcasted_iota(jnp.int32, (1, 2 * quarter), 1), quarter) + p.s * quarter
+    place = lax.broadcasted_iota(jnp.int32, (1, quarter), 1) + p.s * quarter
     limit = jnp.maximum(place, r.prefix[0] - 1)
     group, groups = width, 2
     each = pairs // groups
@@ -702,21 +807,27 @@
         cols = pl.ds(pl.multiple_of(i * LANES, LANES), LANES)
         vcols = pl.ds(pl.multiple_of(i * LANES + pool_half, LANES), LANES)
         start = lax.div(i, each) * group + lax.rem(i, each) * LANES
-        queries = stacked(r.q[:, cols], low, high) * bf16(HEAD**-0.5)
-        grads = stacked(r.mixed_grad[:, cols], low, high)
         keys = r.kv[:, :, cols].reshape(-1, LANES)
         values = r.kv[:, :, vcols].reshape(-1, LANES)
-        scores = dot(keys, queries, NT)
-        key_place = lax.broadcasted_iota(jnp.int32, scores.shape, 0)
-        probs = jnp.exp(jnp.where(key_place <= limit, scores, masked) - r.lse[i])
-        grad_probs = dot(values, grads, NT)
-        score_grad = (probs * (grad_probs - jnp.sum(probs * grad_probs, 0, keepdims=True))).astype(bf16)
-        for offset, part in ((0, dot(score_grad, queries)), (group // 2, dot(probs.astype(bf16), grads))):
+        key_grad = value_grad = 0.0
+        query_grads = []
+        for e, lanes in enumerate((low, high)):
+            queries = r.q[:, cols] * (lanes * bf16(HEAD**-0.5))
+            grads = r.mixed_grad[:, cols] * lanes
+            scores = dot(keys, queries, NT)
+            key_place = lax.broadcasted_iota(jnp.int32, scores.shape, 0)
+            logsum = r.lse[i, :, e * quarter : (e + 1) * quarter]
+            probs = jnp.exp(jnp.where(key_place <= limit, scores, masked) - logsum)
+            grad_probs = dot(values, grads, NT)
+            score_grad = (probs * (grad_probs - jnp.sum(probs * grad_probs, 0, keepdims=True))).astype(bf16)
+            key_grad = key_grad + dot(score_grad, queries)
+            value_grad = value_grad + dot(probs.astype(bf16), grads)
+            query_grads.append(dot(score_grad, keys, TN))
+        for offset, part in ((0, key_grad), (group // 2, value_grad)):
             there = pl.ds(pl.multiple_of(start + offset, LANES), LANES)
             r.gkv[:, :, there] = part.astype(bf16).reshape(4, quarter, LANES)
-        gq = dot(score_grad, keys, TN) * HEAD**-0.5
-        gq = jnp.where(low_lane, gq[:quarter], gq[quarter:])
-        r.q_grad[:, cols] = rotate(gq, cosine, -signed).astype(bf16)
+        query_grad = jnp.where(low_lane, *query_grads) * HEAD**-0.5
+        r.q[:, cols] = rotate(query_grad, cosine, -signed).astype(bf16)
         return carry
 
     for i in range(groups):
@@ -726,7 +837,7 @@
         cols = pl.ds(i * group, group)
         swap.send(f"far{i}", r.gkv.at[p.s_d, :, cols], r.by_act.at[:, cols])
         swap.send(f"near{i}", r.gkv.at[p.s_c, :, cols], r.by_act.at[:, pl.ds((groups + i) * group, group)])
-    swap.send("gq", half(r.q_grad, o, width // 2), r.by_q_grad)
+    swap.send("gq", half(r.q, o, width // 2), r.by_q_grad)
     swap.wait("gcq")
     swap.wait("n2")
     plain_grad(3, r.n2, r.by_n2, r.cq_grad, r.by_cq_grad, width // 2)
@@ -739,7 +850,7 @@
             r.gkv[s, :, cols] = total.astype(bf16)
     half_kv = pl.ds(pl.multiple_of(o * group, LANES), group)
     for j, (name, s) in enumerate((("gkv", p.s), ("gkvy", p.s_y))):
-        swap.send(name, r.gkv.at[s, :, half_kv], r.by_kv_grad.at[pl.ds(j * quarter, quarter)])
+        swap.send(name, r.gkv.at[s, :, half_kv], r.by_hidden_grad.at[:, pl.ds(j * group, group)])
     red.push()
     part = width // 2
 
@@ -751,7 +862,7 @@
     to_y = remote(r.mixed_grad, r.one_y, kv_sem.at[0], kv_sem.at[1], p.to_y)
     to_y.start()
     r.second[...] = grad_one[:quarter] + sum(
-        dot(r.q_grad[:, h * part : (h + 1) * part], half_of(w[0], h, 0, part), NT) for h in range(2)
+        dot(r.q[:, h * part : (h + 1) * part], half_of(w[0], h, 0, part), NT) for h in range(2)
     )
     red.free(0)
     for q in g.chunks_of(0):
@@ -759,13 +870,15 @@
     for name in ("gq", "n1", "gkv", "gkvy"):
         swap.wait(name)
     first_chunk, *kv_chunks, vec_chunk = red.chunks_of(0)
-    plain_grad(0, r.n1.at[:quarter], r.by_n1.at[:quarter], r.q_grad, r.by_q_grad, part, chunks=[first_chunk])
+    plain_grad(0, r.n1.at[:quarter], r.by_n1.at[:quarter], r.q, r.by_q_grad, part, chunks=[first_chunk])
     weight_grad(
         0,
         lambda cols: r.n1[:, cols],
         lambda cols: r.by_n1[:, cols],
         lambda start, n: kv_grads(pl.ds(pl.multiple_of(c * group + start - part, LANES), n)),
-        lambda start, n: r.by_kv_grad[:, start - part : start - part + n],
+        lambda start, n: jnp.concatenate(
+            [r.by_hidden_grad[:, j * group + start - part : j * group + start - part + n] for j in range(2)], 0
+        ),
         3 * part,
         chunks=kv_chunks,
     )
@@ -781,7 +894,7 @@
         )
         if out[s % 2] is not None:
             out[s % 2].wait()
-        stage = r.stage.at[s % 2]
+        stage = r.tokens_grad.at[(s % 2) * rows_n : (s % 2 + 1) * rows_n]
         stage[...] = slot_grad
         out[s % 2] = pltpu.make_async_copy(stage, r.neighbours_grad.at[s], r.out_sem.at[s % 2])
         out[s % 2].start()
@@ -805,6 +918,8 @@
     grad_one = r.second[...] + r.one_y[...].astype(f32)
     back, dg, db = norm_back_at(grad_one, r.tokens[...].astype(f32), gain(0))
     keep_vec(0, dg, db)
+    for cp in out:
+        cp.wait()
     r.tokens_grad[...] = r.first[...] + back
     swap.send("vec", r.vec_sum, r.by_vec)
     swap.wait("vec")
@@ -814,8 +929,6 @@
     red.drain()
     for cp in (*red.sent, *swap.sent, to_y):
         cp.wait_send()
-    for cp in out:
-        cp.wait()
 
 
 def rope_table(length):
@@ -828,26 +941,33 @@
 
 
 def deliver_kernel(*refs):
-    n = 3
-    plain, sums = refs[:n], refs[n : n + 7]
-    outs, sem = refs[n + 7 : -1], refs[-1]
-    copies = [(src, dst) for src, dst in zip(plain, outs[:n])]
-    for k, dst in zip(range(7), outs[n : n + 7]):
-        parts = 3 if k == 0 else 1
-        part = dst.shape[1] // (2 * parts)
+    n = 10
+    sources, outs, held = refs[:n], refs[n : 2 * n + 1], refs[2 * n + 1 : 3 * n + 1]
+    arrive, leave = refs[3 * n + 1 :]
+    taken = [pltpu.make_async_copy(sources[i], held[i], arrive.at[i]) for i in range(n)]
+    for cp in taken:
+        cp.start()
+    left = []
+
+    def put(src, dst):
+        left.append(pltpu.make_async_copy(src, dst, leave.at[len(left)]))
+        left[-1].start()
+
+    for i in range(n):
+        taken[i].wait()
+        if i < 3:
+            put(held[i], outs[i])
+            continue
+        parts = 3 if i == 3 else 1
+        part = outs[i].shape[1] // (2 * parts)
         for h in range(2):
-            for i in range(parts):
-                source, there = i * part, i * 2 * part + h * part
-                copies.append((sums[k].at[h, :, source : source + part], dst.at[:, there : there + part]))
-    copies = [pltpu.make_async_copy(src, dst, sem.at[i]) for i, (src, dst) in enumerate(copies)]
-    for cp in copies:
-        cp.start()
-    half = outs[n].shape[1] // 2
-    turned = jnp.transpose(
-        jnp.concatenate([sums[0][0, :, half:], jnp.zeros((LANES - sums[0].shape[1], LANES), f32)], 0)
-    )
-    outs[n + 7][...] = turned[:8, : outs[n + 7].shape[1]]
-    for cp in copies:
+            for j in range(parts):
+                put(held[i].at[h, :, j * part : (j + 1) * part], outs[i].at[:, (2 * j + h) * part : (2 * j + h + 1) * part])
+        if i == 3:
+            rows = held[i].shape[1]
+            vectors = jnp.concatenate([held[i][0, :, parts * part :], jnp.zeros((LANES - rows, LANES), f32)], 0)
+            outs[n][...] = jnp.transpose(vectors)[:8, :rows]
+    for cp in left:
         cp.wait()
 
 
@@ -858,16 +978,18 @@
     shapes = [out, tokens_grad, neighbours_grad] + [
         jax.ShapeDtypeStruct((v.shape[1], n), f32) for v, n in zip(summed, widths)
     ]
-    vmem, anywhere = pl.BlockSpec(memory_space=pltpu.VMEM), pl.BlockSpec(memory_space=pl.ANY)
+    vmem, hbm = pl.BlockSpec(memory_space=pltpu.VMEM), pl.BlockSpec(memory_space=pltpu.HBM)
+    sources = (out, tokens_grad, neighbours_grad, *summed)
     out, tokens_grad, neighbours_grad, *grads, vectors = pl.pallas_call(
         deliver_kernel,
         out_shape=[jax.ShapeDtypeStruct(v.shape, v.dtype) for v in shapes] + [jax.ShapeDtypeStruct((8, rows), f32)],
-        in_specs=[vmem] * 10,
-        out_specs=[anywhere] * 10 + [vmem],
-        scratch_shapes=[pltpu.SemaphoreType.DMA((21,))],
-        compiler_params=pltpu.CompilerParams(vmem_limit_bytes=32 * 2**20),
+        in_specs=[hbm] * 10,
+        out_specs=[hbm] * 10 + [vmem],
+        scratch_shapes=[pltpu.VMEM(v.shape, v.dtype) for v in sources]
+        + [pltpu.SemaphoreType.DMA((10,)), pltpu.SemaphoreType.DMA((21,))],
+        compiler_params=pltpu.CompilerParams(vmem_limit_bytes=64 * 2**20 - 2**17),
         name="deliver",
-    )(out, tokens_grad, neighbours_grad, *summed)
+    )(*sources)
     return (
         out[None],
         tokens_grad[None],
@@ -954,7 +1076,7 @@
     arrays = dict(
         pack=((2, rows, sum(halves)), f32),
         beside=((rows, sum(halves)), f32),
-        down_sum=((1, *weights[6][0][1:]), bf16),
+        down_sum=weights[6],
         down_beside=((hidden // (8 * nz), width // 2), f32),
         rope=((2, quarter, 2 * LANES), f32),
         n1=((2 * quarter, width), bf16),
@@ -977,9 +1099,7 @@
         mixed_grad=tok,
         cq_grad=tok,
         self_branch=tok,
-        q_grad=tok,
         one_y=tok,
-        stage=((2, rows_n, width), f32),
         gkv=((4, *kv[0]), bf16),
         vec_sum=((8, width), f32),
         by_act=((quarter, hidden), bf16),
@@ -996,7 +1116,6 @@
         by_self_branch=half_tok,
         by_n1=((2 * quarter, width), bf16),
         by_q_grad=half_tok,
-        by_kv_grad=((2 * quarter, width), bf16),
         by_vec=((8, width), f32),
     )
     return weights, arrays, sums
@@ -1051,7 +1170,7 @@
     quarter, width = tokens.shape[1:]
     rows, hidden = w_up.shape
     slots, rows_n = neighbours.shape[1:3]
-    vectors = jnp.stack([gain_one, gain_two, gain_three, shift_one, shift_two, shift_three], 1)
+    vectors = jnp.stack([gain_one, gain_two, gain_three, shift_one, shift_two, shift_three])
     weights, arrays, sums = memory(nz, quarter, width, hidden, slots, rows_n, rows)
     vmem, smem, anywhere = (pl.BlockSpec(memory_space=m) for m in (pltpu.VMEM, pltpu.SMEM, pl.ANY))
     made = [((quarter, width), bf16), ((quarter, width), f32), ((slots, rows_n, width), f32), *sums]
@@ -1069,8 +1188,8 @@
             dma((2, 2)),
             dma((2,)),
             dma((2, 28)),
-            dma((len(GATHER), 12)),
-            dma((len(GATHER), 12)),
+            dma((len(GATHER), 14)),
+            dma((len(GATHER), 14)),
             dma((len(REDUCE), 8)),
             dma((len(REDUCE), 8)),
             pltpu.SemaphoreType.REGULAR((7,)),
@@ -1081,7 +1200,7 @@
     )(
         w_qkv, w_cross_kv, w_out, w_cross_q, w_cross_out, w_up, w_down, vectors,
         tokens[0], cotangent[0], prefix_len, neighbours[0],
-        neighbour_index.reshape(-1), jnp.asarray(rope_table(4 * quarter)),
+        neighbour_index[0], jnp.asarray(rope_table(4 * quarter)),
     )
     return deliver(out, tokens_grad, neighbours_grad, summed)
 

time: 243 us -> 226 us (0.930)
  local copies, waits for them, and re-layouts: 13.8 us -> 4.11 us
  Pallas kernels: 223 us -> 216 us
    unnamed x21 -> x0, local copies, waits for them, and re-layouts: 11.2 us -> none
    pallas_call x1, Pallas kernels: 221 us -> 210 us  [local_fast(): pl.pallas_call(functools.partial(layer_kernel, nz, tuple(arrays)), out_sh...]
    pallas_call x1, Pallas kernels: 2.58 us -> 5.6 us  [deliver(): pl.pallas_call(deliver_kernel, out_shape=[jax.ShapeDtypeStruct(v.shape, v...]
where the time goes in v4:
time: 226 us; the launch traced here: 221 us
  Pallas kernels  216 us (96%)
  local copies, waits for them, and re-layouts  4.11 us (2%)
    pallas_call x1, Pallas kernels, local_fast(): pl.pallas_call(functools.partial(layer_kernel, nz, tuple(arrays)), out_sh...  210 us
    pallas_call x1, Pallas kernels, deliver(): pl.pallas_call(deliver_kernel, out_shape=[jax.ShapeDtypeStruct(v.shape, v...  5.6 us

profile of v4, /device:TPU:1, one launch (start us, length us, event | category | flops | bytes accessed | tf_op | source)
XLA Modules:
  0.0 221.5 jit_solution(12784245556268423759)
XLA Ops:
  1.3 1.3 copy.35.refs_12_
  2.6 1.3 stack.27.refs_7_
  4.0 210.2 %shard_map.306 = (bf16[256,768]{1,0:T(8,128)(2,1)}, f32[256,768]{1,0:T(8,128)}, f32[8,128,768]{2,1,0:T(8,128)}, f32[2,24,1280]{2,1,0:T(8,128)}, f32[2,24,768]{2,...) custom-call(bf16[24,2304]{1,0:T(8,128)(2,1)} %refs_0_.1, ...), custom_call_target="tpu_custom_call" | custom-call | tf_op jit(solution)/shard_map/pallas_call | solution.py:1178
  214.2 5.6 %deliver.1 = (bf16[256,768]{1,0:T(8,128)(2,1)}, f32[256,768]{1,0:T(8,128)}, f32[8,128,768]{2,1,0:T(8,128)}, f32[24,2304]{1,0:T(8,128)}, f32[24,1536]{1,0:T(8,128...) custom-call(bf16[256,768]{1,0:T(8,128)(2,1)} %get-tuple-element.37.r, ...), custom_call_target="tpu_custom_call" | custom-call | tf_op jit(solution)/shard_map/deliver/pallas_call | solution.py:983
  219.8 1.4 slice_bitcast_fusion

commit v5 on v4

--- a/solution.py
+++ b/solution.py
@@ -471,13 +471,13 @@
     return down_part, turned, (first, down, tokens_y, *kv_sent)
 
 
-LAG = 4
+LAGS = (6, 5, 3)
 
 
 class Reduce:
     def __init__(self, place, r, chunks, send, recv):
         self.p, self.r, self.w, self.chunks, self.ss, self.rs = place, r, r.w, chunks, send, recv
-        self.sent, self.open, self.under_way, self.next = [], set(), {}, 0
+        self.sent, self.open, self.under_way, self.phase = [], set(), {}, 0
         self.starts = [sum(v.shape[-1] for v in r.w[:k]) for k in range(7)]
 
     def free(self, k):
@@ -599,7 +599,8 @@
         p, (k, start, width, _) = self.p, self.chunks[q]
         self.wait(q, 7, self.r.sums[k].at[p.o, :, pl.ds(start, width)])
 
-    def push(self, q=None, lag=LAG):
+    def push(self, q=None, lag=None):
+        lag = lag or LAGS[self.phase]
         for other in list(self.under_way):
             stage, age = self.under_way[other]
             if age + 1 < lag:
@@ -837,6 +838,7 @@
         cols = pl.ds(i * group, group)
         swap.send(f"far{i}", r.gkv.at[p.s_d, :, cols], r.by_act.at[:, cols])
         swap.send(f"near{i}", r.gkv.at[p.s_c, :, cols], r.by_act.at[:, pl.ds((groups + i) * group, group)])
+    red.phase = 1
     swap.send("gq", half(r.q, o, width // 2), r.by_q_grad)
     swap.wait("gcq")
     swap.wait("n2")
@@ -900,6 +902,7 @@
         out[s % 2].start()
         if s == slots // 2:
             red.push()
+    red.phase = 2
     red.free(1)
     for q in g.chunks_of(1):
         g.settle(q)
@@ -1046,11 +1049,13 @@
     (6, 256, 128, 2),
 )
 REDUCE = (
-    (6, 0, 256, 2),
+    (6, 0, 128, 2),
+    (6, 128, 128, 2),
     (6, 256, 128, 2),
-    (5, 0, 512, 2),
-    (5, 512, 512, 2),
-    (5, 1024, 512, 2),
+    (5, 0, 384, 2),
+    (5, 384, 384, 2),
+    (5, 768, 384, 2),
+    (5, 1152, 384, 2),
     (4, 0, 384, 2),
     (3, 0, 384, 2),
     (2, 0, 384, 2),

time: 226 us -> 220 us (0.973)
  Pallas kernels: 216 us -> 210 us
    pallas_call x1, Pallas kernels: 210 us -> 204 us  [local_fast(): pl.pallas_call(functools.partial(layer_kernel, nz, tuple(arrays)), out_sh...]
where the time goes in v5:
time: 220 us; the launch traced here: 216 us
  Pallas kernels  210 us (95%)
  local copies, waits for them, and re-layouts  4.11 us (2%)
    pallas_call x1, Pallas kernels, local_fast(): pl.pallas_call(functools.partial(layer_kernel, nz, tuple(arrays)), out_sh...  204 us
    pallas_call x1, Pallas kernels, deliver(): pl.pallas_call(deliver_kernel, out_shape=[jax.ShapeDtypeStruct(v.shape, v...  5.6 us

profile of v5, /device:TPU:1, one launch (start us, length us, event | category | flops | bytes accessed | tf_op | source)
XLA Modules:
  0.0 215.6 jit_solution(8903190239419973301)
XLA Ops:
  1.3 1.3 copy.35.refs_12_
  2.6 1.3 stack.27.refs_7_
  4.0 204.3 %shard_map.306 = (bf16[256,768]{1,0:T(8,128)(2,1)}, f32[256,768]{1,0:T(8,128)}, f32[8,128,768]{2,1,0:T(8,128)}, f32[2,24,1280]{2,1,0:T(8,128)}, f32[2,24,768]{2,...) custom-call(bf16[24,2304]{1,0:T(8,128)(2,1)} %refs_0_.1, ...), custom_call_target="tpu_custom_call" | custom-call | tf_op jit(solution)/shard_map/pallas_call | solution.py:1183
  208.3 5.6 %deliver.1 = (bf16[256,768]{1,0:T(8,128)(2,1)}, f32[256,768]{1,0:T(8,128)}, f32[8,128,768]{2,1,0:T(8,128)}, f32[24,2304]{1,0:T(8,128)}, f32[24,1536]{1,0:T(8,128...) custom-call(bf16[256,768]{1,0:T(8,128)(2,1)} %get-tuple-element.37.r, ...), custom_call_target="tpu_custom_call" | custom-call | tf_op jit(solution)/shard_map/deliver/pallas_call | solution.py:986
  213.9 1.4 slice_bitcast_fusion

commit v6 on v5

--- a/solution.py
+++ b/solution.py
@@ -472,6 +472,7 @@
 
 
 LAGS = (6, 5, 3)
+JOINT = True
 
 
 class Reduce:
@@ -670,19 +671,22 @@
         into, lead = red.array(k, c)
         rows = into.shape[3]
         per = tile // (4 * rows)
-        for q in red.chunks_of(k) if chunks is None else chunks:
-            _, start, n, _ = red.chunks[q]
-            n = min(n, size - start)
-
-            def body(i, carry, start=start, n=n):
+        columns = [(q, red.chunks[q][1]) for q in (red.chunks_of(k) if chunks is None else chunks)]
+        columns = [(q, start, min(red.chunks[q][2], size - start)) for q, start in columns]
+        for together in [columns] if JOINT else [[v] for v in columns]:
+
+            def body(i, carry, together=together):
                 cols = pl.ds(pl.multiple_of(i * tile, LANES), tile)
-                part = dot(left(cols), right(start, n), TN) + dot(left_beside(cols), right_beside(start, n), TN)
-                into[lead, pl.ds(i * per, per), :, :, start : start + n] = part.astype(bf16).reshape(per, 4, rows, n)
+                turned_left, turned_beside = jnp.transpose(left(cols)), jnp.transpose(left_beside(cols))
+                for _, start, n in together:
+                    part = dot(turned_left, right(start, n)) + dot(turned_beside, right_beside(start, n))
+                    into[lead, pl.ds(i * per, per), :, :, start : start + n] = part.astype(bf16).reshape(per, 4, rows, n)
                 return carry
 
             lax.fori_loop(0, p.nz // per, body, 0)
             if push:
-                red.push(q)
+                for q, _, _ in together:
+                    red.push(q)
 
     def plain_grad(k, left, left_beside, right, right_beside, size, tile=384, chunks=None, push=True):
         weight_grad(

time: 220 us -> 221 us (level)
  no operation moved by 1% of the time
where the time goes in v6:
time: 221 us; the launch traced here: 217 us
  Pallas kernels  211 us (95%)
  local copies, waits for them, and re-layouts  4.11 us (2%)
    pallas_call x1, Pallas kernels, local_fast(): pl.pallas_call(functools.partial(layer_kernel, nz, tuple(arrays)), out_sh...  205 us
    pallas_call x1, Pallas kernels, deliver(): pl.pallas_call(deliver_kernel, out_shape=[jax.ShapeDtypeStruct(v.shape, v...  5.6 us

profile of v6, /device:TPU:1, one launch (start us, length us, event | category | flops | bytes accessed | tf_op | source)
XLA Modules:
  0.0 216.5 jit_solution(7745589586495247576)
XLA Ops:
  1.3 1.3 copy.35.refs_12_
  2.6 1.3 stack.27.refs_7_
  4.0 205.3 %shard_map.306 = (bf16[256,768]{1,0:T(8,128)(2,1)}, f32[256,768]{1,0:T(8,128)}, f32[8,128,768]{2,1,0:T(8,128)}, f32[2,24,1280]{2,1,0:T(8,128)}, f32[2,24,768]{2,...) custom-call(bf16[24,2304]{1,0:T(8,128)(2,1)} %refs_0_.1, ...), custom_call_target="tpu_custom_call" | custom-call | tf_op jit(solution)/shard_map/pallas_call | solution.py:1187
  209.3 5.6 %deliver.1 = (bf16[256,768]{1,0:T(8,128)(2,1)}, f32[256,768]{1,0:T(8,128)}, f32[8,128,768]{2,1,0:T(8,128)}, f32[24,2304]{1,0:T(8,128)}, f32[24,1536]{1,0:T(8,128...) custom-call(bf16[256,768]{1,0:T(8,128)(2,1)} %get-tuple-element.37.r, ...), custom_call_target="tpu_custom_call" | custom-call | tf_op jit(solution)/shard_map/deliver/pallas_call | solution.py:990
  214.9 1.4 slice_bitcast_fusion
